TPU v7x, 256 devices: a whole 4x4x8 slice. The times are simulated.
256 devices in a mesh: dp: 64 (over x, z, core), proto: 4 (over y).
Axes of the slice: x: 4, y: 4, z: 8, core: 2. Of those that a mesh axis runs over, the one named last changes fastest.
Arguments:
- teacher_feats: bfloat16 [8192, 2, 256], P('dp'), may hold values from -0.5 to 0.5
- student_embeddings: bfloat16 [8192, 6, 256], P('dp'), may hold values from -0.5 to 0.5
- teacher_weight: float32 [256, 32768], P('dp', 'proto'), may hold values from -0.5 to 0.5
- student_weight: float32 [256, 32768], P('dp', 'proto'), may hold values from -0.375 to 0.375
Outputs:
- weight_grad: float32 [256, 32768], P('dp', 'proto')
- teacher_new: float32 [256, 32768], P('dp', 'proto')
- feature_grad: float32 [8192, 6, 256], P('dp')
All inputs are finite; a program needn't handle non-finite values.
Results may differ from a plain program's by a relative error of at most 0.00135.
The roundings to bfloat16 on the way count: a program that leaves them out, or rounds other values in their place, can miss the bound.
Values may be sent and summed in bfloat16 or wider, within the bound.
No kernel may reach another device: no remote copies, remote signals or barrier semaphores. Data moves between devices by JAX's collectives and lax.ppermute only.
A program may use at most 256 MiB of HBM per device.

v0:
```python
import jax
import jax.numpy as jnp
from jax import lax
from jax.sharding import PartitionSpec as P

BALANCING_ROUNDS = 3


EPS = 1e-06
TEMP_T = 0.07
TEMP_S = 0.1


def local(teacher_feats, student_embeddings, teacher_weight, student_weight):
    images_here = teacher_feats.shape[0]
    bottleneck = teacher_feats.shape[2]
    width = student_weight.shape[1]
    total_k = width * lax.axis_size("proto")
    rows_here = student_weight.shape[0]
    first_row = lax.axis_index("dp") * rows_here
    full_s, full_t = (
        lax.all_gather(student_weight, "dp", axis=0, tiled=True),
        lax.all_gather(teacher_weight, "dp", axis=0, tiled=True),
    )
    col_s = jnp.sqrt(jnp.sum(full_s * full_s, axis=0) + EPS)
    col_t = jnp.sqrt(jnp.sum(full_t * full_t, axis=0) + EPS)
    proto_s = (full_s / col_s).astype(jnp.bfloat16)
    proto_t = (full_t / col_t).astype(jnp.bfloat16)
    shard_s = lax.dynamic_slice_in_dim(proto_s, first_row, rows_here, 0)
    t_rows = teacher_feats.reshape(images_here * 2, bottleneck).astype(jnp.float32)
    t_unit = (t_rows / jnp.sqrt(jnp.sum(t_rows * t_rows, axis=1, keepdims=True) + EPS)).astype(
        jnp.bfloat16
    )
    energy = jnp.exp(jnp.dot(t_unit, proto_t, preferred_element_type=jnp.float32) / TEMP_T)
    scales = jnp.ones((images_here * 2,), jnp.float32)
    for round_number in range(BALANCING_ROUNDS):
        recip = 1.0 / lax.psum(jnp.sum(energy * scales[:, None], axis=0), "dp")
        scales = 1.0 / lax.psum(jnp.sum(energy * recip[None, :], axis=1), "proto")
    targets = (energy * recip[None, :] * scales[:, None]).reshape(images_here, 2, width)
    s_rows = student_embeddings.reshape(images_here * 6, bottleneck).astype(jnp.float32)
    s_norm = jnp.sqrt(jnp.sum(s_rows * s_rows, axis=1, keepdims=True) + EPS)
    s_float = s_rows / s_norm
    s_unit = s_float.astype(jnp.bfloat16)
    prototype_scores = (
        jnp.dot(s_unit, proto_s, preferred_element_type=jnp.float32) / TEMP_S
    ).reshape(images_here, 6, width)
    expsum = jnp.sum(jnp.exp(prototype_scores), axis=-1)
    expsum = lax.psum(expsum, "proto")
    lse = jnp.log(expsum)
    pairing = jnp.array([[0, 1, 1, 1, 1, 1], [1, 0, 1, 1, 1, 1]], jnp.float32)
    counts = jnp.array([1, 1, 2, 2, 2, 2], jnp.float32)
    prob = jnp.exp(prototype_scores - lse[..., None])
    tpart = (
        pairing[0][None, :, None] * targets[:, 0:1, :]
        + pairing[1][None, :, None] * targets[:, 1:2, :]
    )
    slope = (
        (total_k / 16.0 * (counts[None, :, None] * prob - tpart))
        .astype(jnp.bfloat16)
        .reshape(images_here * 6, width)
    )
    unit_portion = lax.dot_general(
        slope, proto_s, (((1,), (1,)), ((), ())), preferred_element_type=jnp.float32
    )
    unit_grad = lax.psum(unit_portion, "proto")
    fgrad = (unit_grad - s_float * jnp.sum(s_float * unit_grad, axis=1, keepdims=True)) / s_norm
    feature_grad = fgrad.reshape(images_here, 6, bottleneck)
    summed_values = lax.psum_scatter(
        lax.dot_general(
            s_unit, slope, (((0,), (0,)), ((), ())), preferred_element_type=jnp.float32
        ),
        "dp",
        scatter_dimension=0,
        tiled=True,
    )
    column_dot = lax.psum(jnp.sum(shard_s * summed_values, axis=0), "dp")
    weight_grad = (summed_values - shard_s * column_dot) / col_s
    teacher_new = 0.994 * teacher_weight + 0.006 * (student_weight - 0.5 * weight_grad)
    return (weight_grad, teacher_new, feature_grad)


def solution(mesh):
    in_specs = (P("dp", None, None), P("dp", None, None), P("dp", "proto"), P("dp", "proto"))
    out_specs = (P("dp", "proto"), P("dp", "proto"), P("dp", None, None))
    return jax.shard_map(local, mesh=mesh, in_specs=in_specs, out_specs=out_specs, check_vma=False)
```

profile of v0, /device:TPU:32, one launch (start us, length us, event | category | flops | bytes accessed | tf_op | source)
XLA Modules:
  0.0 1671.5 jit_solution(10204182328987807837)
XLA Ops:
  7.2 0.7 all-gather.7.cloned.1.call-update
  7.9 0.7 all-gather.5.cloned.1.call-update
  8.7 1.2 copy.13
  9.9 1.2 multiply_reduce_fusion.8
  11.1 0.1 copy.14
  11.2 0.1 sqrt.37
  11.4 0.7 mul.178
  12.0 0.1 mul.179
  12.2 0.7 mul.184
  12.8 0.1 mul.185
  13.0 0.7 mul.206
  13.7 0.1 mul.207
  13.8 0.9 reshape.77
  14.7 1.1 multiply_reduce_fusion.9
  15.9 0.1 sqrt.40
  16.0 0.1 reshape.76
  16.2 80.4 %all-gather.7.cloned.1.call-done = f32[64,4,8192]{2,1,0:T(4,128)} async-done(((f32[1,4,8192]{2,1,0:T(4,128)}), f32[64,4,8192]{2,1,0:T(4,128)}) %all-gather.7.cloned.1.call-update) | async-done | bytes 8388624 | tf_op jit(solution)/shard_map/all_gather | solution.py:23
  96.6 10.0 reshape.81
  106.6 4.2 multiply_reduce_fusion.4
  110.8 68.9 %all-gather.5.cloned.1.call-done = f32[64,4,8192]{2,1,0:T(4,128)} async-done(((f32[1,4,8192]{2,1,0:T(4,128)}), f32[64,4,8192]{2,1,0:T(4,128)}) %all-gather.5.cloned.1.call-update) | async-done | bytes 8388624 | tf_op jit(solution)/shard_map/all_gather | solution.py:22
  179.7 10.0 reshape.79
  189.7 4.2 multiply_reduce_fusion.5
  193.9 1.5 copy-done
  195.4 2.6 divide_convert_fusion.1
  198.1 8.7 fusion.12
  206.7 243.4 %psum.64 = f32[8192]{0:T(1024)S(1)} all-reduce(f32[8192]{0:T(1024)S(1)} %get-tuple-element.18), channel_id=1, replica_groups=mesh['dp'=64,'proto'=4] {'dp'}, use_global_device_ids=true, to_apply=%region_7.0 | all-reduce | flops 8192 | bytes 65536 | tf_op jit(solution)/shard_map/psum | solution.py:37
  450.2 4.2 multiply_reduce_fusion.3
  454.4 10.5 psum.65
  464.9 4.3 multiply_reduce_fusion.2
  469.2 246.1 %psum.66 = f32[8192]{0:T(1024)S(1)} all-reduce(f32[8192]{0:T(1024)S(1)} %multiply_reduce_fusion.2), channel_id=1, replica_groups=mesh['dp'=64,'proto'=4] {'dp'}, use_global_device_ids=true, to_apply=%region_11.0 | all-reduce | flops 8192 | bytes 65536 | tf_op jit(solution)/shard_map/psum | solution.py:37
  715.4 4.2 multiply_reduce_fusion.1
  719.6 7.7 psum.67
  727.3 4.3 multiply_reduce_fusion
  731.6 246.3 %psum.68 = f32[8192]{0:T(1024)S(1)} all-reduce(f32[8192]{0:T(1024)S(1)} %multiply_reduce_fusion), channel_id=1, replica_groups=mesh['dp'=64,'proto'=4] {'dp'}, use_global_device_ids=true, to_apply=%region_15.0 | all-reduce | flops 8192 | bytes 65536 | tf_op jit(solution)/shard_map/psum | solution.py:37
  978.0 4.2 multiply_reduce_fusion.6
  982.2 0.3 copy-done.2
  982.5 10.6 exponential_reduce_fusion
  993.1 0.1 reduce_sum.122
  993.2 17.0 %all-reduce.1 = (f32[256]{0:T(256)S(1)}, f32[128,6]{1,0:T(8,128)S(1)}) all-reduce(f32[256]{0:T(256)S(1)} %multiply_reduce_fusion.6, f32[128,6]{1,0:T(8,128)S(1)} %reduce_sum.122), channel_id=1, replica_groups=mesh['dp'=64,'proto'=4] {'proto'}, use_global_device_ids=true, to_apply=%region_17.0 | all-reduce | flops 1024 | bytes 8192 | tf_op jit(solution)/shard_map/psum | solution.py:38
  1010.3 7.9 multiply_multiply_fusion
  1018.2 10.6 reshape.74
  1028.8 11.9 fusion.11
  1040.6 0.1 sub.24
  1040.8 13.1 copy_bitcast_fusion
  1053.9 11.1 mul.210
  1065.0 24.8 %mul.211 = f32[768,8192]{1,0:T(8,128)} reshape(f32[128,6,8192]{2,1,0:T(8,128)} %mul.210) | data formatting | bytes 50331648 | tf_op jit(solution)/shard_map/mul | solution.py:55
  1089.8 12.8 mul.202
  1102.6 24.8 %mul.203 = f32[768,8192]{1,0:T(8,128)} reshape(f32[128,6,8192]{2,1,0:T(8,128)} %mul.202) | data formatting | bytes 50331648 | tf_op jit(solution)/shard_map/mul | solution.py:54
  1127.4 24.8 %multiply_convert_fusion = bf16[768,8192]{1,0:T(8,128)(2,1)S(1)} fusion(f32[768,8192]{1,0:T(8,128)} %mul.211, f32[768,8192]{1,0:T(8,128)} %mul.203, f32[768,8192]{1,0:T(8,128)} %get-tuple-element.21, f32[768]{0:T(1024)S(1)} %mul.207, f32[768]{0:T(1024)S(1)} %mul.185, f32[768]{0:T(1024)S(1)} %sub.24, f32[768]{0:T(1024)S(1)} %mul.179), kind=kLoop, calls=%fused_computation | loop fusion | flops 56623104 | bytes 88092672 | tf_op jit(solution)/shard_map/convert_element_type | solution.py:59
  1152.2 4.6 copy-done.1
  1156.8 4.3 fusion.13
  1161.1 0.0 all-reduce.7.cloned.1.call-start
  1161.2 10.5 fusion.2
  1171.7 0.6 copy-done.6
  1172.4 0.6 dynamic-slice
  1173.6 34.4 %all-reduce.5.cloned.1.call-done = f32[768,256]{1,0:T(8,128)} async-done(((f32[768,256]{1,0:T(8,128)}), f32[768,256]{1,0:T(8,128)}) %all-reduce.5.cloned.1.call-update) | async-done | bytes 786448 | tf_op jit(solution)/shard_map/psum | solution.py:65
  1208.0 1.4 multiply_reduce_fusion.7
  1209.4 1.4 subtract_divide_fusion
  1210.8 0.1 reshape.75
  1210.9 1.1 copy.15
  1212.1 202.9 %all-reduce.7.cloned.1.call-done = f32[256,8192]{1,0:T(8,128)} async-done(((f32[256,8192]{1,0:T(8,128)}), f32[256,8192]{1,0:T(8,128)}) %all-reduce.7.cloned.1.call-update) | async-done | bytes 8388624
  1415.0 1.1 fusion.6
  1416.1 247.1 %psum.70 = f32[8192]{0:T(1024)S(1)} all-reduce(f32[8192]{0:T(1024)S(1)} %fusion.6), channel_id=1, replica_groups=mesh['dp'=64,'proto'=4] {'dp'}, use_global_device_ids=true, to_apply=%region_20.0 | all-reduce | flops 8192 | bytes 65536 | tf_op jit(solution)/shard_map/psum | solution.py:76
  1663.2 1.8 multiply_add_fusion
  (26 shorter events, 0.3 us)
Async XLA Ops:
  7.2 89.4 %all-gather.7.cloned.1.call-start = ((), (), s32[]{:S(2)}) async-start(), calls=%async_computation.2 | async-start | bytes 8519680 | tf_op jit(solution)/shard_map/all_gather | solution.py:23
  7.9 171.8 %all-gather.5.cloned.1.call-start = ((), (), s32[]{:S(2)}) async-start(), calls=%async_computation.1 | async-start | bytes 8519680 | tf_op jit(solution)/shard_map/all_gather | solution.py:22
  8.6 1199.3 %all-reduce.5.cloned.1.call-start = ((), (), s32[]{:S(2)}) async-start(), calls=%async_computation | async-start | bytes 1572864 | tf_op jit(solution)/shard_map/psum | solution.py:65
  189.7 5.8 copy-start
  978.0 4.6 copy-start.2
  1127.4 29.4 %copy-start.3 = (bf16[256,8192]{1,0:T(8,128)(2,1)S(1)}, bf16[256,8192]{1,0:T(8,128)(2,1)}, u32[]{:S(2)}) copy-start(bf16[256,8192]{1,0:T(8,128)(2,1)} %divide_convert_fusion.1) | copy-start | bytes 12582916
  1152.2 4.6 copy-start.1
  1161.1 253.8 %all-reduce.7.cloned.1.call-start = ((), (), s32[]{:S(2)}) async-start(), calls=%async_computation.3 | async-start | bytes 16777216
  1171.7 0.7 copy-start.6
  1171.7 491.5 %copy-start.4 = (f32[4,8192]{1,0:T(4,128)S(1)}, f32[4,8192]{1,0:T(4,128)}, u32[]{:S(2)}) copy-start(f32[4,8192]{1,0:T(4,128)} %param.9) | copy-start | bytes 393220
  1171.7 491.5 %copy-start.5 = (f32[4,8192]{1,0:T(4,128)S(1)}, f32[4,8192]{1,0:T(4,128)}, u32[]{:S(2)}) copy-start(f32[4,8192]{1,0:T(4,128)} %param.8) | copy-start | bytes 393220
Sparse Core Ops, SparseCore 0:
  10.8 85.7 all-gather.6
  99.4 80.2 all-gather.4
  1161.2 46.7 all-reduce.4
  1211.5 203.4 all-reduce.6
where the time goes:
time: 1680 us; the launch traced here: 1670 us
  blocking collectives  1020 us (61%)
  waiting for transfers between devices  388 us (23%)
  local copies, waits for them, and re-layouts  143 us (9%)
  other arithmetic  73.2 us (4%)
  matrix products  34.1 us (2%)
    psum x3, blocking collectives, local(): recip = 1.0 / lax.psum(jnp.sum(energy * scales[:, None], axis=0), 'dp')  736 us
    psum x1, blocking collectives, local(): column_dot = lax.psum(jnp.sum(shard_s * summed_values, axis=0), 'dp')  247 us
    unnamed x5, waiting for transfers between devices  204 us
    all_gather x1, waiting for transfers between devices, local(): lax.all_gather(teacher_weight, 'dp', axis=0, tiled=True)  80.4 us
    all_gather x1, waiting for transfers between devices, local(): lax.all_gather(student_weight, 'dp', axis=0, tiled=True)  68.9 us
    unnamed x19, local copies, waits for them, and re-layouts  41.8 us
    mul x4, local copies, waits for them, and re-layouts, local(): pairing[0][None, :, None] * targets[:, 0:1, :]  38.4 us
    mul x4, local copies, waits for them, and re-layouts, local(): pairing[1][None, :, None] * targets[:, 1:2, :]  36.7 us
  transfers between devices with their start and end apart: 4, of which 4 were waited for; matrix products, arithmetic and copies ran while one was open for 2% of the time, Pallas kernels for 0%

commit v1 on v0

v1 whole, which is shorter than its diff:
```python
import jax
import jax.numpy as jnp
from jax import lax
from jax.experimental import pallas as pl
from jax.experimental.pallas import tpu as pltpu
from jax.sharding import Mesh, PartitionSpec as P

BALANCING_ROUNDS = 3
EPS = 1e-06
TEMP_T = 0.07
TEMP_S = 0.1
CROPS = 6
COUNTS = (1.0, 1.0, 2.0, 2.0, 2.0, 2.0)
NX, NZ, NC, NY = 4, 8, 2, 4
DP = ("x", "z", "core")
XY = ("x", "proto")


def spread(v, axes, n):
    return lax.all_to_all(jnp.broadcast_to(v, (n,) + v.shape), axes, 0, 0)


def other_core(v):
    return lax.ppermute(v, "core", [(0, 1), (1, 0)])


def shifted(v, axis, n, k):
    return lax.ppermute(v, axis, [(i, (i + k) % n) for i in range(n)])


def along(v, axis, n):
    me = lax.axis_index(axis)
    out = jnp.zeros((n,) + v.shape, v.dtype)
    for k in range(n):
        part = v if k == 0 else shifted(v, axis, n, k)
        out = lax.dynamic_update_index_in_dim(out, part, (me - k) % n, 0)
    return out


def slope_kernel(
    factor, images, tile, place_ref, s_ref, ps_ref, e_ref, r_ref, c_ref, a_ref, ug_ref, pg_ref, slope_ref, total_ref
):
    width = ps_ref.shape[1]

    @pl.when(pl.program_id(0) == 0)
    def _():
        total_ref[...] = jnp.zeros_like(total_ref)

    def columns(j, _):
        at = pl.ds(pl.multiple_of(j * tile, tile), tile)
        recip = r_ref[:, at] * factor
        t0 = e_ref[0, :images, at] * recip * c_ref[0, :images, :]
        t1 = e_ref[0, images:, at] * recip * c_ref[0, images:, :]
        both = t0 + t1
        for crop in range(CROPS):
            rows = slice(crop * images, (crop + 1) * images)
            scores = jnp.dot(s_ref[0, rows, :], ps_ref[:, at], preferred_element_type=jnp.float32)
            part = a_ref[0, rows, :] * jnp.exp(scores * (1.0 / TEMP_S))
            minus = t1 if crop == 0 else t0 if crop == 1 else both
            slope_ref[rows, at] = (part - minus).astype(jnp.bfloat16)
        total_ref[:, at] += lax.dot_general(
            s_ref[0], slope_ref[:, at], (((0,), (0,)), ((), ())), preferred_element_type=jnp.float32
        )
        return 0

    lax.fori_loop(0, width // tile, columns, 0)
    unit = lax.dot_general(
        slope_ref[...], ps_ref[...], (((1,), (1,)), ((), ())), preferred_element_type=jnp.float32
    )
    part = images // NY
    for crop in range(CROPS):
        for y in range(NY):
            ug_ref[0, y, crop * part : (crop + 1) * part, :] = unit[crop * images + y * part :][:part]

    @pl.when(pl.program_id(0) == pl.num_programs(0) - 1)
    def _():
        sub = pg_ref.shape[3]
        for side in range(NC):
            for k in range(NZ):
                z = lax.rem(place_ref[0] + k, NZ)
                c = lax.rem(place_ref[1] + side, NC)
                pg_ref[side, k] = total_ref[:, pl.ds(pl.multiple_of((c * NZ + z) * sub, sub), sub)]


def slopes(place, s_unit, proto_s, energy, recip, scales, amount, factor):
    groups, rows, bottleneck = s_unit.shape
    t_rows = energy.shape[1]
    width = proto_s.shape[1]
    images = rows // CROPS
    sub = width // (NC * NZ)
    return pl.pallas_call(
        lambda *refs: slope_kernel(factor, images, 512, *refs),
        grid=(groups,),
        in_specs=[
            pl.BlockSpec(memory_space=pltpu.SMEM),
            pl.BlockSpec((1, rows, bottleneck), lambda g: (g, 0, 0)),
            pl.BlockSpec((bottleneck, width), lambda g: (0, 0)),
            pl.BlockSpec((1, t_rows, width), lambda g: (g, 0, 0)),
            pl.BlockSpec((1, width), lambda g: (0, 0)),
            pl.BlockSpec((1, t_rows, 1), lambda g: (g, 0, 0)),
            pl.BlockSpec((1, rows, 1), lambda g: (g, 0, 0)),
        ],
        out_specs=[
            pl.BlockSpec((1, NY, rows // NY, bottleneck), lambda g: (g, 0, 0, 0)),
            pl.BlockSpec((NC, NZ, bottleneck, sub), lambda g: (0, 0, 0, 0)),
        ],
        out_shape=[
            jax.ShapeDtypeStruct((groups, NY, rows // NY, bottleneck), jnp.float32),
            jax.ShapeDtypeStruct((NC, NZ, bottleneck, sub), jnp.float32),
        ],
        scratch_shapes=[pltpu.VMEM((rows, width), jnp.bfloat16), pltpu.VMEM((bottleneck, width), jnp.float32)],
        compiler_params=pltpu.CompilerParams(vmem_limit_bytes=48 * 1024 * 1024),
        cost_estimate=pl.CostEstimate(
            flops=6 * groups * rows * bottleneck * width,
            bytes_accessed=4 * groups * (t_rows * width + rows * bottleneck),
            transcendentals=groups * rows * width,
        ),
    )(place, s_unit, proto_s, energy, recip, scales, amount)


def local(teacher_feats, student_embeddings, teacher_weight, student_weight):
    images, _, bottleneck = teacher_feats.shape
    rows_here, wide = student_weight.shape
    sub = wide // (NX * NZ * NC)
    width = wide // NX
    total_k = wide * NY
    s_rows = images * CROPS
    t_rows = images * 2

    shards = jnp.stack([teacher_weight, student_weight]).reshape(2 * rows_here, NX * NZ * NC, sub)
    moved = lax.all_to_all(shards.transpose(1, 0, 2), DP, 0, 0)
    moved = moved.reshape(NX * NZ * NC, 2, rows_here, sub)
    cols_t = moved[:, 0].reshape(bottleneck, sub)
    cols_s = moved[:, 1].reshape(bottleneck, sub)
    col_t = jnp.sqrt(jnp.sum(cols_t * cols_t, axis=0) + EPS)
    col_s = jnp.sqrt(jnp.sum(cols_s * cols_s, axis=0) + EPS)
    mine_t = (cols_t / col_t).astype(jnp.bfloat16)
    mine_s = (cols_s / col_s).astype(jnp.bfloat16)

    place = jnp.stack([lax.axis_index("z"), lax.axis_index("core")]).astype(jnp.int32)

    def gather_columns(mine):
        own = spread(mine, "z", NZ)
        other = other_core(own)
        first = lax.axis_index("core") == 0
        both = jnp.stack([jnp.where(first, own, other), jnp.where(first, other, own)])
        return both.transpose(2, 0, 1, 3).reshape(bottleneck, width)

    t_float = teacher_feats.transpose(1, 0, 2).reshape(t_rows, bottleneck).astype(jnp.float32)
    t_unit = (t_float / jnp.sqrt(jnp.sum(t_float * t_float, axis=1, keepdims=True) + EPS)).astype(jnp.bfloat16)
    s_raw = student_embeddings.transpose(1, 0, 2).reshape(s_rows, bottleneck).astype(jnp.float32)
    s_norm = jnp.sqrt(jnp.sum(s_raw * s_raw, axis=1, keepdims=True) + EPS)
    s_float = s_raw / s_norm
    s_unit = s_float.astype(jnp.bfloat16)
    t_all = along(t_unit, "x", NX)
    s_all = lax.all_gather(s_unit, "x")

    proto_t = gather_columns(mine_t)
    energy = jnp.exp(
        jnp.dot(t_all.reshape(NX * t_rows, bottleneck), proto_t, preferred_element_type=jnp.float32) / TEMP_T
    )
    proto_s = lax.all_gather(mine_s, ("core", "z")).transpose(1, 0, 2).reshape(bottleneck, width)
    scores = jnp.dot(s_all.reshape(NX * s_rows, bottleneck), proto_s, preferred_element_type=jnp.float32)
    expsum = jnp.sum(jnp.exp(scores / TEMP_S), axis=1)

    scales = None
    for round_number in range(BALANCING_ROUNDS):
        weighted = energy if scales is None else energy * scales[:, None]
        over_rows = jnp.sum(weighted, axis=0)
        recip = 1.0 / jnp.sum(spread(over_rows, ("z", "core"), NZ * NC), axis=0)
        over_cols = jnp.sum(energy * recip[None, :], axis=1)
        if round_number == BALANCING_ROUNDS - 1:
            over_cols = jnp.concatenate([over_cols, expsum])
        summed = jnp.sum(spread(over_cols, XY, NX * NY), axis=0)
        scales = 1.0 / summed[: NX * t_rows]
    expsum = summed[NX * t_rows :].reshape(NX, CROPS, images)

    factor = total_k / 16.0
    amount = factor * jnp.array(COUNTS, jnp.float32)[None, :, None] / expsum
    unit_part, proto_part = slopes(
        place,
        s_all,
        proto_s,
        energy.reshape(NX, t_rows, width),
        recip.reshape(1, width),
        scales.reshape(NX, t_rows, 1),
        amount.reshape(NX, s_rows, 1),
        factor,
    )

    half = (proto_part[0] + other_core(proto_part[1])) * (1.0 / 512.0)
    proto_grad = half[0]
    for k in range(1, NZ):
        proto_grad = proto_grad + shifted(half[k].astype(jnp.float16), "z", NZ, k).astype(jnp.float32)
    proto_grad = proto_grad * 512.0
    proto_float = mine_s.astype(jnp.float32)
    column_dot = jnp.sum(proto_float * proto_grad, axis=0)
    grad_cols = (proto_grad - proto_float * column_dot) / col_s
    grad_rows = lax.all_to_all(grad_cols.reshape(NX * NZ * NC, rows_here, sub), DP, 0, 0)
    weight_grad = grad_rows.transpose(1, 0, 2).reshape(rows_here, wide)
    teacher_new = 0.994 * teacher_weight + 0.006 * (student_weight - 0.5 * weight_grad)

    quarter = images // NY
    sent = (unit_part.reshape(NX * NY, CROPS * quarter, bottleneck) * 4.0).astype(jnp.float16)
    unit_grad = jnp.sum(lax.all_to_all(sent, XY, 0, 0).astype(jnp.float32), axis=0) * 0.25
    unit_grad = unit_grad.reshape(CROPS, quarter, bottleneck)
    first = lax.axis_index("proto") * quarter
    part_float = lax.dynamic_slice_in_dim(s_float.reshape(CROPS, images, bottleneck), first, quarter, 1)
    part_norm = lax.dynamic_slice_in_dim(s_norm.reshape(CROPS, images, 1), first, quarter, 1)
    fgrad = (unit_grad - part_float * jnp.sum(part_float * unit_grad, axis=2, keepdims=True)) / part_norm
    feature_grad = along(fgrad.transpose(1, 0, 2), "proto", NY).reshape(images, CROPS, bottleneck)
    return weight_grad, teacher_new, feature_grad


def solution(mesh):
    fine = Mesh(mesh.devices.reshape(NX, NZ, NC, NY), ("x", "z", "core", "proto"))
    in_specs = (P(DP, None, None), P(DP, None, None), P(DP, "proto"), P(DP, "proto"))
    out_specs = (P(DP, "proto"), P(DP, "proto"), P(DP, None, None))
    return jax.shard_map(local, mesh=fine, in_specs=in_specs, out_specs=out_specs, check_vma=False)
```

time: 1680 us -> 266 us (0.16)
  blocking collectives: 1020 us -> 0 us
  waiting for transfers between devices: 388 us -> 81.1 us
  local copies, waits for them, and re-layouts: 143 us -> 14.3 us
  starting transfers between devices: 0.16 us -> 81 us
  other arithmetic: 73.2 us -> 40.4 us
  matrix products: 34.1 us -> 9.96 us
  Pallas kernels: 0 us -> 22.1 us
    psum x7 -> x0, blocking collectives: 1020 us -> none  [the longest x3 736 us: local(): recip = 1.0 / lax.psum(jnp.sum(energy * scales[:, None], axis=0), 'dp')]
    unnamed x5 -> x2, waiting for transfers between devices: 204 us -> 0.06 us
    all_gather x2, waiting for transfers between devices: 149 us -> 0.03 us  [the longest x1 0.02 us: local(): lax.all_gather(mine_s, ('core', 'z')).transpose(1, 0, 2)]
    mul x10 -> x0, local copies, waits for them, and re-layouts: 75.9 us -> none  [the longest x4 38.4 us: local(): pairing[0][None, :, None] * targets[:, 0:1, :]]
    all_to_all x0 -> x10, waiting for transfers between devices: none -> 64.4 us  [the longest x7 48.1 us: spread(): return lax.all_to_all(jnp.broadcast_to(v, (n,) + v.shape), axes, 0, 0)]
    all_to_all x0 -> x10, starting transfers between devices: none -> 57.2 us  [the longest x7 33 us: spread(): return lax.all_to_all(jnp.broadcast_to(v, (n,) + v.shape), axes, 0, 0)]
    unnamed x19 -> x13, local copies, waits for them, and re-layouts: 41.8 us -> 0.94 us
    psum x1 -> x0, waiting for transfers between devices: 34.4 us -> none  [local(): unit_grad = lax.psum(unit_portion, 'proto')]
  transfers between devices with their start and end apart: 4 -> 27, of which waited for: 4 -> 15; matrix products, arithmetic and copies ran while one was open for 2% -> 19% of each run, Pallas kernels for 0% -> 0%
where the time goes in v1:
time: 266 us; the launch traced here: 263 us
  waiting for transfers between devices  81.1 us (30%)
  starting transfers between devices  81 us (30%)
  other arithmetic  40.4 us (15%)
  Pallas kernels  22.1 us (8%)
  between operations  14.6 us (5%)
  local copies, waits for them, and re-layouts  14.3 us (5%)
  matrix products  9.96 us (4%)
    all_to_all x7, waiting for transfers between devices, spread(): return lax.all_to_all(jnp.broadcast_to(v, (n,) + v.shape), axes, 0, 0)  48.1 us
    all_to_all x7, starting transfers between devices, spread(): return lax.all_to_all(jnp.broadcast_to(v, (n,) + v.shape), axes, 0, 0)  33 us
    ppermute x13, starting transfers between devices, shifted(): return lax.ppermute(v, axis, [(i, (i + k) % n) for i in range(n)])  23.7 us
    pallas_call x1, Pallas kernels, slopes(): pl.pallas_call(lambda *refs: slope_kernel(factor, images, 512, *refs), gr...  22.1 us
    ppermute x13, waiting for transfers between devices, shifted(): return lax.ppermute(v, axis, [(i, (i + k) % n) for i in range(n)])  14.7 us
    reduce_sum x3, other arithmetic, local(): over_cols = jnp.sum(energy * recip[None, :], axis=1)  12.2 us
    all_to_all x1, starting transfers between devices, local(): moved = lax.all_to_all(shards.transpose(1, 0, 2), DP, 0, 0)  11.6 us
    all_to_all x1, waiting for transfers between devices, local(): moved = lax.all_to_all(shards.transpose(1, 0, 2), DP, 0, 0)  9.79 us
  transfers between devices with their start and end apart: 27, of which 15 were waited for; matrix products, arithmetic and copies ran while one was open for 19% of the time, Pallas kernels for 0%

profile of v1, /device:TPU:32, one launch (start us, length us, event | category | flops | bytes accessed | tf_op | source)
XLA Modules:
  0.0 263.3 jit_solution(12053935687326043600)
XLA Ops:
  7.2 1.0 pad_maximum_fusion.1
  8.4 0.9 copy.100
  9.2 11.6 %all-to-all-start = ((f32[64,8,128]{2,1,0:T(8,128)}), f32[64,8,128]{2,1,0:T(8,128)S(1)}, u32[]{:S(2)}, u32[]{:S(2)}) async-start(f32[64,8,128]{2,1,0:T(8,128)} %copy.100), calls=%async_computation | async-start | bytes 524288 | tf_op jit(solution)/shard_map/all_to_all | solution.py:131
  20.8 1.0 multiply_reduce_fusion.6
  21.9 0.9 copy_convert_fusion
  22.8 9.8 %all-to-all-done = f32[64,8,128]{2,1,0:T(8,128)S(1)} async-done(((f32[64,8,128]{2,1,0:T(8,128)}), f32[64,8,128]{2,1,0:T(8,128)S(1)}, u32[]{:S(2)}, u32[]{:S(2)}) %all-to-all-start) | async-done | bytes 262176 | tf_op jit(solution)/shard_map/all_to_all | solution.py:131
  33.0 0.8 broadcast_in_dim.68
  33.8 4.8 %all-to-all-start.1 = ((bf16[8,256,128]{1,2,0:T(8,128)(2,1)}), bf16[8,256,128]{1,2,0:T(8,128)(2,1)S(1)}, u32[]{:S(2)}, u32[]{:S(2)}) async-start(bf16[8,256,128]{1,2,0:T(8,128)(2,1)} %broadcast_in_dim.68), calls=%async_computation.1 | async-start | bytes 1048576 | tf_op jit(solution)/shard_map/all_to_all | solution.py:20
  38.7 0.7 collective-permute-start
  39.4 2.7 %collective-permute-start.1 = (bf16[256,256]{1,0:T(8,128)(2,1)S(1)}, bf16[256,256]{1,0:T(8,128)(2,1)S(1)}, u32[]{:S(2)}, u32[]{:S(2)}) collective-permute-start(bf16[256,256]{1,0:T(8,128)(2,1)S(1)} %fusion.6), channel_id=1, source_target_pairs={{0,128},{64,192},{128,0},{192,64},{1,129},{65,193},{129,1},{193,65... | collective-permute-start | bytes 393224 | tf_op jit(solution)/shard_map/ppermute | solution.py:28
  42.1 1.4 collective-permute-start.2
  43.4 1.2 multiply_reduce_fusion.5
  44.6 1.9 fusion.5
  46.8 8.1 %all-to-all-done.1 = bf16[8,256,128]{1,2,0:T(8,128)(2,1)S(1)} async-done(((bf16[8,256,128]{1,2,0:T(8,128)(2,1)}), bf16[8,256,128]{1,2,0:T(8,128)(2,1)S(1)}, u32[]{:S(2)}, u32[]{:S(2)}) %all-to-all-start.1) | async-done | bytes 524320 | tf_op jit(solution)/shard_map/all_to_all | solution.py:20
  55.0 1.8 collective-permute-done.3
  57.0 4.6 %fusion.25 = (f32[2048]{0:T(1024)S(1)}, f32[1024,2048]{1,0:T(8,128)}) fusion(bf16[1024,256]{1,0:T(8,128)(2,1)S(1)} %bitcast.137, bf16[256,2048]{0,1:T(8,128)(2,1)S(1)} %bitcast.136), kind=kOutput, calls=%fused_computation.88 | convolution fusion | flops 1077934080 | bytes 9969664 | tf_op jit(solution)/shard_map/dot_general | solution.py:160
  62.3 4.8 %all-to-all-start.2 = ((f32[16,1,2048]{2,1,0:T(1,128)}), f32[16,1,2048]{2,1,0:T(1,128)S(1)}, u32[]{:S(2)}, u32[]{:S(2)}) async-start(f32[16,1,2048]{2,1,0:T(1,128)} %broadcast_in_dim.69), calls=%async_computation.2 | async-start | bytes 262144 | tf_op jit(solution)/shard_map/all_to_all | solution.py:20
  67.2 7.5 %all-to-all-done.2 = f32[16,1,2048]{2,1,0:T(1,128)S(1)} async-done(((f32[16,1,2048]{2,1,0:T(1,128)}), f32[16,1,2048]{2,1,0:T(1,128)S(1)}, u32[]{:S(2)}, u32[]{:S(2)}) %all-to-all-start.2) | async-done | bytes 131104 | tf_op jit(solution)/shard_map/all_to_all | solution.py:20
  74.8 4.0 %multiply_reduce_fusion.4 = f32[1024]{0:T(1024)S(1)} fusion(f32[1024,2048]{1,0:T(8,128)} %get-tuple-element.27, f32[2048]{0:T(1024)S(1)} %broadcast_divide_fusion.3), kind=kLoop, calls=%fused_computation.6 | loop fusion | flops 4193280 | bytes 8400896 | tf_op jit(solution)/shard_map/reduce_sum | solution.py:171
  79.5 6.4 %all-to-all-start.3 = ((f32[16,1,1024]{2,1,0:T(1,128)}), f32[16,1,1024]{2,1,0:T(1,128)S(1)}, u32[]{:S(2)}, u32[]{:S(2)}) async-start(f32[16,1,1024]{2,1,0:T(1,128)} %broadcast_in_dim.70), calls=%async_computation.3 | async-start | bytes 131072 | tf_op jit(solution)/shard_map/all_to_all | solution.py:20
  86.7 6.9 %all-to-all-done.3 = f32[16,1,1024]{2,1,0:T(1,128)S(1)} async-done(((f32[16,1,1024]{2,1,0:T(1,128)}), f32[16,1,1024]{2,1,0:T(1,128)S(1)}, u32[]{:S(2)}, u32[]{:S(2)}) %all-to-all-start.3) | async-done | bytes 65568 | tf_op jit(solution)/shard_map/all_to_all | solution.py:20
  93.7 4.0 %multiply_reduce_fusion.3 = f32[2048]{0:T(1024)S(1)} fusion(f32[1024,2048]{1,0:T(8,128)} %get-tuple-element.27, f32[1024]{0:T(1024)S(1)} %broadcast_divide_fusion.5), kind=kLoop, calls=%fused_computation.5 | loop fusion | flops 4192256 | bytes 8400896 | tf_op jit(solution)/shard_map/reduce_sum | solution.py:169
  98.4 4.6 %all-to-all-start.4 = ((f32[16,1,2048]{2,1,0:T(1,128)}), f32[16,1,2048]{2,1,0:T(1,128)S(1)}, u32[]{:S(2)}, u32[]{:S(2)}) async-start(f32[16,1,2048]{2,1,0:T(1,128)} %broadcast_in_dim.71), calls=%async_computation.4 | async-start | bytes 262144 | tf_op jit(solution)/shard_map/all_to_all | solution.py:20
  103.1 8.0 %all-to-all-done.4 = f32[16,1,2048]{2,1,0:T(1,128)S(1)} async-done(((f32[16,1,2048]{2,1,0:T(1,128)}), f32[16,1,2048]{2,1,0:T(1,128)S(1)}, u32[]{:S(2)}, u32[]{:S(2)}) %all-to-all-start.4) | async-done | bytes 131104 | tf_op jit(solution)/shard_map/all_to_all | solution.py:20
  111.2 4.1 %multiply_reduce_fusion.2 = f32[1024]{0:T(1024)S(1)} fusion(f32[1024,2048]{1,0:T(8,128)} %get-tuple-element.27, f32[2048]{0:T(1024)S(1)} %broadcast_divide_fusion.2), kind=kLoop, calls=%fused_computation.4 | loop fusion | flops 4193280 | bytes 8400896 | tf_op jit(solution)/shard_map/reduce_sum | solution.py:171
  115.9 3.6 %all-to-all-start.5 = ((f32[16,1,1024]{2,1,0:T(1,128)}), f32[16,1,1024]{2,1,0:T(1,128)S(1)}, u32[]{:S(2)}, u32[]{:S(2)}) async-start(f32[16,1,1024]{2,1,0:T(1,128)} %broadcast_in_dim.72), calls=%async_computation.5 | async-start | bytes 131072 | tf_op jit(solution)/shard_map/all_to_all | solution.py:20
  119.6 7.6 %all-to-all-done.5 = f32[16,1,1024]{2,1,0:T(1,128)S(1)} async-done(((f32[16,1,1024]{2,1,0:T(1,128)}), f32[16,1,1024]{2,1,0:T(1,128)S(1)}, u32[]{:S(2)}, u32[]{:S(2)}) %all-to-all-start.5) | async-done | bytes 65568 | tf_op jit(solution)/shard_map/all_to_all | solution.py:20
  127.2 4.0 %multiply_reduce_fusion.1 = f32[2048]{0:T(1024)S(1)} fusion(f32[1024,2048]{1,0:T(8,128)} %get-tuple-element.27, f32[1024]{0:T(1024)S(1)} %broadcast_divide_fusion.4), kind=kLoop, calls=%fused_computation.3 | loop fusion | flops 4192256 | bytes 8400896 | tf_op jit(solution)/shard_map/reduce_sum | solution.py:169
  132.0 5.2 %all-to-all-start.6 = ((f32[16,1,2048]{2,1,0:T(1,128)}), f32[16,1,2048]{2,1,0:T(1,128)S(1)}, u32[]{:S(2)}, u32[]{:S(2)}) async-start(f32[16,1,2048]{2,1,0:T(1,128)} %broadcast_in_dim.73), calls=%async_computation.6 | async-start | bytes 262144 | tf_op jit(solution)/shard_map/all_to_all | solution.py:20
  137.2 5.3 %exponential_reduce_fusion = f32[3072]{0:T(1024)S(1)} fusion(bf16[3072,256]{1,0:T(8,128)(2,1)} %bitcast.134, bf16[16,256,128]{2,1,0:T(8,128)(2,1)} %all-gather.5.cloned.1.call-done), kind=kOutput, calls=%fused_computation.1 | convolution fusion | flops 3233805312 | bytes 2633728 | tf_op jit(solution)/shard_map/dot_general | solution.py:163
  142.5 2.0 all-to-all-done.6
  144.6 4.1 %multiply_reduce_fusion = f32[1024]{0:T(1024)S(1)} fusion(f32[1024,2048]{1,0:T(8,128)} %get-tuple-element.27, f32[2048]{0:T(1024)S(1)} %broadcast_divide_fusion.1), kind=kLoop, calls=%fused_computation.2 | loop fusion | flops 4193280 | bytes 8400896 | tf_op jit(solution)/shard_map/reduce_sum | solution.py:171
  148.8 0.9 broadcast_in_dim.74
  149.7 3.5 %all-to-all-start.7 = ((f32[16,1,4096]{2,1,0:T(1,128)}), f32[16,1,4096]{2,1,0:T(1,128)S(1)}, u32[]{:S(2)}, u32[]{:S(2)}) async-start(f32[16,1,4096]{2,1,0:T(1,128)} %broadcast_in_dim.74), calls=%async_computation.7 | async-start | bytes 524288 | tf_op jit(solution)/shard_map/all_to_all | solution.py:20
  153.2 1.4 copy_bitcast_fusion.refs_2_
  154.6 8.2 %all-to-all-done.7 = f32[16,1,4096]{2,1,0:T(1,128)S(1)} async-done(((f32[16,1,4096]{2,1,0:T(1,128)}), f32[16,1,4096]{2,1,0:T(1,128)S(1)}, u32[]{:S(2)}, u32[]{:S(2)}) %all-to-all-start.7) | async-done | bytes 262176 | tf_op jit(solution)/shard_map/all_to_all | solution.py:20
  163.0 2.6 reshape.334
  165.9 1.6 broadcast_divide_fusion.refs_6_
  167.5 22.1 %shard_map.76 = (f32[4,4,192,256]{3,2,1,0:T(8,128)}, f32[2,8,256,128]{3,2,1,0:T(8,128)}) custom-call(s32[2]{0:T(128)S(1)} %pad_add_fusion.refs_0_, bf16[4,768,256]{2,1,0:T(8,128)(2,1)S(1)} %copy-done, bf16[256,2048]{1,0:T(8,128)(2,1)S(1)} %copy_bitcast_fusion.refs_2_, f32[4,256,2048]{2,1,0:T(8,128)} %bitcast.135, f32[1,2048]{1,0:T(1,128)S(1)} %bitcast.133, ...), custom_call_target="tpu_custom_call" | custom-call | flops 9663676416 | bytes 11534336 | tf_op jit(solution)/shard_map/pallas_call | solution.py:91
  189.6 1.3 slice_bitcast_fusion
  191.1 3.4 %multiply_convert_fusion = f16[4,4,192,256]{3,2,1,0:T(8,128)(2,1)} fusion(f32[4,4,192,256]{3,2,1,0:T(8,128)} %get-tuple-element.6), kind=kLoop, calls=%fused_computation.9 | loop fusion | flops 1572864 | bytes 4718592 | tf_op jit(solution)/shard_map/convert_element_type | solution.py:204
  194.5 3.8 %all-to-all-start.9 = ((f16[16,192,256]{2,1,0:T(8,128)(2,1)}), f16[16,192,256]{2,1,0:T(8,128)(2,1)S(1)}, u32[]{:S(2)}, u32[]{:S(2)}) async-start(f16[16,192,256]{2,1,0:T(8,128)(2,1)} %bitcast.45), calls=%async_computation.9 | async-start | bytes 3145728 | tf_op jit(solution)/shard_map/all_to_all | solution.py:205
  198.3 1.7 fusion.23
  200.1 0.8 slice_bitcast_fusion.8
  200.8 1.2 collective-permute-start.10
  202.0 1.0 collective-permute-start.11
  203.0 0.9 convert_bitcast_fusion
  204.0 1.1 collective-permute-start.5
  205.1 2.9 %collective-permute-start.6 = (f16[256,128]{1,0:T(8,128)(2,1)}, f16[256,128]{1,0:T(8,128)(2,1)S(1)}, u32[]{:S(2)}, u32[]{:S(2)}) collective-permute-start(f16[256,128]{1,0:T(8,128)(2,1)} %get-tuple-element.21), channel_id=1, source_target_pairs={{0,16},{8,24},{16,32},{24,40},{32,48},{40,56},{48,0},{56,8},{1,17}... | collective-permute-start | bytes 196616 | tf_op jit(solution)/shard_map/ppermute | solution.py:28
  207.9 0.8 collective-permute-start.7
  208.8 4.2 %collective-permute-start.8 = (f16[256,128]{1,0:T(8,128)(2,1)S(1)}, f16[256,128]{1,0:T(8,128)(2,1)S(1)}, u32[]{:S(2)}, u32[]{:S(2)}) collective-permute-start(f16[256,128]{1,0:T(8,128)(2,1)S(1)} %get-tuple-element.19), channel_id=1, source_target_pairs={{0,32},{8,40},{16,48},{24,56},{32,0},{40,8},{48,16},{56,24},{1,33}... | collective-permute-start | bytes 196616 | tf_op jit(solution)/shard_map/ppermute | solution.py:28
  213.0 2.0 collective-permute-start.9
  215.1 3.6 %collective-permute-done.7 = f16[256,128]{1,0:T(8,128)(2,1)S(1)} collective-permute-done((f16[256,128]{1,0:T(8,128)(2,1)}, f16[256,128]{1,0:T(8,128)(2,1)S(1)}, u32[]{:S(2)}, u32[]{:S(2)}) %collective-permute-start.7) | collective-permute-done | bytes 65568 | tf_op jit(solution)/shard_map/ppermute | solution.py:28
  218.7 2.6 collective-permute-done.9
  221.3 1.0 fusion.9
  223.2 8.8 %all-to-all-start.8 = ((f32[64,4,128]{2,1,0:T(4,128)}), f32[64,4,128]{2,1,0:T(4,128)S(1)}, u32[]{:S(2)}, u32[]{:S(2)}) async-start(f32[64,4,128]{2,1,0:T(4,128)} %bitcast.41), calls=%async_computation.8 | async-start | bytes 262144 | tf_op jit(solution)/shard_map/all_to_all | solution.py:199
  232.4 1.9 bitcast_dynamic-update-slice_fusion.3
  234.3 1.5 collective-permute-start.12
  235.9 6.2 %all-to-all-done.8 = f32[64,4,128]{2,1,0:T(4,128)S(1)} async-done(((f32[64,4,128]{2,1,0:T(4,128)}), f32[64,4,128]{2,1,0:T(4,128)S(1)}, u32[]{:S(2)}, u32[]{:S(2)}) %all-to-all-start.8) | async-done | bytes 131104 | tf_op jit(solution)/shard_map/all_to_all | solution.py:199
  242.1 0.7 multiply_add_fusion
  242.8 3.0 %collective-permute-start.13 = (f32[32,6,256]{2,0,1:T(8,128)S(1)}, f32[32,6,256]{2,0,1:T(8,128)S(1)}, u32[]{:S(2)}, u32[]{:S(2)}) collective-permute-start(f32[32,6,256]{2,0,1:T(8,128)S(1)} %bitcast.150), channel_id=1, source_target_pairs={{0,2},{1,3},{2,0},{3,1},{4,6},{5,7},{6,4},{7,5},{8,10},{9,11},{10,... | collective-permute-start | bytes 589832 | tf_op jit(solution)/shard_map/ppermute | solution.py:28
  245.8 1.1 collective-permute-start.14
  247.0 4.3 %collective-permute-done.13 = f32[32,6,256]{2,0,1:T(8,128)S(1)} collective-permute-done((f32[32,6,256]{2,0,1:T(8,128)S(1)}, f32[32,6,256]{2,0,1:T(8,128)S(1)}, u32[]{:S(2)}, u32[]{:S(2)}) %collective-permute-start.13) | collective-permute-done | bytes 196640 | tf_op jit(solution)/shard_map/ppermute | solution.py:28
  251.3 4.3 %collective-permute-done.14 = f32[32,6,256]{2,0,1:T(8,128)S(1)} collective-permute-done((f32[32,6,256]{2,0,1:T(8,128)S(1)}, f32[32,6,256]{2,0,1:T(8,128)S(1)}, u32[]{:S(2)}, u32[]{:S(2)}) %collective-permute-start.14) | collective-permute-done | bytes 196640 | tf_op jit(solution)/shard_map/ppermute | solution.py:28
  (82 shorter events, 8.9 us)
Async XLA Ops:
  9.2 23.3 %all-to-all-start = ((f32[64,8,128]{2,1,0:T(8,128)}), f32[64,8,128]{2,1,0:T(8,128)S(1)}, u32[]{:S(2)}, u32[]{:S(2)}) async-start(f32[64,8,128]{2,1,0:T(8,128)} %copy.100), calls=%async_computation | async-start | bytes 524288 | tf_op jit(solution)/shard_map/all_to_all | solution.py:131
  33.8 21.1 %all-to-all-start.1 = ((bf16[8,256,128]{1,2,0:T(8,128)(2,1)}), bf16[8,256,128]{1,2,0:T(8,128)(2,1)S(1)}, u32[]{:S(2)}, u32[]{:S(2)}) async-start(bf16[8,256,128]{1,2,0:T(8,128)(2,1)} %broadcast_in_dim.68), calls=%async_computation.1 | async-start | bytes 1048576 | tf_op jit(solution)/shard_map/all_to_all | solution.py:20
  38.6 98.6 %all-gather.3.cloned.1.call-start = ((), (), s32[]{:S(2)}) async-start(), calls=%async_computation.10 | async-start | bytes 1966080 | tf_op jit(solution)/shard_map/all_gather | solution.py:156
  38.7 16.2 %collective-permute-start = (bf16[256,256]{1,0:T(8,128)(2,1)S(1)}, bf16[256,256]{1,0:T(8,128)(2,1)S(1)}, u32[]{:S(2)}, u32[]{:S(2)}) collective-permute-start(bf16[256,256]{1,0:T(8,128)(2,1)S(1)} %fusion.6), channel_id=1, source_target_pairs={{0,64},{64,128},{128,192},{192,0},{1,65},{65,129},{129,193},{193,1... | collective-permute-start | bytes 393224 | tf_op jit(solution)/shard_map/ppermute | solution.py:28
  39.4 15.5 %collective-permute-start.1 = (bf16[256,256]{1,0:T(8,128)(2,1)S(1)}, bf16[256,256]{1,0:T(8,128)(2,1)S(1)}, u32[]{:S(2)}, u32[]{:S(2)}) collective-permute-start(bf16[256,256]{1,0:T(8,128)(2,1)S(1)} %fusion.6), channel_id=1, source_target_pairs={{0,128},{64,192},{128,0},{192,64},{1,129},{65,193},{129,1},{193,65... | collective-permute-start | bytes 393224 | tf_op jit(solution)/shard_map/ppermute | solution.py:28
  42.1 12.9 %collective-permute-start.2 = (bf16[256,256]{1,0:T(8,128)(2,1)S(1)}, bf16[256,256]{1,0:T(8,128)(2,1)S(1)}, u32[]{:S(2)}, u32[]{:S(2)}) collective-permute-start(bf16[256,256]{1,0:T(8,128)(2,1)S(1)} %fusion.6), channel_id=1, source_target_pairs={{0,192},{64,0},{128,64},{192,128},{1,193},{65,1},{129,65},{193,129... | collective-permute-start | bytes 393224 | tf_op jit(solution)/shard_map/ppermute | solution.py:28
  54.9 1.9 collective-permute-start.3
  62.3 12.3 %all-to-all-start.2 = ((f32[16,1,2048]{2,1,0:T(1,128)}), f32[16,1,2048]{2,1,0:T(1,128)S(1)}, u32[]{:S(2)}, u32[]{:S(2)}) async-start(f32[16,1,2048]{2,1,0:T(1,128)} %broadcast_in_dim.69), calls=%async_computation.2 | async-start | bytes 262144 | tf_op jit(solution)/shard_map/all_to_all | solution.py:20
  74.8 28.3 %copy-start.5 = (f32[6]{0:T(128)S(1)}, f32[6]{0:T(128)}, u32[]{:S(2)}) copy-start(f32[6]{0:T(128)} %constant.134) | copy-start | bytes 76
  79.5 14.1 %all-to-all-start.3 = ((f32[16,1,1024]{2,1,0:T(1,128)}), f32[16,1,1024]{2,1,0:T(1,128)S(1)}, u32[]{:S(2)}, u32[]{:S(2)}) async-start(f32[16,1,1024]{2,1,0:T(1,128)} %broadcast_in_dim.70), calls=%async_computation.3 | async-start | bytes 131072 | tf_op jit(solution)/shard_map/all_to_all | solution.py:20
  85.9 51.3 %all-gather.5.cloned.1.call-start = ((), (), s32[]{:S(2)}) async-start(), calls=%async_computation.11 | async-start | bytes 1114112 | tf_op jit(solution)/shard_map/all_gather | solution.py:162
  98.4 12.7 %all-to-all-start.4 = ((f32[16,1,2048]{2,1,0:T(1,128)}), f32[16,1,2048]{2,1,0:T(1,128)S(1)}, u32[]{:S(2)}, u32[]{:S(2)}) async-start(f32[16,1,2048]{2,1,0:T(1,128)} %broadcast_in_dim.71), calls=%async_computation.4 | async-start | bytes 262144 | tf_op jit(solution)/shard_map/all_to_all | solution.py:20
  115.9 11.3 %all-to-all-start.5 = ((f32[16,1,1024]{2,1,0:T(1,128)}), f32[16,1,1024]{2,1,0:T(1,128)S(1)}, u32[]{:S(2)}, u32[]{:S(2)}) async-start(f32[16,1,1024]{2,1,0:T(1,128)} %broadcast_in_dim.72), calls=%async_computation.5 | async-start | bytes 131072 | tf_op jit(solution)/shard_map/all_to_all | solution.py:20
  132.0 12.6 %all-to-all-start.6 = ((f32[16,1,2048]{2,1,0:T(1,128)}), f32[16,1,2048]{2,1,0:T(1,128)S(1)}, u32[]{:S(2)}, u32[]{:S(2)}) async-start(f32[16,1,2048]{2,1,0:T(1,128)} %broadcast_in_dim.73), calls=%async_computation.6 | async-start | bytes 262144 | tf_op jit(solution)/shard_map/all_to_all | solution.py:20
  144.6 22.9 %copy-start = (bf16[4,768,256]{2,1,0:T(8,128)(2,1)S(1)}, bf16[4,768,256]{2,1,0:T(8,128)(2,1)}, u32[]{:S(2)}) copy-start(bf16[4,768,256]{2,1,0:T(8,128)(2,1)} %all-gather.3.cloned.1.call-done.refs_1_) | copy-start | bytes 4718596
  149.7 13.1 %all-to-all-start.7 = ((f32[16,1,4096]{2,1,0:T(1,128)}), f32[16,1,4096]{2,1,0:T(1,128)S(1)}, u32[]{:S(2)}, u32[]{:S(2)}) async-start(f32[16,1,4096]{2,1,0:T(1,128)} %broadcast_in_dim.74), calls=%async_computation.7 | async-start | bytes 524288 | tf_op jit(solution)/shard_map/all_to_all | solution.py:20
  189.6 13.4 %copy-start.1 = (bf16[128,6,256]{2,0,1:T(8,128)(2,1)S(1)}, bf16[128,6,256]{2,0,1:T(8,128)(2,1)}, u32[]{:S(2)}) copy-start(bf16[128,6,256]{2,0,1:T(8,128)(2,1)} %param.6) | copy-start | bytes 1179652
  190.9 7.4 %collective-permute-start.4 = (f32[8,256,128]{2,1,0:T(8,128)S(1)}, f32[8,256,128]{2,1,0:T(8,128)}, u32[]{:S(2)}, u32[]{:S(2)}) collective-permute-start(f32[8,256,128]{2,1,0:T(8,128)S(1)} %slice_bitcast_fusion), channel_id=1, source_target_pairs={{0,4},{4,0},{1,5},{5,1},{2,6},{6,2},{3,7},{7,3},{8,12},{12,8},{9,1... | collective-permute-start | bytes 3145736 | tf_op jit(solution)/shard_map/ppermute | solution.py:24
  194.5 47.6 %copy-start.3 = (f32[4,8192]{1,0:T(4,128)S(1)}, f32[4,8192]{1,0:T(4,128)}, u32[]{:S(2)}) copy-start(f32[4,8192]{1,0:T(4,128)} %param.8) | copy-start | bytes 393220
  194.5 47.6 %copy-start.4 = (f32[4,8192]{1,0:T(4,128)S(1)}, f32[4,8192]{1,0:T(4,128)}, u32[]{:S(2)}) copy-start(f32[4,8192]{1,0:T(4,128)} %param.7) | copy-start | bytes 393220
  194.5 28.8 %all-to-all-start.9 = ((f16[16,192,256]{2,1,0:T(8,128)(2,1)}), f16[16,192,256]{2,1,0:T(8,128)(2,1)S(1)}, u32[]{:S(2)}, u32[]{:S(2)}) async-start(f16[16,192,256]{2,1,0:T(8,128)(2,1)} %bitcast.45), calls=%async_computation.9 | async-start | bytes 3145728 | tf_op jit(solution)/shard_map/all_to_all | solution.py:205
  200.8 8.0 %collective-permute-start.10 = (f16[256,128]{1,0:T(8,128)(2,1)}, f16[256,128]{1,0:T(8,128)(2,1)}, u32[]{:S(2)}, u32[]{:S(2)}) collective-permute-start(f16[256,128]{1,0:T(8,128)(2,1)} %get-tuple-element.17), channel_id=1, source_target_pairs={{0,48},{8,56},{16,0},{24,8},{32,16},{40,24},{48,32},{56,40},{1,49}... | collective-permute-start | bytes 196616 | tf_op jit(solution)/shard_map/ppermute | solution.py:28
  202.0 11.0 %collective-permute-start.11 = (f16[256,128]{1,0:T(8,128)(2,1)}, f16[256,128]{1,0:T(8,128)(2,1)}, u32[]{:S(2)}, u32[]{:S(2)}) collective-permute-start(f16[256,128]{1,0:T(8,128)(2,1)} %get-tuple-element.16), channel_id=1, source_target_pairs={{0,56},{8,0},{16,8},{24,16},{32,24},{40,32},{48,40},{56,48},{1,57}... | collective-permute-start | bytes 196616 | tf_op jit(solution)/shard_map/ppermute | solution.py:28
  204.0 11.2 %collective-permute-start.5 = (f16[256,128]{1,0:T(8,128)(2,1)}, f16[256,128]{1,0:T(8,128)(2,1)S(1)}, u32[]{:S(2)}, u32[]{:S(2)}) collective-permute-start(f16[256,128]{1,0:T(8,128)(2,1)} %get-tuple-element.15), channel_id=1, source_target_pairs={{0,8},{8,16},{16,24},{24,32},{32,40},{40,48},{48,56},{56,0},{1,9},... | collective-permute-start | bytes 196616 | tf_op jit(solution)/shard_map/ppermute | solution.py:28
  205.1 10.1 %collective-permute-start.6 = (f16[256,128]{1,0:T(8,128)(2,1)}, f16[256,128]{1,0:T(8,128)(2,1)S(1)}, u32[]{:S(2)}, u32[]{:S(2)}) collective-permute-start(f16[256,128]{1,0:T(8,128)(2,1)} %get-tuple-element.21), channel_id=1, source_target_pairs={{0,16},{8,24},{16,32},{24,40},{32,48},{40,56},{48,0},{56,8},{1,17}... | collective-permute-start | bytes 196616 | tf_op jit(solution)/shard_map/ppermute | solution.py:28
  207.9 10.8 %collective-permute-start.7 = (f16[256,128]{1,0:T(8,128)(2,1)}, f16[256,128]{1,0:T(8,128)(2,1)S(1)}, u32[]{:S(2)}, u32[]{:S(2)}) collective-permute-start(f16[256,128]{1,0:T(8,128)(2,1)} %get-tuple-element.20), channel_id=1, source_target_pairs={{0,24},{8,32},{16,40},{24,48},{32,56},{40,0},{48,8},{56,16},{1,25}... | collective-permute-start | bytes 196616 | tf_op jit(solution)/shard_map/ppermute | solution.py:28
  208.8 10.0 %collective-permute-start.8 = (f16[256,128]{1,0:T(8,128)(2,1)S(1)}, f16[256,128]{1,0:T(8,128)(2,1)S(1)}, u32[]{:S(2)}, u32[]{:S(2)}) collective-permute-start(f16[256,128]{1,0:T(8,128)(2,1)S(1)} %get-tuple-element.19), channel_id=1, source_target_pairs={{0,32},{8,40},{16,48},{24,56},{32,0},{40,8},{48,16},{56,24},{1,33}... | collective-permute-start | bytes 196616 | tf_op jit(solution)/shard_map/ppermute | solution.py:28
  213.0 8.3 %collective-permute-start.9 = (f16[256,128]{1,0:T(8,128)(2,1)S(1)}, f16[256,128]{1,0:T(8,128)(2,1)S(1)}, u32[]{:S(2)}, u32[]{:S(2)}) collective-permute-start(f16[256,128]{1,0:T(8,128)(2,1)S(1)} %get-tuple-element.18), channel_id=1, source_target_pairs={{0,40},{8,48},{16,56},{24,0},{32,8},{40,16},{48,24},{56,32},{1,41}... | collective-permute-start | bytes 196616 | tf_op jit(solution)/shard_map/ppermute | solution.py:28
  223.2 18.8 %all-to-all-start.8 = ((f32[64,4,128]{2,1,0:T(4,128)}), f32[64,4,128]{2,1,0:T(4,128)S(1)}, u32[]{:S(2)}, u32[]{:S(2)}) async-start(f32[64,4,128]{2,1,0:T(4,128)} %bitcast.41), calls=%async_computation.8 | async-start | bytes 262144 | tf_op jit(solution)/shard_map/all_to_all | solution.py:199
  234.3 12.7 %collective-permute-start.12 = (f32[32,6,256]{2,0,1:T(8,128)S(1)}, f32[32,6,256]{2,0,1:T(8,128)S(1)}, u32[]{:S(2)}, u32[]{:S(2)}) collective-permute-start(f32[32,6,256]{2,0,1:T(8,128)S(1)} %bitcast.149), channel_id=1, source_target_pairs={{0,1},{1,2},{2,3},{3,0},{4,5},{5,6},{6,7},{7,4},{8,9},{9,10},{10,1... | collective-permute-start | bytes 589832 | tf_op jit(solution)/shard_map/ppermute | solution.py:28
  242.8 8.4 %collective-permute-start.13 = (f32[32,6,256]{2,0,1:T(8,128)S(1)}, f32[32,6,256]{2,0,1:T(8,128)S(1)}, u32[]{:S(2)}, u32[]{:S(2)}) collective-permute-start(f32[32,6,256]{2,0,1:T(8,128)S(1)} %bitcast.150), channel_id=1, source_target_pairs={{0,2},{1,3},{2,0},{3,1},{4,6},{5,7},{6,4},{7,5},{8,10},{9,11},{10,... | collective-permute-start | bytes 589832 | tf_op jit(solution)/shard_map/ppermute | solution.py:28
  245.8 9.7 %collective-permute-start.14 = (f32[32,6,256]{2,0,1:T(8,128)S(1)}, f32[32,6,256]{2,0,1:T(8,128)S(1)}, u32[]{:S(2)}, u32[]{:S(2)}) collective-permute-start(f32[32,6,256]{2,0,1:T(8,128)S(1)} %bitcast.151), channel_id=1, source_target_pairs={{0,3},{1,0},{2,1},{3,2},{4,7},{5,4},{6,5},{7,6},{8,11},{9,8},{10,9... | collective-permute-start | bytes 589832 | tf_op jit(solution)/shard_map/ppermute | solution.py:28
  255.6 0.9 copy-start.2
Sparse Core Ops, SparseCore 0:
  46.7 28.7 all-gather.2
  89.2 37.7 all-gather.4

commit v2 on v1

v2 whole, which is shorter than its diff:
```python
import functools

import jax
import jax.numpy as jnp
from jax import lax
from jax.experimental import pallas as pl
from jax.experimental.pallas import tpu as pltpu
from jax.sharding import Mesh, PartitionSpec as P

BALANCING_ROUNDS = 3
EPS = 1e-06
TEMP_T = 0.07
TEMP_S = 0.1
CROPS = 6
NX, NZ, NC, NY = 4, 8, 2, 4
DP = ("x", "z", "core")
XY = ("x", "proto")
ZC = ("z", "core")
LANES = 128
BY_BITS = [b4 * 4 + b2 * 2 + b1 for b2 in range(2) for b1 in range(2) for b4 in range(2)]
LOG2E = 1.4426950408889634
MIB = 1024 * 1024
VMEM = pl.BlockSpec(memory_space=pltpu.VMEM)
SMEM = pl.BlockSpec(memory_space=pltpu.SMEM)
HBM = pl.BlockSpec(memory_space=pltpu.HBM)


def swap(v, axes):
    return lax.all_to_all(v, axes, 0, 0)


def spread(v, axes, n):
    return swap(jnp.broadcast_to(v, (n,) + v.shape), axes)


def other_core(v):
    return lax.ppermute(v, "core", [(0, 1), (1, 0)])


def shifted(v, axis, n, k):
    return lax.ppermute(v, axis, [(i, (i + k) % n) for i in range(n)])


def along(v, axis, n):
    me = lax.axis_index(axis)
    out = jnp.zeros((n,) + v.shape, v.dtype)
    for k in range(n):
        part = v if k == 0 else shifted(v, axis, n, k)
        out = lax.dynamic_update_index_in_dim(out, part, (me - k) % n, 0)
    return out


def exchanged(v, axis, n, step):
    return v, lax.ppermute(v, axis, [(i, i ^ step) for i in range(n)])


def merged(pair, axis, step):
    own, got = pair
    high = (lax.axis_index(axis) // step) % 2 == 1
    return jnp.concatenate([jnp.where(high, got, own), jnp.where(high, own, got)])


def whole(*shape):
    return pl.BlockSpec(shape, lambda *at: (0,) * len(shape))


def call(kernel, out_shape, in_specs, scratch=(), out_specs=None, grid=(), limit=8, flops=0, moved=0, exps=0):
    return pl.pallas_call(
        kernel,
        grid=grid,
        out_shape=out_shape,
        in_specs=in_specs,
        out_specs=out_specs or [VMEM] * len(out_shape),
        scratch_shapes=list(scratch),
        compiler_params=pltpu.CompilerParams(vmem_limit_bytes=limit * MIB),
        cost_estimate=pl.CostEstimate(flops=flops, bytes_accessed=moved, transcendentals=exps),
    )


def down(row):
    return jnp.transpose(jnp.broadcast_to(row, (LANES, LANES)))


def fold(v, rows):
    return jnp.sum(v.reshape(v.shape[0] // rows, rows, v.shape[1]), axis=0)


def join_columns(place_ref, own_ref, other_ref, out_ref, order=range(NZ)):
    for side, ref in enumerate((own_ref, other_ref)):
        half = lax.rem(place_ref[1] + side, NC) * NZ
        for i, z in enumerate(order):
            out_ref[:, pl.ds(pl.multiple_of((half + z) * LANES, LANES), LANES)] = ref[i]


def to_all(acc, out_ref, n):
    total = jnp.sum(acc, axis=0, keepdims=True)
    count = total.shape[1] // LANES
    lines = jnp.concatenate([total[:, i * LANES : (i + 1) * LANES] for i in range(count)], axis=0)
    for p in range(n):
        out_ref[p, :count] = lines


def energy_kernel(place_ref, norm_ref, t_ref, own_ref, other_ref, e_ref, out_ref, proto_ref, acc_ref, held_ref, sem_ref):
    join_columns(place_ref, own_ref, other_ref, proto_ref)
    width = e_ref.shape[1]
    tile = 256

    def copy(j):
        at = pl.ds(pl.multiple_of(j * tile, tile), tile)
        return pltpu.make_async_copy(held_ref.at[:, at], e_ref.at[:, at], sem_ref.at[j])

    def columns(j, _):
        at = pl.ds(pl.multiple_of(j * tile, tile), tile)
        dots = jnp.dot(t_ref[...], proto_ref[:, at], preferred_element_type=jnp.float32)
        energy = jnp.exp(dots * (1.0 / TEMP_T))
        held_ref[:, at] = energy
        acc_ref[:, at] = fold(energy, 8)
        copy(j).start()
        return 0

    lax.fori_loop(0, width // tile, columns, 0)
    to_all(acc_ref[...], out_ref, out_ref.shape[0])
    for p in range(out_ref.shape[0]):
        out_ref[p, width // LANES : width // LANES + 1] = norm_ref[...]
    for j in range(width // tile):
        copy(j).wait()


def fetch(e_ref, held_ref, sem_ref):
    blocks = e_ref.shape[0] // LANES

    def copy(b):
        at = pl.ds(pl.multiple_of(b * LANES, LANES), LANES)
        return pltpu.make_async_copy(e_ref.at[at], held_ref.at[at], sem_ref.at[b])

    for b in range(blocks):
        copy(b).start()
    return blocks, lambda b: copy(b).wait()


def by_row_kernel(got_ref, e_ref, *refs):
    more = refs[:-5]
    recip_ref, out_ref, lines_ref, held_ref, sem_ref = refs[-5:]
    blocks, wait = fetch(e_ref, held_ref, sem_ref)
    width = e_ref.shape[1]
    count = width // LANES
    recip = 1.0 / jnp.sum(got_ref[:, :count], axis=0)
    for i in range(count):
        recip_ref[:, i * LANES : (i + 1) * LANES] = recip[i : i + 1, :]

    def block(b, _):
        wait(b)
        at = pl.ds(pl.multiple_of(b * LANES, LANES), LANES)
        acc = jnp.zeros((LANES, LANES), jnp.float32)
        for j in range(width // LANES):
            lanes = slice(j * LANES, (j + 1) * LANES)
            acc += held_ref[at, lanes] * recip_ref[:, lanes]
        lines_ref[pl.ds(b, 1), :] = jnp.sum(jnp.transpose(acc), axis=0, keepdims=True)
        return 0

    lax.fori_loop(0, blocks, block, 0)
    for p in range(out_ref.shape[0]):
        out_ref[p, :8] = lines_ref[...]
        at = 8
        for ref in more:
            out_ref[p, at : at + ref.shape[0]] = ref[...]
            at += ref.shape[0]


def by_column_kernel(got_ref, e_ref, out_ref, lines_ref, acc_ref, held_ref, sem_ref):
    blocks, wait = fetch(e_ref, held_ref, sem_ref)
    width = e_ref.shape[1]
    lines_ref[...] = 1.0 / jnp.sum(got_ref[...], axis=0)
    acc_ref[...] = jnp.zeros_like(acc_ref)

    def block(b, _):
        wait(b)
        at = pl.ds(pl.multiple_of(b * LANES, LANES), LANES)
        scale = down(lines_ref[pl.ds(b, 1), :])
        for j in range(width // LANES):
            lanes = slice(j * LANES, (j + 1) * LANES)
            acc_ref[:, lanes] += fold(held_ref[at, lanes] * scale, 8)
        return 0

    lax.fori_loop(0, blocks, block, 0)
    to_all(acc_ref[...], out_ref, out_ref.shape[0])


def student_sums(s_ref, proto_ref, sums_ref):
    width = proto_ref.shape[1]

    def block(b, _):
        at = pl.ds(pl.multiple_of(b * 2 * LANES, 2 * LANES), 2 * LANES)
        acc = jnp.zeros((2 * LANES, LANES), jnp.float32)
        for j in range(width // 256):
            dots = jnp.dot(
                s_ref[at, :], proto_ref[:, j * 256 : (j + 1) * 256], preferred_element_type=jnp.float32
            )
            powers = jnp.exp2(dots * (LOG2E / TEMP_S))
            acc += powers[:, :LANES] + powers[:, LANES:]
        for i in range(2):
            part = acc[i * LANES : (i + 1) * LANES]
            sums_ref[pl.ds(b * 2 + i, 1), :] = jnp.sum(jnp.transpose(part), axis=0, keepdims=True)
        return 0

    lax.fori_loop(0, s_ref.shape[0] // (2 * LANES), block, 0)


def student_kernel(place_ref, s_ref, own_ref, other_ref, proto_ref, sums_ref):
    join_columns(place_ref, own_ref, other_ref, proto_ref, BY_BITS)
    student_sums(s_ref, proto_ref, sums_ref)


def slope_kernel(
    factor, place_ref, got_ref, recip_ref, s_ref, st_ref, ps_ref, psp_ref, e_ref,
    ug_ref, keep_ref, give_ref, slope_ref, total_ref, lines_ref, down_ref,
):
    rows = st_ref.shape[2]
    width = ps_ref.shape[1]
    images = rows // CROPS
    tile = 1024
    g = pl.program_id(0)
    groups = pl.num_programs(0)

    @pl.when(g == 0)
    def _():
        lines_ref[...] = factor / jnp.sum(got_ref[...], axis=0)
        total_ref[...] = jnp.zeros_like(total_ref)

    for i in range(2):
        down_ref[i] = down(lines_ref[pl.ds(g * 2 + i, 1), :])
    for crop in range(CROPS):
        line = down(lines_ref[pl.ds(groups * 2 + g * CROPS + crop, 1), :])
        down_ref[2 + crop] = line if crop < 2 else 2.0 * line

    def columns(j, _):
        at = pl.ds(pl.multiple_of(j * tile, tile), tile)
        wide = lambda i: jnp.concatenate([down_ref[i]] * (tile // LANES), axis=1)
        recip = recip_ref[:, at]
        t0 = e_ref[:images, at] * recip * wide(0)
        t1 = e_ref[images:, at] * recip * wide(1)
        both = t0 + t1
        scores = jnp.dot(s_ref[0], ps_ref[:, at], preferred_element_type=jnp.float32)
        for crop in range(CROPS):
            lines = slice(crop * images, (crop + 1) * images)
            part = wide(2 + crop) * jnp.exp2(scores[lines] * (LOG2E / TEMP_S))
            minus = t1 if crop == 0 else t0 if crop == 1 else both
            slope_ref[lines, at] = (part - minus).astype(jnp.bfloat16)
        return 0

    lax.fori_loop(0, width // tile, columns, 0)
    total_ref[...] += jnp.dot(st_ref[0], slope_ref[...], preferred_element_type=jnp.float32)
    unit = lax.dot_general(
        slope_ref[...], ps_ref[...], (((1,), (1,)), ((), ())), preferred_element_type=jnp.float32
    )
    part = images // NY
    for crop in range(CROPS):
        for y in range(NY):
            ug_ref[0, y, crop * part : (crop + 1) * part, :] = unit[crop * images + y * part :][:part]

    @pl.when(g == groups - 1)
    def _():
        blocks = width // LANES
        part = total_ref.shape[0] // (NC * NZ)
        size = blocks * part
        for b in range(blocks):
            lanes = slice(b * LANES, (b + 1) * LANES)
            dot = jnp.sum(psp_ref[:, lanes].astype(jnp.float32) * total_ref[:, lanes], axis=0, keepdims=True)
            keep_ref[NZ * size + b : NZ * size + b + 1, :] = dot
            give_ref[NZ * size + b : NZ * size + b + 1, :] = dot
        for side, ref in enumerate((keep_ref, give_ref)):
            half = lax.rem(place_ref[1] + side, NC) * NZ
            for k in range(NZ):
                z = lax.rem(place_ref[0] + k, NZ)
                lines = total_ref[pl.ds(pl.multiple_of((half + z) * part, part), part), :]
                for b in range(blocks):
                    at = k * size + b * part
                    ref[at : at + part, :] = lines[:, b * LANES : (b + 1) * LANES]


def local(teacher_feats, student_embeddings, teacher_weight, student_weight):
    images, _, bottleneck = teacher_feats.shape
    rows_here, wide = student_weight.shape
    sub = wide // (NX * NZ * NC)
    width = wide // NX
    total_k = wide * NY
    s_rows = images * CROPS
    t_rows = images * 2
    f32, bf16 = jnp.float32, jnp.bfloat16
    shape = jax.ShapeDtypeStruct
    place = jnp.stack([lax.axis_index("z"), lax.axis_index("core")]).astype(jnp.int32)
    exact = NX * t_rows * width

    t_float = teacher_feats.transpose(1, 0, 2).reshape(t_rows, bottleneck).astype(f32)
    t_unit = (t_float / jnp.sqrt(jnp.sum(t_float * t_float, axis=1, keepdims=True) + EPS)).astype(bf16)

    shards = jnp.stack([teacher_weight, student_weight]).reshape(2 * rows_here, NX * NZ * NC, sub)
    moved, t_unit = lax.optimization_barrier((swap(shards.transpose(1, 0, 2), DP), t_unit))
    t_all = along(t_unit, "x", NX).reshape(NX * t_rows, bottleneck)
    moved = moved.reshape(NX * NZ * NC, 2, rows_here, sub)
    cols_t = moved[:, 0].reshape(bottleneck, sub)
    cols_s = moved[:, 1].reshape(bottleneck, sub)
    col_t = jnp.sqrt(jnp.sum(cols_t * cols_t, axis=0) + EPS)
    col_s = jnp.sqrt(jnp.sum(cols_s * cols_s, axis=0) + EPS)
    mine_t = (cols_t / col_t).astype(bf16)
    mine_s = (cols_s / col_s).astype(bf16)

    s_raw = student_embeddings.transpose(1, 0, 2).reshape(s_rows, bottleneck).astype(f32)
    s_norm = jnp.sqrt(jnp.sum(s_raw * s_raw, axis=1, keepdims=True) + EPS)
    s_float = s_raw / s_norm
    s_unit, mine_t, mine_s = lax.optimization_barrier((s_float.astype(bf16), mine_t, mine_s))
    pair = exchanged(mine_s[None], "z", NZ, 4)
    s_pair = exchanged(s_unit[None], "x", NX, 1)
    own_t = spread(mine_t, "z", NZ)
    energy, to_devices = call(
        energy_kernel,
        [pltpu.HBM((NX * t_rows, width), f32), shape((NZ * NC, width // LANES + 8, LANES), f32)],
        [SMEM, VMEM, VMEM, VMEM, VMEM],
        [
            pltpu.VMEM((bottleneck, width), bf16),
            pltpu.VMEM((8, width), f32),
            pltpu.VMEM((NX * t_rows, width), f32),
            pltpu.SemaphoreType.DMA((width // 256,)),
        ],
        [HBM, VMEM],
        limit=24,
        flops=2 * exact * bottleneck,
        exps=exact,
    )(place, col_s.reshape(1, sub), t_all, own_t, other_core(own_t))

    energy = pltpu.with_memory_space_constraint(energy, pltpu.HBM)
    blocks = NX * t_rows // LANES
    held = [pltpu.VMEM((NX * t_rows, width), f32), pltpu.SemaphoreType.DMA((blocks,))]
    quarter = images // NY
    first = lax.axis_index("proto") * quarter
    part_float = lax.dynamic_slice_in_dim(s_float.reshape(CROPS, images, bottleneck), first, quarter, 1)
    part_norm = lax.dynamic_slice_in_dim(s_norm.reshape(CROPS, images, 1), first, quarter, 1)
    part_float, part_norm, to_devices = lax.optimization_barrier((part_float, part_norm, to_devices))

    def by_row(got, *more):
        lines = 8 + sum(m.shape[0] for m in more)
        return call(
            by_row_kernel,
            [shape((1, width), f32), shape((NX * NY, lines, LANES), f32)],
            [VMEM, HBM] + [VMEM] * len(more),
            [pltpu.VMEM((8, LANES), f32)] + held,
            limit=12,
            flops=2 * exact,
            moved=4 * exact,
        )(got, energy, *more)

    def by_column(got):
        (to_devices,) = call(
            by_column_kernel,
            [shape((NZ * NC, width // LANES, LANES), f32)],
            [VMEM, HBM],
            [pltpu.VMEM((8, LANES), f32), pltpu.VMEM((8, width), f32)] + held,
            limit=12,
            flops=2 * exact,
            moved=4 * exact,
        )(got, energy)
        return to_devices

    half_rows = NX * s_rows // 2
    student = dict(limit=58, flops=exact * 3 * bottleneck, exps=exact * 3 // 2)

    to_devices, own_s = lax.optimization_barrier((to_devices, merged(pair, "z", 4)))
    got = swap(to_devices, ZC)
    pair = exchanged(own_s, "z", NZ, 1)
    col_s = got[:, width // LANES].reshape(NZ, NC, LANES).transpose(1, 0, 2).reshape(NZ * NC, 1, LANES)
    _, to_devices = by_row(got)
    to_devices, own_s, s_all = lax.optimization_barrier((to_devices, merged(pair, "z", 1), merged(s_pair, "x", 1)))
    got = swap(to_devices, XY)
    pair = exchanged(own_s, "z", NZ, 2)
    to_devices = by_column(got)

    to_devices, own_s, s_all = lax.optimization_barrier((to_devices, merged(pair, "z", 2), s_all))
    got = swap(to_devices, ZC)
    other_s = other_core(own_s)
    s_pair = exchanged(s_all, "x", NX, 2)
    _, to_devices = by_row(got)
    to_devices, other_s, s_pair = lax.optimization_barrier((to_devices, other_s, s_pair))
    got = swap(to_devices, XY)
    s_all = merged(s_pair, "x", 2)
    s_halves = s_all.reshape(2, half_rows, bottleneck)
    proto_s, first_sums = call(
        student_kernel,
        [shape((bottleneck, width), bf16), shape((half_rows // LANES, LANES), f32)],
        [SMEM, VMEM, VMEM, VMEM],
        **student,
    )(place, s_halves[0], own_s, other_s)
    to_devices = by_column(got)

    to_devices, proto_s, s_all, first_sums = lax.optimization_barrier((to_devices, proto_s, s_all, first_sums))
    got = swap(to_devices, ZC)
    (last_sums,) = call(
        student_sums, [shape((half_rows // LANES, LANES), f32)], [VMEM, VMEM], **student
    )(s_all.reshape(2, half_rows, bottleneck)[1], proto_s)
    recip, to_devices = by_row(got, first_sums, last_sums)
    to_devices, proto_s, s_all = lax.optimization_barrier((to_devices, proto_s, s_all))
    got = swap(to_devices, XY)

    order = jnp.arange(bottleneck).reshape(NX, NZ, NC, rows_here).transpose(2, 1, 0, 3).reshape(-1)
    ordered = (order[:, None] == jnp.arange(bottleneck)[None, :]).astype(bf16)
    proto_o = jnp.dot(ordered, proto_s, preferred_element_type=f32).astype(bf16)
    s_o = jnp.einsum("pb,grb->gpr", ordered, s_all, preferred_element_type=f32).astype(bf16)
    size = bottleneck * width // (NC * NZ * LANES)
    unit_part, keep, give = call(
        functools.partial(slope_kernel, total_k / 16.0),
        [pltpu.VMEM((NX, NY, s_rows // NY, bottleneck), f32)] + [pltpu.HBM((NZ * size + width // LANES, LANES), f32)] * NC,
        [
            SMEM,
            whole(NX * NY, NX * (2 + CROPS), LANES),
            whole(1, width),
            pl.BlockSpec((1, s_rows, bottleneck), lambda g: (g, 0, 0)),
            pl.BlockSpec((1, bottleneck, s_rows), lambda g: (g, 0, 0)),
            whole(bottleneck, width),
            whole(bottleneck, width),
            pl.BlockSpec((t_rows, width), lambda g: (g, 0)),
        ],
        [
            pltpu.VMEM((s_rows, width), bf16),
            pltpu.VMEM((bottleneck, width), f32),
            pltpu.VMEM((NX * (2 + CROPS), LANES), f32),
            pltpu.VMEM((2 + CROPS, LANES, LANES), f32),
        ],
        [
            pl.BlockSpec((1, NY, s_rows // NY, bottleneck), lambda g: (g, 0, 0, 0)),
            whole(NZ * size + width // LANES, LANES),
            whole(NZ * size + width // LANES, LANES),
        ],
        (NX,),
        limit=40,
        flops=6 * exact * 3 * bottleneck,
        moved=4 * exact,
        exps=exact * 3,
    )(
        place,
        pltpu.with_memory_space_constraint(got, pltpu.HBM),
        recip,
        *(pltpu.with_memory_space_constraint(v, pltpu.HBM) for v in (s_all, s_o, proto_s, proto_o)),
        energy,
    )

    half = (keep + other_core(give)) * (1.0 / 512.0)
    dots = half[NZ * size :]
    high = lax.reduce_precision(dots, 5, 10)
    ends = [high.astype(jnp.float16), ((dots - high) * 1024.0).astype(jnp.float16)]
    proto_grad = half[:size]
    for k in range(1, NZ):
        sent = jnp.concatenate([half[k * size : (k + 1) * size].astype(jnp.float16)] + ends)
        came = shifted(sent, "z", NZ, k).astype(f32)
        proto_grad = proto_grad + came[:size]
        dots = dots + (came[size : size + NZ * NC] + came[size + NZ * NC :] * (1.0 / 1024.0))
    lines = bottleneck // (NC * NZ)
    proto_grad = proto_grad.reshape(NC * NZ, lines, LANES) * 512.0
    column_dot = dots.reshape(NC * NZ, 1, LANES) * 512.0
    at = (lax.axis_index("core") * NZ + lax.axis_index("z")) * lines
    proto_float = lax.dynamic_slice_in_dim(proto_o, at, lines, 0).astype(f32)
    proto_float = proto_float.reshape(lines, NC * NZ, LANES).transpose(1, 0, 2)
    grad_lines = (proto_grad - proto_float * column_dot) / col_s

    sent = (unit_part.reshape(NX * NY, CROPS * quarter, bottleneck) * 4.0).astype(jnp.float16)
    unit_grad = jnp.sum(swap(sent, XY).astype(f32), axis=0) * 0.25
    unit_grad = unit_grad.reshape(CROPS, quarter, bottleneck)
    fgrad = (unit_grad - part_float * jnp.sum(part_float * unit_grad, axis=2, keepdims=True)) / part_norm

    grad_lines, fgrad = lax.optimization_barrier((grad_lines, fgrad))
    feature_grad = along(fgrad.transpose(1, 0, 2), "proto", NY).reshape(images, CROPS, bottleneck)
    grad_lines = grad_lines.reshape(NC * NZ, NX, rows_here, LANES).transpose(1, 0, 2, 3)
    grad_rows = swap(grad_lines, "x").reshape(NX, NC, NZ, rows_here, LANES)
    weight_grad = grad_rows.transpose(3, 0, 2, 1, 4).reshape(rows_here, wide)
    teacher_new = 0.994 * teacher_weight + 0.006 * (student_weight - 0.5 * weight_grad)
    return weight_grad, teacher_new, feature_grad


def solution(mesh):
    fine = Mesh(mesh.devices.reshape(NX, NZ, NC, NY), ("x", "z", "core", "proto"))
    in_specs = (P(DP, None, None), P(DP, None, None), P(DP, "proto"), P(DP, "proto"))
    out_specs = (P(DP, "proto"), P(DP, "proto"), P(DP, None, None))
    return jax.shard_map(local, mesh=fine, in_specs=in_specs, out_specs=out_specs, check_vma=False)
```

time: 266 us -> 236 us (0.89)
  Pallas kernels: 22.1 us -> 56.7 us
  other arithmetic: 40.4 us -> 9.09 us
  waiting for transfers between devices: 81.1 us -> 67.8 us
  between operations: 14.6 us -> 1.51 us
  starting transfers between devices: 81 us -> 89.5 us
  local copies, waits for them, and re-layouts: 14.3 us -> 6.95 us
  matrix products: 9.96 us -> 3.21 us
    pallas_call x1 -> x9, Pallas kernels: 22.1 us -> 56.7 us  [the longest x1 18.3 us: local(): call(functools.partial(slope_kernel, total_k / 16.0), [pltpu.VMEM((NX, NY...]
    reduce_sum x13 -> x1, other arithmetic: 22 us -> 0.21 us  [local(): unit_grad = jnp.sum(swap(sent, XY).astype(f32), axis=0) * 0.25]
    all_to_all x10, waiting for transfers between devices: 64.4 us -> 47.7 us  [swap(): return lax.all_to_all(v, axes, 0, 0)]
    ppermute x0 -> x5, waiting for transfers between devices: none -> 10.8 us  [exchanged(): return (v, lax.ppermute(v, axis, [(i, i ^ step) for i in range(n)]))]
    ppermute x0 -> x5, starting transfers between devices: none -> 9.82 us  [exchanged(): return (v, lax.ppermute(v, axis, [(i, i ^ step) for i in range(n)]))]
    ppermute x13, waiting for transfers between devices: 14.7 us -> 7.62 us  [shifted(): return lax.ppermute(v, axis, [(i, (i + k) % n) for i in range(n)])]
    dot_general x2, matrix products: 9.96 us -> 3.21 us  [the longest x1 1.75 us: local(): jnp.einsum('pb,grb->gpr', ordered, s_all, preferred_element_type=f32)]
    broadcast_in_dim x7 -> x1, local copies, waits for them, and re-layouts: 5.23 us -> 0.86 us  [spread(): return swap(jnp.broadcast_to(v, (n,) + v.shape), axes)]
  transfers between devices with their start and end apart: 27 -> 31, of which waited for: 15 -> 16; matrix products, arithmetic and copies ran while one was open for 19% -> 5% of each run, Pallas kernels for 0% -> 8%
where the time goes in v2:
time: 236 us; the launch traced here: 235 us
  starting transfers between devices  89.5 us (38%)
  waiting for transfers between devices  67.8 us (29%)
  Pallas kernels  56.7 us (24%)
  other arithmetic  9.09 us (4%)
  local copies, waits for them, and re-layouts  6.95 us (3%)
  matrix products  3.21 us (1%)
    all_to_all x10, starting transfers between devices, swap(): return lax.all_to_all(v, axes, 0, 0)  54.9 us
    all_to_all x10, waiting for transfers between devices, swap(): return lax.all_to_all(v, axes, 0, 0)  47.7 us
    ppermute x13, starting transfers between devices, shifted(): return lax.ppermute(v, axis, [(i, (i + k) % n) for i in range(n)])  24.7 us
    pallas_call x1, Pallas kernels, local(): call(functools.partial(slope_kernel, total_k / 16.0), [pltpu.VMEM((NX, NY...  18.3 us
    pallas_call x3, Pallas kernels, by_row(): call(by_row_kernel, [shape((1, width), f32), shape((NX * NY, lines, LANES...  12.9 us
    ppermute x5, waiting for transfers between devices, exchanged(): return (v, lax.ppermute(v, axis, [(i, i ^ step) for i in range(n)]))  10.8 us
    ppermute x5, starting transfers between devices, exchanged(): return (v, lax.ppermute(v, axis, [(i, i ^ step) for i in range(n)]))  9.82 us
    pallas_call x2, Pallas kernels, by_column(): call(by_column_kernel, [shape((NZ * NC, width // LANES, LANES), f32)], [V...  8.58 us
  transfers between devices with their start and end apart: 31, of which 16 were waited for; matrix products, arithmetic and copies ran while one was open for 5% of the time, Pallas kernels for 8%

profile of v2, /device:TPU:32, one launch (start us, length us, event | category | flops | bytes accessed | tf_op | source)
XLA Modules:
  0.0 234.8 jit_solution(15640193032951005722)
XLA Ops:
  0.6 1.1 pad_maximum_fusion.3
  1.9 0.9 copy.45
  2.8 11.6 %all-to-all-start = ((f32[64,8,128]{2,1,0:T(8,128)}), f32[64,8,128]{2,1,0:T(8,128)S(1)}, u32[]{:S(2)}, u32[]{:S(2)}) async-start(f32[64,8,128]{2,1,0:T(8,128)} %copy.45), calls=%async_computation | async-start | bytes 524288 | tf_op jit(solution)/shard_map/all_to_all | solution.py:29
  15.5 10.7 %all-to-all-done = f32[64,8,128]{2,1,0:T(8,128)S(1)} async-done(((f32[64,8,128]{2,1,0:T(8,128)}), f32[64,8,128]{2,1,0:T(8,128)S(1)}, u32[]{:S(2)}, u32[]{:S(2)}) %all-to-all-start) | async-done | bytes 262176 | tf_op jit(solution)/shard_map/all_to_all | solution.py:29
  26.5 0.9 broadcast_in_dim.52
  27.4 4.8 %all-to-all-start.1 = ((bf16[8,256,128]{2,1,0:T(8,128)(2,1)}), bf16[8,256,128]{2,1,0:T(8,128)(2,1)S(1)}, u32[]{:S(2)}, u32[]{:S(2)}) async-start(bf16[8,256,128]{2,1,0:T(8,128)(2,1)} %broadcast_in_dim.52), calls=%async_computation.1 | async-start | bytes 1048576 | tf_op jit(solution)/shard_map/all_to_all | solution.py:29
  32.9 2.7 %collective-permute-start.1 = (bf16[256,256]{1,0:T(8,128)(2,1)S(1)}, bf16[256,256]{1,0:T(8,128)(2,1)S(1)}, u32[]{:S(2)}, u32[]{:S(2)}) collective-permute-start(bf16[256,256]{1,0:T(8,128)(2,1)S(1)} %fusion.6), channel_id=1, source_target_pairs={{0,128},{64,192},{128,0},{192,64},{1,129},{65,193},{129,1},{193,65... | collective-permute-start | bytes 393224 | tf_op jit(solution)/shard_map/ppermute | solution.py:41
  35.6 1.4 collective-permute-start.2
  36.9 0.7 collective-permute-start.6
  37.6 4.5 %collective-permute-start.4 = (bf16[1,256,128]{2,1,0:T(8,128)(2,1)S(1)}, bf16[1,256,128]{2,1,0:T(8,128)(2,1)S(1)}, u32[]{:S(2)}, u32[]{:S(2)}) collective-permute-start(bf16[1,256,128]{2,1,0:T(8,128)(2,1)S(1)} %bitcast.116), channel_id=1, source_target_pairs={{0,32},{8,40},{16,48},{24,56},{32,0},{40,8},{48,16},{56,24},{1,33}... | collective-permute-start | bytes 196616 | tf_op jit(solution)/shard_map/ppermute | solution.py:54
  42.2 9.1 %collective-permute-done.4 = bf16[1,256,128]{2,1,0:T(8,128)(2,1)S(1)} collective-permute-done((bf16[1,256,128]{2,1,0:T(8,128)(2,1)S(1)}, bf16[1,256,128]{2,1,0:T(8,128)(2,1)S(1)}, u32[]{:S(2)}, u32[]{:S(2)}) %collective-permute-start.4) | collective-permute-done | bytes 65568 | tf_op jit(solution)/shard_map/ppermute | solution.py:54
  51.6 1.8 collective-permute-done.3.other_ref
  53.4 5.7 %shard_map.67 = (f32[1024,2048]{1,0:T(8,128)}, f32[16,24,128]{2,1,0:T(8,128)}) custom-call(s32[2]{0:T(128)S(1)} %pad_add_fusion.place_ref, f32[1,128]{1,0:T(1,128)S(1)} %get-tuple-element.117.norm_ref, bf16[1024,256]{1,0:T(8,128)(2,1)S(1)} %bitcast.102, bf16[8,256,128]{2,1,0:T(8,128)(2,1)S(1)} %all-to-all-done.1.own_ref, ...), custom_call_target="tpu_custom_call" | custom-call | flops 1073741824 | tf_op jit(solution)/shard_map/pallas_call | solution.py:315
  59.1 1.6 collective-permute-start.5
  60.6 3.9 %all-to-all-start.2 = ((f32[16,24,128]{2,1,0:T(8,128)}), f32[16,24,128]{2,1,0:T(8,128)S(1)}, u32[]{:S(2)}, u32[]{:S(2)}) async-start(f32[16,24,128]{2,1,0:T(8,128)} %get-tuple-element.49), calls=%async_computation.2 | async-start | bytes 393216 | tf_op jit(solution)/shard_map/all_to_all | solution.py:29
  64.8 8.3 %all-to-all-done.2.got_ref = f32[16,24,128]{2,1,0:T(8,128)S(1)} async-done(((f32[16,24,128]{2,1,0:T(8,128)}), f32[16,24,128]{2,1,0:T(8,128)S(1)}, u32[]{:S(2)}, u32[]{:S(2)}) %all-to-all-start.2) | async-done | bytes 196640 | tf_op jit(solution)/shard_map/all_to_all | solution.py:29
  73.1 4.3 %shard_map.68 = (f32[1,2048]{1,0:T(1,128)}, f32[16,8,128]{2,1,0:T(8,128)}) custom-call(f32[16,24,128]{2,1,0:T(8,128)S(1)} %all-to-all-done.2.got_ref, f32[1024,2048]{1,0:T(8,128)} %get-tuple-element.50.e_ref), custom_call_target="tpu_custom_call" | custom-call | flops 4194304 | bytes 8388608 | tf_op jit(solution)/shard_map/pallas_call | solution.py:342
  77.4 1.8 collective-permute-start.7
  79.2 6.4 %all-to-all-start.3 = ((f32[16,8,128]{2,1,0:T(8,128)}), f32[16,8,128]{2,1,0:T(8,128)S(1)}, u32[]{:S(2)}, u32[]{:S(2)}) async-start(f32[16,8,128]{2,1,0:T(8,128)} %get-tuple-element.54), calls=%async_computation.3 | async-start | bytes 131072 | tf_op jit(solution)/shard_map/all_to_all | solution.py:29
  85.6 7.6 %all-to-all-done.3.got_ref = f32[16,8,128]{2,1,0:T(8,128)S(1)} async-done(((f32[16,8,128]{2,1,0:T(8,128)}), f32[16,8,128]{2,1,0:T(8,128)S(1)}, u32[]{:S(2)}, u32[]{:S(2)}) %all-to-all-start.3) | async-done | bytes 65568 | tf_op jit(solution)/shard_map/all_to_all | solution.py:29
  93.2 4.3 %shard_map.69 = f32[16,16,128]{2,1,0:T(8,128)} custom-call(f32[16,8,128]{2,1,0:T(8,128)S(1)} %all-to-all-done.3.got_ref, f32[1024,2048]{1,0:T(8,128)} %get-tuple-element.50.e_ref), custom_call_target="tpu_custom_call" | custom-call | flops 4194304 | bytes 8388608 | tf_op jit(solution)/shard_map/pallas_call | solution.py:353
  97.7 1.3 collective-permute-start.9
  99.0 4.9 %all-to-all-start.4 = ((f32[16,16,128]{2,1,0:T(8,128)}), f32[16,16,128]{2,1,0:T(8,128)S(1)}, u32[]{:S(2)}, u32[]{:S(2)}) async-start(f32[16,16,128]{2,1,0:T(8,128)} %shard_map.69), calls=%async_computation.4 | async-start | bytes 262144 | tf_op jit(solution)/shard_map/all_to_all | solution.py:29
  103.9 7.4 %all-to-all-done.4.got_ref = f32[16,16,128]{2,1,0:T(8,128)S(1)} async-done(((f32[16,16,128]{2,1,0:T(8,128)}), f32[16,16,128]{2,1,0:T(8,128)S(1)}, u32[]{:S(2)}, u32[]{:S(2)}) %all-to-all-start.4) | async-done | bytes 131104 | tf_op jit(solution)/shard_map/all_to_all | solution.py:29
  111.3 4.3 %shard_map.70 = (f32[1,2048]{1,0:T(1,128)}, f32[16,8,128]{2,1,0:T(8,128)}) custom-call(f32[16,16,128]{2,1,0:T(8,128)S(1)} %all-to-all-done.4.got_ref, f32[1024,2048]{1,0:T(8,128)} %get-tuple-element.50.e_ref), custom_call_target="tpu_custom_call" | custom-call | flops 4194304 | bytes 8388608 | tf_op jit(solution)/shard_map/pallas_call | solution.py:342
  115.6 1.5 collective-permute-done.9
  117.1 3.7 %all-to-all-start.5 = ((f32[16,8,128]{2,1,0:T(8,128)}), f32[16,8,128]{2,1,0:T(8,128)S(1)}, u32[]{:S(2)}, u32[]{:S(2)}) async-start(f32[16,8,128]{2,1,0:T(8,128)} %get-tuple-element.61), calls=%async_computation.5 | async-start | bytes 131072 | tf_op jit(solution)/shard_map/all_to_all | solution.py:29
  121.1 0.7 copy-done.6
  121.9 6.0 %shard_map.72 = (bf16[256,2048]{1,0:T(8,128)(2,1)}, f32[12,128]{1,0:T(8,128)}) custom-call(s32[2]{0:T(128)} %copy-done.2, bf16[1536,256]{1,0:T(8,128)(2,1)} %bitcast.104, bf16[8,256,128]{2,1,0:T(8,128)(2,1)} %copy-done.11, bf16[8,256,128]{2,1,0:T(8,128)(2,1)} %copy-done.16), custom_call_target="tpu_custom_call" | custom-call | flops 1610612736 | tf_op jit(solution)/shard_map/pallas_call | solution.py:386
  128.5 4.3 %shard_map.71 = f32[16,16,128]{2,1,0:T(8,128)} custom-call(f32[16,8,128]{2,1,0:T(8,128)S(1)} %all-to-all-done.5.got_ref, f32[1024,2048]{1,0:T(8,128)} %get-tuple-element.50.e_ref), custom_call_target="tpu_custom_call" | custom-call | flops 4194304 | bytes 8388608 | tf_op jit(solution)/shard_map/pallas_call | solution.py:353
  132.8 4.9 %all-to-all-start.6 = ((f32[16,16,128]{2,1,0:T(8,128)}), f32[16,16,128]{2,1,0:T(8,128)S(1)}, u32[]{:S(2)}, u32[]{:S(2)}) async-start(f32[16,16,128]{2,1,0:T(8,128)} %shard_map.71), calls=%async_computation.6 | async-start | bytes 262144 | tf_op jit(solution)/shard_map/all_to_all | solution.py:29
  137.8 0.9 slice.114
  138.8 5.2 %shard_map.73.refs_1_ = f32[12,128]{1,0:T(8,128)} custom-call(bf16[1536,256]{1,0:T(8,128)(2,1)} %bitcast.108, bf16[256,2048]{1,0:T(8,128)(2,1)} %get-tuple-element.75.proto_ref.ps_ref), custom_call_target="tpu_custom_call" | custom-call | flops 1610612736 | tf_op jit(solution)/shard_map/pallas_call | solution.py:396
  144.0 1.1 all-to-all-done.6.got_ref
  145.1 0.7 copy-done.1
  145.8 4.3 %shard_map.74 = (f32[1,2048]{1,0:T(1,128)S(1)}, f32[16,32,128]{2,1,0:T(8,128)}) custom-call(f32[16,16,128]{2,1,0:T(8,128)S(1)} %all-to-all-done.6.got_ref, f32[1024,2048]{1,0:T(8,128)} %get-tuple-element.50.e_ref, f32[12,128]{1,0:T(8,128)S(1)} %copy-done, f32[12,128]{1,0:T(8,128)S(1)} %copy-done.1), custom_call_target="tpu_custom_call" | custom-call | flops 4194304 | bytes 8388608 | tf_op jit(solution)/shard_map/pallas_call | solution.py:342
  150.1 6.6 %all-to-all-start.7 = ((f32[16,32,128]{2,1,0:T(8,128)}), f32[16,32,128]{2,1,0:T(8,128)S(1)}, u32[]{:S(2)}, u32[]{:S(2)}) async-start(f32[16,32,128]{2,1,0:T(8,128)} %get-tuple-element.72), calls=%async_computation.7 | async-start | bytes 524288 | tf_op jit(solution)/shard_map/all_to_all | solution.py:29
  156.8 1.8 fusion.1.st_ref
  158.5 1.5 convolution_convert_fusion.psp_ref
  160.0 6.1 %all-to-all-done.7.got_ref = f32[16,32,128]{2,1,0:T(8,128)S(1)} async-done(((f32[16,32,128]{2,1,0:T(8,128)}), f32[16,32,128]{2,1,0:T(8,128)S(1)}, u32[]{:S(2)}, u32[]{:S(2)}) %all-to-all-start.7) | async-done | bytes 262176 | tf_op jit(solution)/shard_map/all_to_all | solution.py:29
  166.1 0.7 copy-done.15
  166.8 18.3 %shard_map.75 = (f32[4,4,192,256]{3,2,1,0:T(8,128)S(1)}, f32[2064,128]{1,0:T(8,128)}, f32[2064,128]{1,0:T(8,128)}) custom-call(s32[2]{0:T(128)S(1)} %copy-done.3, f32[16,32,128]{2,1,0:T(8,128)} %copy-done.15, f32[1,2048]{1,0:T(1,128)S(1)} %get-tuple-element.73.recip_ref, bf16[4,768,256]{2,1,0:T(8,128)(2,1)} %copy-done.4, bf16[4,256,768]{2,1,0:T(8,128)(2,1)} %fusion.1.st_ref, ...), custom_call_target="tpu_custom_call" | custom-call | flops 9663676416 | bytes 8388608 | tf_op jit(solution)/shard_map/pallas_call | solution.py:408
  185.1 1.5 multiply_convert_fusion
  186.6 3.8 %all-to-all-start.8 = ((f16[16,192,256]{2,1,0:T(8,128)(2,1)}), f16[16,192,256]{2,1,0:T(8,128)(2,1)S(1)}, u32[]{:S(2)}, u32[]{:S(2)}) async-start(f16[16,192,256]{2,1,0:T(8,128)(2,1)} %bitcast.103), calls=%async_computation.8 | async-start | bytes 3145728 | tf_op jit(solution)/shard_map/all_to_all | solution.py:29
  190.5 1.4 fusion.33
  192.1 0.8 collective-permute-start.11
  192.9 2.8 %collective-permute-start.12 = (f16[288,128]{1,0:T(8,128)(2,1)S(1)}, f16[288,128]{1,0:T(8,128)(2,1)S(1)}, u32[]{:S(2)}, u32[]{:S(2)}) collective-permute-start(f16[288,128]{1,0:T(8,128)(2,1)S(1)} %get-tuple-element.109), channel_id=1, source_target_pairs={{0,16},{8,24},{16,32},{24,40},{32,48},{40,56},{48,0},{56,8},{1,17}... | collective-permute-start | bytes 221192 | tf_op jit(solution)/shard_map/ppermute | solution.py:41
  196.4 3.2 %collective-permute-start.14 = (f16[288,128]{1,0:T(8,128)(2,1)S(1)}, f16[288,128]{1,0:T(8,128)(2,1)S(1)}, u32[]{:S(2)}, u32[]{:S(2)}) collective-permute-start(f16[288,128]{1,0:T(8,128)(2,1)S(1)} %get-tuple-element.111), channel_id=1, source_target_pairs={{0,32},{8,40},{16,48},{24,56},{32,0},{40,8},{48,16},{56,24},{1,33}... | collective-permute-start | bytes 221192 | tf_op jit(solution)/shard_map/ppermute | solution.py:41
  199.6 4.3 %collective-permute-start.15 = (f16[288,128]{1,0:T(8,128)(2,1)S(1)}, f16[288,128]{1,0:T(8,128)(2,1)S(1)}, u32[]{:S(2)}, u32[]{:S(2)}) collective-permute-start(f16[288,128]{1,0:T(8,128)(2,1)S(1)} %get-tuple-element.112), channel_id=1, source_target_pairs={{0,40},{8,48},{16,56},{24,0},{32,8},{40,16},{48,24},{56,32},{1,41}... | collective-permute-start | bytes 221192 | tf_op jit(solution)/shard_map/ppermute | solution.py:41
  204.0 2.4 %collective-permute-start.17 = (f16[288,128]{1,0:T(8,128)(2,1)S(1)}, f16[288,128]{1,0:T(8,128)(2,1)S(1)}, u32[]{:S(2)}, u32[]{:S(2)}) collective-permute-start(f16[288,128]{1,0:T(8,128)(2,1)S(1)} %pad_maximum_fusion.5), channel_id=1, source_target_pairs={{0,56},{8,0},{16,8},{24,16},{32,24},{40,32},{48,40},{56,48},{1,57}... | collective-permute-start | bytes 221192 | tf_op jit(solution)/shard_map/ppermute | solution.py:41
  206.4 0.8 convert_bitcast_fusion.1
  207.4 1.1 collective-permute-done.13
  208.5 3.2 %collective-permute-done.15 = f16[288,128]{1,0:T(8,128)(2,1)S(1)} collective-permute-done((f16[288,128]{1,0:T(8,128)(2,1)S(1)}, f16[288,128]{1,0:T(8,128)(2,1)S(1)}, u32[]{:S(2)}, u32[]{:S(2)}) %collective-permute-start.15) | collective-permute-done | bytes 73760 | tf_op jit(solution)/shard_map/ppermute | solution.py:41
  211.8 2.1 collective-permute-done.16
  213.9 1.2 collective-permute-done.17
  215.2 0.7 fusion.11
  216.1 0.7 fusion.4
  216.8 1.6 collective-permute-start.18
  218.4 2.7 %collective-permute-start.19 = (f32[32,6,256]{2,0,1:T(8,128)S(1)}, f32[32,6,256]{2,0,1:T(8,128)S(1)}, u32[]{:S(2)}, u32[]{:S(2)}) collective-permute-start(f32[32,6,256]{2,0,1:T(8,128)S(1)} %bitcast.118), channel_id=1, source_target_pairs={{0,2},{1,3},{2,0},{3,1},{4,6},{5,7},{6,4},{7,5},{8,10},{9,11},{10,... | collective-permute-start | bytes 589832 | tf_op jit(solution)/shard_map/ppermute | solution.py:41
  221.1 1.5 collective-permute-start.20
  222.6 4.3 %all-to-all-start.9 = ((f32[4,16,4,128]{3,1,2,0:T(8,128)}), f32[4,16,4,128]{3,1,2,0:T(8,128)S(1)}, u32[]{:S(2)}, u32[]{:S(2)}) async-start(f32[4,16,4,128]{3,1,2,0:T(8,128)} %bitcast.37), calls=%async_computation.9 | async-start | bytes 262144 | tf_op jit(solution)/shard_map/all_to_all | solution.py:29
  227.0 5.9 %all-to-all-done.9 = f32[4,16,4,128]{3,1,2,0:T(8,128)S(1)} async-done(((f32[4,16,4,128]{3,1,2,0:T(8,128)}), f32[4,16,4,128]{3,1,2,0:T(8,128)S(1)}, u32[]{:S(2)}, u32[]{:S(2)}) %all-to-all-start.9) | async-done | bytes 131104 | tf_op jit(solution)/shard_map/all_to_all | solution.py:29
  233.1 0.7 multiply_add_fusion
  234.0 0.9 copy-done.9
  (115 shorter events, 5.7 us)
Async XLA Ops:
  0.6 13.8 %copy-start.10 = (bf16[128,2,256]{2,1,0:T(2,128)(2,1)S(1)}, bf16[128,2,256]{2,1,0:T(2,128)(2,1)}, u32[]{:S(2)}) copy-start(bf16[128,2,256]{2,1,0:T(2,128)(2,1)} %param.4) | copy-start | bytes 393220
  0.6 13.9 %copy-start.5 = (bf16[128,6,256]{2,0,1:T(8,128)(2,1)S(1)}, bf16[128,6,256]{2,0,1:T(8,128)(2,1)}, u32[]{:S(2)}) copy-start(bf16[128,6,256]{2,0,1:T(8,128)(2,1)} %param.5) | copy-start | bytes 1179652
  2.8 23.4 %all-to-all-start = ((f32[64,8,128]{2,1,0:T(8,128)}), f32[64,8,128]{2,1,0:T(8,128)S(1)}, u32[]{:S(2)}, u32[]{:S(2)}) async-start(f32[64,8,128]{2,1,0:T(8,128)} %copy.45), calls=%async_computation | async-start | bytes 524288 | tf_op jit(solution)/shard_map/all_to_all | solution.py:29
  27.4 24.0 %all-to-all-start.1 = ((bf16[8,256,128]{2,1,0:T(8,128)(2,1)}), bf16[8,256,128]{2,1,0:T(8,128)(2,1)S(1)}, u32[]{:S(2)}, u32[]{:S(2)}) async-start(bf16[8,256,128]{2,1,0:T(8,128)(2,1)} %broadcast_in_dim.52), calls=%async_computation.1 | async-start | bytes 1048576 | tf_op jit(solution)/shard_map/all_to_all | solution.py:29
  32.2 21.1 %copy-start.2 = (s32[2]{0:T(128)}, s32[2]{0:T(128)S(1)}, u32[]{:S(2)}) copy-start(s32[2]{0:T(128)S(1)} %pad_add_fusion.place_ref) | copy-start | bytes 28
  32.2 19.1 %collective-permute-start = (bf16[256,256]{1,0:T(8,128)(2,1)S(1)}, bf16[256,256]{1,0:T(8,128)(2,1)S(1)}, u32[]{:S(2)}, u32[]{:S(2)}) collective-permute-start(bf16[256,256]{1,0:T(8,128)(2,1)S(1)} %fusion.6), channel_id=1, source_target_pairs={{0,64},{64,128},{128,192},{192,0},{1,65},{65,129},{129,193},{193,1... | collective-permute-start | bytes 393224 | tf_op jit(solution)/shard_map/ppermute | solution.py:41
  32.9 18.5 %collective-permute-start.1 = (bf16[256,256]{1,0:T(8,128)(2,1)S(1)}, bf16[256,256]{1,0:T(8,128)(2,1)S(1)}, u32[]{:S(2)}, u32[]{:S(2)}) collective-permute-start(bf16[256,256]{1,0:T(8,128)(2,1)S(1)} %fusion.6), channel_id=1, source_target_pairs={{0,128},{64,192},{128,0},{192,64},{1,129},{65,193},{129,1},{193,65... | collective-permute-start | bytes 393224 | tf_op jit(solution)/shard_map/ppermute | solution.py:41
  35.6 15.9 %collective-permute-start.2 = (bf16[256,256]{1,0:T(8,128)(2,1)S(1)}, bf16[256,256]{1,0:T(8,128)(2,1)S(1)}, u32[]{:S(2)}, u32[]{:S(2)}) collective-permute-start(bf16[256,256]{1,0:T(8,128)(2,1)S(1)} %fusion.6), channel_id=1, source_target_pairs={{0,192},{64,0},{128,64},{192,128},{1,193},{65,1},{129,65},{193,129... | collective-permute-start | bytes 393224 | tf_op jit(solution)/shard_map/ppermute | solution.py:41
  36.9 14.6 %collective-permute-start.6 = (bf16[1,768,256]{2,1,0:T(8,128)(2,1)S(1)}, bf16[1,768,256]{2,1,0:T(8,128)(2,1)S(1)}, u32[]{:S(2)}, u32[]{:S(2)}) collective-permute-start(bf16[1,768,256]{2,1,0:T(8,128)(2,1)S(1)} %bitcast.105), channel_id=1, source_target_pairs={{0,64},{64,0},{128,192},{192,128},{1,65},{65,1},{129,193},{193,129... | collective-permute-start | bytes 1179656 | tf_op jit(solution)/shard_map/ppermute | solution.py:54
  37.6 13.7 %collective-permute-start.4 = (bf16[1,256,128]{2,1,0:T(8,128)(2,1)S(1)}, bf16[1,256,128]{2,1,0:T(8,128)(2,1)S(1)}, u32[]{:S(2)}, u32[]{:S(2)}) collective-permute-start(bf16[1,256,128]{2,1,0:T(8,128)(2,1)S(1)} %bitcast.116), channel_id=1, source_target_pairs={{0,32},{8,40},{16,48},{24,56},{32,0},{40,8},{48,16},{56,24},{1,33}... | collective-permute-start | bytes 196616 | tf_op jit(solution)/shard_map/ppermute | solution.py:54
  51.4 2.0 collective-permute-start.3
  59.1 5.6 %collective-permute-start.5 = (bf16[2,256,128]{2,1,0:T(8,128)(2,1)S(1)}, bf16[2,256,128]{2,1,0:T(8,128)(2,1)S(1)}, u32[]{:S(2)}, u32[]{:S(2)}) collective-permute-start(bf16[2,256,128]{2,1,0:T(8,128)(2,1)S(1)} %pad_maximum_fusion.19), channel_id=1, source_target_pairs={{0,8},{8,0},{16,24},{24,16},{32,40},{40,32},{48,56},{56,48},{1,9},... | collective-permute-start | bytes 393224 | tf_op jit(solution)/shard_map/ppermute | solution.py:54
  60.6 12.5 %all-to-all-start.2 = ((f32[16,24,128]{2,1,0:T(8,128)}), f32[16,24,128]{2,1,0:T(8,128)S(1)}, u32[]{:S(2)}, u32[]{:S(2)}) async-start(f32[16,24,128]{2,1,0:T(8,128)} %get-tuple-element.49), calls=%async_computation.2 | async-start | bytes 393216 | tf_op jit(solution)/shard_map/all_to_all | solution.py:29
  77.4 20.1 %collective-permute-start.7 = (bf16[4,256,128]{2,1,0:T(8,128)(2,1)S(1)}, bf16[4,256,128]{2,1,0:T(8,128)(2,1)S(1)}, u32[]{:S(2)}, u32[]{:S(2)}) collective-permute-start(bf16[4,256,128]{2,1,0:T(8,128)(2,1)S(1)} %pad_maximum_fusion.4), channel_id=1, source_target_pairs={{0,16},{8,24},{16,0},{24,8},{32,48},{40,56},{48,32},{56,40},{1,17}... | collective-permute-start | bytes 786440 | tf_op jit(solution)/shard_map/ppermute | solution.py:54
  79.2 14.1 %all-to-all-start.3 = ((f32[16,8,128]{2,1,0:T(8,128)}), f32[16,8,128]{2,1,0:T(8,128)S(1)}, u32[]{:S(2)}, u32[]{:S(2)}) async-start(f32[16,8,128]{2,1,0:T(8,128)} %get-tuple-element.54), calls=%async_computation.3 | async-start | bytes 131072 | tf_op jit(solution)/shard_map/all_to_all | solution.py:29
  97.7 17.9 %copy-start.11 = (bf16[8,256,128]{2,1,0:T(8,128)(2,1)}, bf16[8,256,128]{2,1,0:T(8,128)(2,1)S(1)}, u32[]{:S(2)}) copy-start(bf16[8,256,128]{2,1,0:T(8,128)(2,1)S(1)} %pad_maximum_fusion.2.own_ref) | copy-start | bytes 1572868
  97.7 19.4 %collective-permute-start.9 = (bf16[2,768,256]{2,1,0:T(8,128)(2,1)S(1)}, bf16[2,768,256]{2,1,0:T(8,128)(2,1)S(1)}, u32[]{:S(2)}, u32[]{:S(2)}) collective-permute-start(bf16[2,768,256]{2,1,0:T(8,128)(2,1)S(1)} %pad_maximum_fusion.1), channel_id=1, source_target_pairs={{0,128},{64,192},{128,0},{192,64},{1,129},{65,193},{129,1},{193,65... | collective-permute-start | bytes 2359304 | tf_op jit(solution)/shard_map/ppermute | solution.py:54
  99.0 16.6 %collective-permute-start.8 = (bf16[8,256,128]{2,1,0:T(8,128)(2,1)S(1)}, bf16[8,256,128]{2,1,0:T(8,128)(2,1)S(1)}, u32[]{:S(2)}, u32[]{:S(2)}) collective-permute-start(bf16[8,256,128]{2,1,0:T(8,128)(2,1)S(1)} %pad_maximum_fusion.2.own_ref), channel_id=1, source_target_pairs={{0,4},{4,0},{1,5},{5,1},{2,6},{6,2},{3,7},{7,3},{8,12},{12,8},{9,1... | collective-permute-start | bytes 1572872 | tf_op jit(solution)/shard_map/ppermute | solution.py:37
  99.0 12.3 %all-to-all-start.4 = ((f32[16,16,128]{2,1,0:T(8,128)}), f32[16,16,128]{2,1,0:T(8,128)S(1)}, u32[]{:S(2)}, u32[]{:S(2)}) async-start(f32[16,16,128]{2,1,0:T(8,128)} %shard_map.69), calls=%async_computation.4 | async-start | bytes 262144 | tf_op jit(solution)/shard_map/all_to_all | solution.py:29
  115.6 5.4 %copy-start.16 = (bf16[8,256,128]{2,1,0:T(8,128)(2,1)}, bf16[8,256,128]{2,1,0:T(8,128)(2,1)S(1)}, u32[]{:S(2)}) copy-start(bf16[8,256,128]{2,1,0:T(8,128)(2,1)S(1)} %collective-permute-done.8.other_ref) | copy-start | bytes 1572868
  117.1 11.4 %all-to-all-start.5 = ((f32[16,8,128]{2,1,0:T(8,128)}), f32[16,8,128]{2,1,0:T(8,128)S(1)}, u32[]{:S(2)}, u32[]{:S(2)}) async-start(f32[16,8,128]{2,1,0:T(8,128)} %get-tuple-element.61), calls=%async_computation.5 | async-start | bytes 131072 | tf_op jit(solution)/shard_map/all_to_all | solution.py:29
  121.0 0.9 copy-start.6
  121.9 34.9 %copy-start.4 = (bf16[4,768,256]{2,1,0:T(8,128)(2,1)}, bf16[4,768,256]{2,1,0:T(8,128)(2,1)S(1)}, u32[]{:S(2)}) copy-start(bf16[4,768,256]{2,1,0:T(8,128)(2,1)S(1)} %pad_maximum_fusion.s_ref) | copy-start | bytes 4718596
  132.8 12.3 %all-to-all-start.6 = ((f32[16,16,128]{2,1,0:T(8,128)}), f32[16,16,128]{2,1,0:T(8,128)S(1)}, u32[]{:S(2)}, u32[]{:S(2)}) async-start(f32[16,16,128]{2,1,0:T(8,128)} %shard_map.71), calls=%async_computation.6 | async-start | bytes 262144 | tf_op jit(solution)/shard_map/all_to_all | solution.py:29
  138.8 6.3 %copy-start = (f32[12,128]{1,0:T(8,128)S(1)}, f32[12,128]{1,0:T(8,128)}, u32[]{:S(2)}) copy-start(f32[12,128]{1,0:T(8,128)} %get-tuple-element.68.refs_0_) | copy-start | bytes 18436
  145.1 0.7 copy-start.1
  150.1 15.9 %all-to-all-start.7 = ((f32[16,32,128]{2,1,0:T(8,128)}), f32[16,32,128]{2,1,0:T(8,128)S(1)}, u32[]{:S(2)}, u32[]{:S(2)}) async-start(f32[16,32,128]{2,1,0:T(8,128)} %get-tuple-element.72), calls=%async_computation.7 | async-start | bytes 524288 | tf_op jit(solution)/shard_map/all_to_all | solution.py:29
  156.8 1.8 copy-start.8
  158.5 8.2 %copy-start.3 = (s32[2]{0:T(128)S(1)}, s32[2]{0:T(128)}, u32[]{:S(2)}) copy-start(s32[2]{0:T(128)} %copy-done.2) | copy-start | bytes 28
  166.1 0.7 copy-start.15
  185.0 5.4 %collective-permute-start.10 = (f32[2064,128]{1,0:T(8,128)}, f32[2064,128]{1,0:T(8,128)}, u32[]{:S(2)}, u32[]{:S(2)}) collective-permute-start(f32[2064,128]{1,0:T(8,128)} %get-tuple-element.77), channel_id=1, source_target_pairs={{0,4},{4,0},{1,5},{5,1},{2,6},{6,2},{3,7},{7,3},{8,12},{12,8},{9,1... | collective-permute-start | bytes 3170312 | tf_op jit(solution)/shard_map/ppermute | solution.py:37
  186.6 3.9 %copy-start.7 = (f32[2064,128]{1,0:T(8,128)S(1)}, f32[2064,128]{1,0:T(8,128)}, u32[]{:S(2)}) copy-start(f32[2064,128]{1,0:T(8,128)} %get-tuple-element.76) | copy-start | bytes 3170308
  186.6 29.2 %all-to-all-start.8 = ((f16[16,192,256]{2,1,0:T(8,128)(2,1)}), f16[16,192,256]{2,1,0:T(8,128)(2,1)S(1)}, u32[]{:S(2)}, u32[]{:S(2)}) async-start(f16[16,192,256]{2,1,0:T(8,128)(2,1)} %bitcast.103), calls=%async_computation.8 | async-start | bytes 3145728 | tf_op jit(solution)/shard_map/all_to_all | solution.py:29
  192.1 11.8 %collective-permute-start.11 = (f16[288,128]{1,0:T(8,128)(2,1)S(1)}, f16[288,128]{1,0:T(8,128)(2,1)S(1)}, u32[]{:S(2)}, u32[]{:S(2)}) collective-permute-start(f16[288,128]{1,0:T(8,128)(2,1)S(1)} %get-tuple-element.108), channel_id=1, source_target_pairs={{0,8},{8,16},{16,24},{24,32},{32,40},{40,48},{48,56},{56,0},{1,9},... | collective-permute-start | bytes 221192 | tf_op jit(solution)/shard_map/ppermute | solution.py:41
  192.9 11.1 %collective-permute-start.12 = (f16[288,128]{1,0:T(8,128)(2,1)S(1)}, f16[288,128]{1,0:T(8,128)(2,1)S(1)}, u32[]{:S(2)}, u32[]{:S(2)}) collective-permute-start(f16[288,128]{1,0:T(8,128)(2,1)S(1)} %get-tuple-element.109), channel_id=1, source_target_pairs={{0,16},{8,24},{16,32},{24,40},{32,48},{40,56},{48,0},{56,8},{1,17}... | collective-permute-start | bytes 221192 | tf_op jit(solution)/shard_map/ppermute | solution.py:41
  195.7 12.8 %collective-permute-start.13 = (f16[288,128]{1,0:T(8,128)(2,1)S(1)}, f16[288,128]{1,0:T(8,128)(2,1)S(1)}, u32[]{:S(2)}, u32[]{:S(2)}) collective-permute-start(f16[288,128]{1,0:T(8,128)(2,1)S(1)} %get-tuple-element.110), channel_id=1, source_target_pairs={{0,24},{8,32},{16,40},{24,48},{32,56},{40,0},{48,8},{56,16},{1,25}... | collective-permute-start | bytes 221192 | tf_op jit(solution)/shard_map/ppermute | solution.py:41
  196.4 12.1 %collective-permute-start.14 = (f16[288,128]{1,0:T(8,128)(2,1)S(1)}, f16[288,128]{1,0:T(8,128)(2,1)S(1)}, u32[]{:S(2)}, u32[]{:S(2)}) collective-permute-start(f16[288,128]{1,0:T(8,128)(2,1)S(1)} %get-tuple-element.111), channel_id=1, source_target_pairs={{0,32},{8,40},{16,48},{24,56},{32,0},{40,8},{48,16},{56,24},{1,33}... | collective-permute-start | bytes 221192 | tf_op jit(solution)/shard_map/ppermute | solution.py:41
  199.6 12.2 %collective-permute-start.15 = (f16[288,128]{1,0:T(8,128)(2,1)S(1)}, f16[288,128]{1,0:T(8,128)(2,1)S(1)}, u32[]{:S(2)}, u32[]{:S(2)}) collective-permute-start(f16[288,128]{1,0:T(8,128)(2,1)S(1)} %get-tuple-element.112), channel_id=1, source_target_pairs={{0,40},{8,48},{16,56},{24,0},{32,8},{40,16},{48,24},{56,32},{1,41}... | collective-permute-start | bytes 221192 | tf_op jit(solution)/shard_map/ppermute | solution.py:41
  203.9 9.9 %collective-permute-start.16 = (f16[288,128]{1,0:T(8,128)(2,1)S(1)}, f16[288,128]{1,0:T(8,128)(2,1)S(1)}, u32[]{:S(2)}, u32[]{:S(2)}) collective-permute-start(f16[288,128]{1,0:T(8,128)(2,1)S(1)} %get-tuple-element.113), channel_id=1, source_target_pairs={{0,48},{8,56},{16,0},{24,8},{32,16},{40,24},{48,32},{56,40},{1,49}... | collective-permute-start | bytes 221192 | tf_op jit(solution)/shard_map/ppermute | solution.py:41
  204.0 11.0 %collective-permute-start.17 = (f16[288,128]{1,0:T(8,128)(2,1)S(1)}, f16[288,128]{1,0:T(8,128)(2,1)S(1)}, u32[]{:S(2)}, u32[]{:S(2)}) collective-permute-start(f16[288,128]{1,0:T(8,128)(2,1)S(1)} %pad_maximum_fusion.5), channel_id=1, source_target_pairs={{0,56},{8,0},{16,8},{24,16},{32,24},{40,32},{48,40},{56,48},{1,57}... | collective-permute-start | bytes 221192 | tf_op jit(solution)/shard_map/ppermute | solution.py:41
  216.1 17.0 %copy-start.13 = (f32[4,8192]{1,0:T(4,128)S(1)}, f32[4,8192]{1,0:T(4,128)}, u32[]{:S(2)}) copy-start(f32[4,8192]{1,0:T(4,128)} %param.7) | copy-start | bytes 393220
  216.1 17.0 %copy-start.14 = (f32[4,8192]{1,0:T(4,128)S(1)}, f32[4,8192]{1,0:T(4,128)}, u32[]{:S(2)}) copy-start(f32[4,8192]{1,0:T(4,128)} %param.6) | copy-start | bytes 393220
  216.8 17.0 %collective-permute-start.18 = (f32[32,6,256]{2,0,1:T(8,128)S(1)}, f32[32,6,256]{2,0,1:T(8,128)S(1)}, u32[]{:S(2)}, u32[]{:S(2)}) collective-permute-start(f32[32,6,256]{2,0,1:T(8,128)S(1)} %bitcast.117), channel_id=1, source_target_pairs={{0,1},{1,2},{2,3},{3,0},{4,5},{5,6},{6,7},{7,4},{8,9},{9,10},{10,1... | collective-permute-start | bytes 589832 | tf_op jit(solution)/shard_map/ppermute | solution.py:41
  218.4 15.4 %collective-permute-start.19 = (f32[32,6,256]{2,0,1:T(8,128)S(1)}, f32[32,6,256]{2,0,1:T(8,128)S(1)}, u32[]{:S(2)}, u32[]{:S(2)}) collective-permute-start(f32[32,6,256]{2,0,1:T(8,128)S(1)} %bitcast.118), channel_id=1, source_target_pairs={{0,2},{1,3},{2,0},{3,1},{4,6},{5,7},{6,4},{7,5},{8,10},{9,11},{10,... | collective-permute-start | bytes 589832 | tf_op jit(solution)/shard_map/ppermute | solution.py:41
  221.1 12.8 %collective-permute-start.20 = (f32[32,6,256]{2,0,1:T(8,128)S(1)}, f32[32,6,256]{2,0,1:T(8,128)S(1)}, u32[]{:S(2)}, u32[]{:S(2)}) collective-permute-start(f32[32,6,256]{2,0,1:T(8,128)S(1)} %bitcast.119), channel_id=1, source_target_pairs={{0,3},{1,0},{2,1},{3,2},{4,7},{5,4},{6,5},{7,6},{8,11},{9,8},{10,9... | collective-permute-start | bytes 589832 | tf_op jit(solution)/shard_map/ppermute | solution.py:41
  222.6 10.3 %all-to-all-start.9 = ((f32[4,16,4,128]{3,1,2,0:T(8,128)}), f32[4,16,4,128]{3,1,2,0:T(8,128)S(1)}, u32[]{:S(2)}, u32[]{:S(2)}) async-start(f32[4,16,4,128]{3,1,2,0:T(8,128)} %bitcast.37), calls=%async_computation.9 | async-start | bytes 262144 | tf_op jit(solution)/shard_map/all_to_all | solution.py:29
  233.1 0.9 copy-start.12
  233.9 0.9 copy-start.9

commit v3 on v2

--- a/solution.py
+++ b/solution.py
@@ -100,6 +100,14 @@
         out_ref[p, :count] = lines
 
 
+def pack_kernel(t_ref, s_ref, out_ref):
+    lines = t_ref.shape[0]
+    for d in range(out_ref.shape[0]):
+        lanes = slice(d * LANES, (d + 1) * LANES)
+        out_ref[d, :lines] = t_ref[:, lanes]
+        out_ref[d, lines:] = s_ref[:, lanes]
+
+
 def energy_kernel(place_ref, norm_ref, t_ref, own_ref, other_ref, e_ref, out_ref, proto_ref, acc_ref, held_ref, sem_ref):
     join_columns(place_ref, own_ref, other_ref, proto_ref)
     width = e_ref.shape[1]
@@ -220,45 +228,56 @@
     images = rows // CROPS
     tile = 1024
     g = pl.program_id(0)
-    groups = pl.num_programs(0)
+    groups = pl.num_programs(0) - 1
 
     @pl.when(g == 0)
     def _():
         lines_ref[...] = factor / jnp.sum(got_ref[...], axis=0)
         total_ref[...] = jnp.zeros_like(total_ref)
-
-    for i in range(2):
-        down_ref[i] = down(lines_ref[pl.ds(g * 2 + i, 1), :])
-    for crop in range(CROPS):
-        line = down(lines_ref[pl.ds(groups * 2 + g * CROPS + crop, 1), :])
-        down_ref[2 + crop] = line if crop < 2 else 2.0 * line
-
-    def columns(j, _):
-        at = pl.ds(pl.multiple_of(j * tile, tile), tile)
-        wide = lambda i: jnp.concatenate([down_ref[i]] * (tile // LANES), axis=1)
-        recip = recip_ref[:, at]
-        t0 = e_ref[:images, at] * recip * wide(0)
-        t1 = e_ref[images:, at] * recip * wide(1)
-        both = t0 + t1
-        scores = jnp.dot(s_ref[0], ps_ref[:, at], preferred_element_type=jnp.float32)
+        slope_ref[1] = jnp.zeros_like(slope_ref[1])
+
+    def products(slot):
+        total_ref[...] += jnp.dot(st_ref[0], slope_ref[slot], preferred_element_type=jnp.float32)
+        unit = lax.dot_general(
+            slope_ref[slot], ps_ref[...], (((1,), (1,)), ((), ())), preferred_element_type=jnp.float32
+        )
+        part = images // NY
         for crop in range(CROPS):
-            lines = slice(crop * images, (crop + 1) * images)
-            part = wide(2 + crop) * jnp.exp2(scores[lines] * (LOG2E / TEMP_S))
-            minus = t1 if crop == 0 else t0 if crop == 1 else both
-            slope_ref[lines, at] = (part - minus).astype(jnp.bfloat16)
-        return 0
-
-    lax.fori_loop(0, width // tile, columns, 0)
-    total_ref[...] += jnp.dot(st_ref[0], slope_ref[...], preferred_element_type=jnp.float32)
-    unit = lax.dot_general(
-        slope_ref[...], ps_ref[...], (((1,), (1,)), ((), ())), preferred_element_type=jnp.float32
-    )
-    part = images // NY
-    for crop in range(CROPS):
-        for y in range(NY):
-            ug_ref[0, y, crop * part : (crop + 1) * part, :] = unit[crop * images + y * part :][:part]
-
-    @pl.when(g == groups - 1)
+            for y in range(NY):
+                ug_ref[0, y, crop * part : (crop + 1) * part, :] = unit[crop * images + y * part :][:part]
+
+    def slopes_into(slot):
+        for i in range(2):
+            down_ref[i] = down(lines_ref[pl.ds(g * 2 + i, 1), :])
+        for crop in range(CROPS):
+            line = down(lines_ref[pl.ds(groups * 2 + g * CROPS + crop, 1), :])
+            down_ref[2 + crop] = line if crop < 2 else 2.0 * line
+        for j in range(width // tile):
+            at = slice(j * tile, (j + 1) * tile)
+            wide = lambda i: jnp.concatenate([down_ref[i]] * (tile // LANES), axis=1)
+            recip = recip_ref[:, at]
+            t0 = e_ref[:images, at] * recip * wide(0)
+            t1 = e_ref[images:, at] * recip * wide(1)
+            both = t0 + t1
+            scores = jnp.dot(s_ref[0], ps_ref[:, at], preferred_element_type=jnp.float32)
+            for crop in range(CROPS):
+                lines = slice(crop * images, (crop + 1) * images)
+                part = wide(2 + crop) * jnp.exp2(scores[lines] * (LOG2E / TEMP_S))
+                minus = t1 if crop == 0 else t0 if crop == 1 else both
+                slope_ref[slot, lines, at] = (part - minus).astype(jnp.bfloat16)
+
+    for slot in range(2):
+
+        @pl.when((g < groups) & (g % 2 == slot))
+        def _():
+            slopes_into(slot)
+            products(1 - slot)
+
+    @pl.when(g == groups)
+    def _():
+        products((NX - 1) % 2)
+
+    @pl.when(g == groups)
     def _():
         blocks = width // LANES
         part = total_ref.shape[0] // (NC * NZ)
@@ -294,8 +313,10 @@
     t_float = teacher_feats.transpose(1, 0, 2).reshape(t_rows, bottleneck).astype(f32)
     t_unit = (t_float / jnp.sqrt(jnp.sum(t_float * t_float, axis=1, keepdims=True) + EPS)).astype(bf16)
 
-    shards = jnp.stack([teacher_weight, student_weight]).reshape(2 * rows_here, NX * NZ * NC, sub)
-    moved, t_unit = lax.optimization_barrier((swap(shards.transpose(1, 0, 2), DP), t_unit))
+    (shards,) = call(
+        pack_kernel, [shape((NX * NZ * NC, 2 * rows_here, sub), f32)], [VMEM, VMEM], limit=58
+    )(teacher_weight, student_weight)
+    moved, t_unit = lax.optimization_barrier((swap(shards, DP), t_unit))
     t_all = along(t_unit, "x", NX).reshape(NX * t_rows, bottleneck)
     moved = moved.reshape(NX * NZ * NC, 2, rows_here, sub)
     cols_t = moved[:, 0].reshape(bottleneck, sub)
@@ -362,7 +383,7 @@
         return to_devices
 
     half_rows = NX * s_rows // 2
-    student = dict(limit=58, flops=exact * 3 * bottleneck, exps=exact * 3 // 2)
+    student = dict(limit=20, flops=exact * 3 * bottleneck, exps=exact * 3 // 2)
 
     to_devices, own_s = lax.optimization_barrier((to_devices, merged(pair, "z", 4)))
     got = swap(to_devices, ZC)
@@ -412,24 +433,24 @@
             SMEM,
             whole(NX * NY, NX * (2 + CROPS), LANES),
             whole(1, width),
-            pl.BlockSpec((1, s_rows, bottleneck), lambda g: (g, 0, 0)),
-            pl.BlockSpec((1, bottleneck, s_rows), lambda g: (g, 0, 0)),
+            pl.BlockSpec((1, s_rows, bottleneck), lambda g: (jnp.minimum(g, NX - 1), 0, 0)),
+            pl.BlockSpec((1, bottleneck, s_rows), lambda g: (jnp.maximum(g - 1, 0), 0, 0)),
             whole(bottleneck, width),
             whole(bottleneck, width),
-            pl.BlockSpec((t_rows, width), lambda g: (g, 0)),
+            pl.BlockSpec((t_rows, width), lambda g: (jnp.minimum(g, NX - 1), 0)),
         ],
         [
-            pltpu.VMEM((s_rows, width), bf16),
+            pltpu.VMEM((2, s_rows, width), bf16),
             pltpu.VMEM((bottleneck, width), f32),
             pltpu.VMEM((NX * (2 + CROPS), LANES), f32),
             pltpu.VMEM((2 + CROPS, LANES, LANES), f32),
         ],
         [
-            pl.BlockSpec((1, NY, s_rows // NY, bottleneck), lambda g: (g, 0, 0, 0)),
+            pl.BlockSpec((1, NY, s_rows // NY, bottleneck), lambda g: (jnp.maximum(g - 1, 0), 0, 0, 0)),
             whole(NZ * size + width // LANES, LANES),
             whole(NZ * size + width // LANES, LANES),
         ],
-        (NX,),
+        (NX + 1,),
         limit=40,
         flops=6 * exact * 3 * bottleneck,
         moved=4 * exact,

time: 236 us -> 234 us (level)
  Pallas kernels: 56.7 us -> 53.3 us
  other arithmetic: 9.09 us -> 12.3 us
  transfers between devices with their start and end apart: 31 -> 31, of which waited for: 16 -> 16; matrix products, arithmetic and copies ran while one was open for 5% -> 8% of each run, Pallas kernels for 8% -> 7%
where the time goes in v3:
time: 234 us; the launch traced here: 233 us
  starting transfers between devices  88.1 us (38%)
  waiting for transfers between devices  67.5 us (29%)
  Pallas kernels  53.3 us (23%)
  other arithmetic  12.3 us (5%)
  local copies, waits for them, and re-layouts  5.36 us (2%)
  matrix products  4.62 us (2%)
    all_to_all x10, starting transfers between devices, swap(): return lax.all_to_all(v, axes, 0, 0)  55 us
    all_to_all x10, waiting for transfers between devices, swap(): return lax.all_to_all(v, axes, 0, 0)  47 us
    ppermute x13, starting transfers between devices, shifted(): return lax.ppermute(v, axis, [(i, (i + k) % n) for i in range(n)])  23.3 us
    pallas_call x1, Pallas kernels, local(): call(functools.partial(slope_kernel, total_k / 16.0), [pltpu.VMEM((NX, NY...  17.1 us
    pallas_call x3, Pallas kernels, by_row(): call(by_row_kernel, [shape((1, width), f32), shape((NX * NY, lines, LANES...  12.9 us
    ppermute x5, waiting for transfers between devices, exchanged(): return (v, lax.ppermute(v, axis, [(i, i ^ step) for i in range(n)]))  10.8 us
    ppermute x5, starting transfers between devices, exchanged(): return (v, lax.ppermute(v, axis, [(i, i ^ step) for i in range(n)]))  9.82 us
    pallas_call x2, Pallas kernels, by_column(): call(by_column_kernel, [shape((NZ * NC, width // LANES, LANES), f32)], [V...  8.58 us
  transfers between devices with their start and end apart: 31, of which 16 were waited for; matrix products, arithmetic and copies ran while one was open for 8% of the time, Pallas kernels for 7%

profile of v3, /device:TPU:32, one launch (start us, length us, event | category | flops | bytes accessed | tf_op | source)
XLA Modules:
  0.0 232.6 jit_solution(728485111219400323)
XLA Ops:
  0.6 1.8 shard_map.67
  2.4 11.6 %all-to-all-start = ((f32[64,8,128]{2,1,0:T(8,128)}), f32[64,8,128]{2,1,0:T(8,128)S(1)}, u32[]{:S(2)}, u32[]{:S(2)}) async-start(f32[64,8,128]{2,1,0:T(8,128)} %shard_map.67), calls=%async_computation | async-start | bytes 524288 | tf_op jit(solution)/shard_map/all_to_all | solution.py:29
  14.0 0.9 copy_convert_fusion
  14.9 1.0 multiply_reduce_fusion.1
  16.9 8.9 %all-to-all-done = f32[64,8,128]{2,1,0:T(8,128)S(1)} async-done(((f32[64,8,128]{2,1,0:T(8,128)}), f32[64,8,128]{2,1,0:T(8,128)S(1)}, u32[]{:S(2)}, u32[]{:S(2)}) %all-to-all-start) | async-done | bytes 262176 | tf_op jit(solution)/shard_map/all_to_all | solution.py:29
  26.0 0.9 broadcast_in_dim.52
  26.9 4.8 %all-to-all-start.1 = ((bf16[8,256,128]{2,1,0:T(8,128)(2,1)}), bf16[8,256,128]{2,1,0:T(8,128)(2,1)S(1)}, u32[]{:S(2)}, u32[]{:S(2)}) async-start(bf16[8,256,128]{2,1,0:T(8,128)(2,1)} %broadcast_in_dim.52), calls=%async_computation.1 | async-start | bytes 1048576 | tf_op jit(solution)/shard_map/all_to_all | solution.py:29
  32.4 2.7 %collective-permute-start.1 = (bf16[256,256]{1,0:T(8,128)(2,1)S(1)}, bf16[256,256]{1,0:T(8,128)(2,1)S(1)}, u32[]{:S(2)}, u32[]{:S(2)}) collective-permute-start(bf16[256,256]{1,0:T(8,128)(2,1)S(1)} %fusion.6), channel_id=1, source_target_pairs={{0,128},{64,192},{128,0},{192,64},{1,129},{65,193},{129,1},{193,65... | collective-permute-start | bytes 393224 | tf_op jit(solution)/shard_map/ppermute | solution.py:41
  35.1 1.4 collective-permute-start.2
  37.1 4.5 %collective-permute-start.4 = (bf16[1,256,128]{2,1,0:T(8,128)(2,1)S(1)}, bf16[1,256,128]{2,1,0:T(8,128)(2,1)S(1)}, u32[]{:S(2)}, u32[]{:S(2)}) collective-permute-start(bf16[1,256,128]{2,1,0:T(8,128)(2,1)S(1)} %bitcast.116), channel_id=1, source_target_pairs={{0,32},{8,40},{16,48},{24,56},{32,0},{40,8},{48,16},{56,24},{1,33}... | collective-permute-start | bytes 196616 | tf_op jit(solution)/shard_map/ppermute | solution.py:54
  41.7 9.1 %collective-permute-done.4 = bf16[1,256,128]{2,1,0:T(8,128)(2,1)S(1)} collective-permute-done((bf16[1,256,128]{2,1,0:T(8,128)(2,1)S(1)}, bf16[1,256,128]{2,1,0:T(8,128)(2,1)S(1)}, u32[]{:S(2)}, u32[]{:S(2)}) %collective-permute-start.4) | collective-permute-done | bytes 65568 | tf_op jit(solution)/shard_map/ppermute | solution.py:54
  51.1 1.7 collective-permute-done.3.other_ref
  52.9 5.7 %shard_map.68 = (f32[1024,2048]{1,0:T(8,128)}, f32[16,24,128]{2,1,0:T(8,128)}) custom-call(s32[2]{0:T(128)S(1)} %pad_add_fusion.place_ref, f32[1,128]{1,0:T(1,128)S(1)} %get-tuple-element.116.norm_ref, bf16[1024,256]{1,0:T(8,128)(2,1)S(1)} %bitcast.106, bf16[8,256,128]{2,1,0:T(8,128)(2,1)S(1)} %all-to-all-done.1.own_ref, ...), custom_call_target="tpu_custom_call" | custom-call | flops 1073741824 | tf_op jit(solution)/shard_map/pallas_call | solution.py:336
  58.6 1.6 collective-permute-start.5
  60.1 3.9 %all-to-all-start.2 = ((f32[16,24,128]{2,1,0:T(8,128)}), f32[16,24,128]{2,1,0:T(8,128)S(1)}, u32[]{:S(2)}, u32[]{:S(2)}) async-start(f32[16,24,128]{2,1,0:T(8,128)} %get-tuple-element.49), calls=%async_computation.2 | async-start | bytes 393216 | tf_op jit(solution)/shard_map/all_to_all | solution.py:29
  64.3 8.3 %all-to-all-done.2.got_ref = f32[16,24,128]{2,1,0:T(8,128)S(1)} async-done(((f32[16,24,128]{2,1,0:T(8,128)}), f32[16,24,128]{2,1,0:T(8,128)S(1)}, u32[]{:S(2)}, u32[]{:S(2)}) %all-to-all-start.2) | async-done | bytes 196640 | tf_op jit(solution)/shard_map/all_to_all | solution.py:29
  72.6 4.3 %shard_map.69 = (f32[1,2048]{1,0:T(1,128)}, f32[16,8,128]{2,1,0:T(8,128)}) custom-call(f32[16,24,128]{2,1,0:T(8,128)S(1)} %all-to-all-done.2.got_ref, f32[1024,2048]{1,0:T(8,128)} %get-tuple-element.50.e_ref), custom_call_target="tpu_custom_call" | custom-call | flops 4194304 | bytes 8388608 | tf_op jit(solution)/shard_map/pallas_call | solution.py:363
  76.9 1.8 collective-permute-start.7
  78.7 6.4 %all-to-all-start.3 = ((f32[16,8,128]{2,1,0:T(8,128)}), f32[16,8,128]{2,1,0:T(8,128)S(1)}, u32[]{:S(2)}, u32[]{:S(2)}) async-start(f32[16,8,128]{2,1,0:T(8,128)} %get-tuple-element.54), calls=%async_computation.3 | async-start | bytes 131072 | tf_op jit(solution)/shard_map/all_to_all | solution.py:29
  85.1 7.6 %all-to-all-done.3.got_ref = f32[16,8,128]{2,1,0:T(8,128)S(1)} async-done(((f32[16,8,128]{2,1,0:T(8,128)}), f32[16,8,128]{2,1,0:T(8,128)S(1)}, u32[]{:S(2)}, u32[]{:S(2)}) %all-to-all-start.3) | async-done | bytes 65568 | tf_op jit(solution)/shard_map/all_to_all | solution.py:29
  92.7 4.3 %shard_map.70 = f32[16,16,128]{2,1,0:T(8,128)} custom-call(f32[16,8,128]{2,1,0:T(8,128)S(1)} %all-to-all-done.3.got_ref, f32[1024,2048]{1,0:T(8,128)} %get-tuple-element.50.e_ref), custom_call_target="tpu_custom_call" | custom-call | flops 4194304 | bytes 8388608 | tf_op jit(solution)/shard_map/pallas_call | solution.py:374
  97.1 1.3 collective-permute-start.9
  98.5 4.9 %all-to-all-start.4 = ((f32[16,16,128]{2,1,0:T(8,128)}), f32[16,16,128]{2,1,0:T(8,128)S(1)}, u32[]{:S(2)}, u32[]{:S(2)}) async-start(f32[16,16,128]{2,1,0:T(8,128)} %shard_map.70), calls=%async_computation.4 | async-start | bytes 262144 | tf_op jit(solution)/shard_map/all_to_all | solution.py:29
  103.4 7.4 %all-to-all-done.4.got_ref = f32[16,16,128]{2,1,0:T(8,128)S(1)} async-done(((f32[16,16,128]{2,1,0:T(8,128)}), f32[16,16,128]{2,1,0:T(8,128)S(1)}, u32[]{:S(2)}, u32[]{:S(2)}) %all-to-all-start.4) | async-done | bytes 131104 | tf_op jit(solution)/shard_map/all_to_all | solution.py:29
  110.7 4.3 %shard_map.71 = (f32[1,2048]{1,0:T(1,128)}, f32[16,8,128]{2,1,0:T(8,128)}) custom-call(f32[16,16,128]{2,1,0:T(8,128)S(1)} %all-to-all-done.4.got_ref, f32[1024,2048]{1,0:T(8,128)} %get-tuple-element.50.e_ref), custom_call_target="tpu_custom_call" | custom-call | flops 4194304 | bytes 8388608 | tf_op jit(solution)/shard_map/pallas_call | solution.py:363
  115.0 1.6 collective-permute-done.9
  116.6 0.9 copy-done.4
  117.5 3.7 %all-to-all-start.5 = ((f32[16,8,128]{2,1,0:T(8,128)}), f32[16,8,128]{2,1,0:T(8,128)S(1)}, u32[]{:S(2)}, u32[]{:S(2)}) async-start(f32[16,8,128]{2,1,0:T(8,128)} %get-tuple-element.61), calls=%async_computation.5 | async-start | bytes 131072 | tf_op jit(solution)/shard_map/all_to_all | solution.py:29
  121.2 1.2 broadcast_select_fusion
  122.4 1.3 pad_maximum_fusion.s_ref
  123.7 4.0 %shard_map.73 = (bf16[256,2048]{1,0:T(8,128)(2,1)S(1)}, f32[12,128]{1,0:T(8,128)S(1)}) custom-call(s32[2]{0:T(128)S(1)} %pad_add_fusion.place_ref, bf16[1536,256]{1,0:T(8,128)(2,1)S(1)} %bitcast.104, bf16[8,256,128]{2,1,0:T(8,128)(2,1)S(1)} %pad_maximum_fusion.2.own_ref, bf16[8,256,128]{2,1,0:T(8,128)(2,1)S(1)} %collective-permute-done.8.other_ref), custom_call_target="tpu_custom_call" | custom-call | flops 1610612736 | tf_op jit(solution)/shard_map/pallas_call | solution.py:407
  127.7 1.1 all-to-all-done.5.got_ref
  128.9 4.3 %shard_map.72 = f32[16,16,128]{2,1,0:T(8,128)} custom-call(f32[16,8,128]{2,1,0:T(8,128)S(1)} %all-to-all-done.5.got_ref, f32[1024,2048]{1,0:T(8,128)} %get-tuple-element.50.e_ref), custom_call_target="tpu_custom_call" | custom-call | flops 4194304 | bytes 8388608 | tf_op jit(solution)/shard_map/pallas_call | solution.py:374
  133.2 5.1 %all-to-all-start.6 = ((f32[16,16,128]{2,1,0:T(8,128)}), f32[16,16,128]{2,1,0:T(8,128)S(1)}, u32[]{:S(2)}, u32[]{:S(2)}) async-start(f32[16,16,128]{2,1,0:T(8,128)} %shard_map.72), calls=%async_computation.6 | async-start | bytes 262144 | tf_op jit(solution)/shard_map/all_to_all | solution.py:29
  138.4 1.2 slice.114
  139.6 3.2 %shard_map.74.refs_1_ = f32[12,128]{1,0:T(8,128)S(1)} custom-call(bf16[1536,256]{1,0:T(8,128)(2,1)S(1)} %bitcast.105, bf16[256,2048]{1,0:T(8,128)(2,1)S(1)} %get-tuple-element.75.proto_ref.ps_ref), custom_call_target="tpu_custom_call" | custom-call | flops 1610612736 | tf_op jit(solution)/shard_map/pallas_call | solution.py:417
  142.8 2.9 %all-to-all-done.6.got_ref = f32[16,16,128]{2,1,0:T(8,128)S(1)} async-done(((f32[16,16,128]{2,1,0:T(8,128)}), f32[16,16,128]{2,1,0:T(8,128)S(1)}, u32[]{:S(2)}, u32[]{:S(2)}) %all-to-all-start.6) | async-done | bytes 131104 | tf_op jit(solution)/shard_map/all_to_all | solution.py:29
  145.6 4.3 %shard_map.75 = (f32[1,2048]{1,0:T(1,128)S(1)}, f32[16,32,128]{2,1,0:T(8,128)}) custom-call(f32[16,16,128]{2,1,0:T(8,128)S(1)} %all-to-all-done.6.got_ref, f32[1024,2048]{1,0:T(8,128)} %get-tuple-element.50.e_ref, f32[12,128]{1,0:T(8,128)S(1)} %get-tuple-element.68.refs_0_, f32[12,128]{1,0:T(8,128)S(1)} %shard_map.74.refs_1_), custom_call_target="tpu_custom_call" | custom-call | flops 4194304 | bytes 8388608 | tf_op jit(solution)/shard_map/pallas_call | solution.py:363
  150.0 6.5 %all-to-all-start.7 = ((f32[16,32,128]{2,1,0:T(8,128)}), f32[16,32,128]{2,1,0:T(8,128)S(1)}, u32[]{:S(2)}, u32[]{:S(2)}) async-start(f32[16,32,128]{2,1,0:T(8,128)} %get-tuple-element.72), calls=%async_computation.7 | async-start | bytes 524288 | tf_op jit(solution)/shard_map/all_to_all | solution.py:29
  156.4 3.2 %fusion.1.st_ref = bf16[4,256,768]{2,1,0:T(8,128)(2,1)} fusion(bf16[4,768,256]{2,1,0:T(8,128)(2,1)} %pad_maximum_fusion.s_ref, s32[256]{0:T(256)S(1)} %reshape.210), kind=kOutput, calls=%fused_computation.6 | convolution fusion | flops 403505152 | bytes 3146752 | tf_op jit(solution)/shard_map/pb,grb->gpr/dot_general | solution.py:427
  159.6 1.5 convolution_convert_fusion.psp_ref
  161.1 4.7 %all-to-all-done.7.got_ref = f32[16,32,128]{2,1,0:T(8,128)S(1)} async-done(((f32[16,32,128]{2,1,0:T(8,128)}), f32[16,32,128]{2,1,0:T(8,128)S(1)}, u32[]{:S(2)}, u32[]{:S(2)}) %all-to-all-start.7) | async-done | bytes 262176 | tf_op jit(solution)/shard_map/all_to_all | solution.py:29
  166.5 17.1 %shard_map.76 = (f32[4,4,192,256]{3,2,1,0:T(8,128)S(1)}, f32[2064,128]{1,0:T(8,128)}, f32[2064,128]{1,0:T(8,128)}) custom-call(s32[2]{0:T(128)S(1)} %pad_add_fusion.place_ref, f32[16,32,128]{2,1,0:T(8,128)} %copy-done.8, f32[1,2048]{1,0:T(1,128)S(1)} %get-tuple-element.73.recip_ref, bf16[4,768,256]{2,1,0:T(8,128)(2,1)} %pad_maximum_fusion.s_ref, ...), custom_call_target="tpu_custom_call" | custom-call | flops 9663676416 | bytes 8388608 | tf_op jit(solution)/shard_map/pallas_call | solution.py:429
  183.6 1.6 multiply_convert_fusion
  185.2 3.8 %all-to-all-start.8 = ((f16[16,192,256]{2,1,0:T(8,128)(2,1)}), f16[16,192,256]{2,1,0:T(8,128)(2,1)S(1)}, u32[]{:S(2)}, u32[]{:S(2)}) async-start(f16[16,192,256]{2,1,0:T(8,128)(2,1)} %bitcast.107), calls=%async_computation.8 | async-start | bytes 3145728 | tf_op jit(solution)/shard_map/all_to_all | solution.py:29
  189.1 1.4 fusion.34
  190.7 0.8 collective-permute-start.11
  191.5 1.0 collective-permute-start.12
  192.5 2.4 %collective-permute-start.13 = (f16[288,128]{1,0:T(8,128)(2,1)S(1)}, f16[288,128]{1,0:T(8,128)(2,1)S(1)}, u32[]{:S(2)}, u32[]{:S(2)}) collective-permute-start(f16[288,128]{1,0:T(8,128)(2,1)S(1)} %get-tuple-element.109), channel_id=1, source_target_pairs={{0,24},{8,32},{16,40},{24,48},{32,56},{40,0},{48,8},{56,16},{1,25}... | collective-permute-start | bytes 221192 | tf_op jit(solution)/shard_map/ppermute | solution.py:41
  194.9 3.3 %collective-permute-start.14 = (f16[288,128]{1,0:T(8,128)(2,1)S(1)}, f16[288,128]{1,0:T(8,128)(2,1)S(1)}, u32[]{:S(2)}, u32[]{:S(2)}) collective-permute-start(f16[288,128]{1,0:T(8,128)(2,1)S(1)} %get-tuple-element.110), channel_id=1, source_target_pairs={{0,32},{8,40},{16,48},{24,56},{32,0},{40,8},{48,16},{56,24},{1,33}... | collective-permute-start | bytes 221192 | tf_op jit(solution)/shard_map/ppermute | solution.py:41
  198.2 4.3 %collective-permute-start.15 = (f16[288,128]{1,0:T(8,128)(2,1)S(1)}, f16[288,128]{1,0:T(8,128)(2,1)S(1)}, u32[]{:S(2)}, u32[]{:S(2)}) collective-permute-start(f16[288,128]{1,0:T(8,128)(2,1)S(1)} %get-tuple-element.111), channel_id=1, source_target_pairs={{0,40},{8,48},{16,56},{24,0},{32,8},{40,16},{48,24},{56,32},{1,41}... | collective-permute-start | bytes 221192 | tf_op jit(solution)/shard_map/ppermute | solution.py:41
  202.6 1.3 collective-permute-start.17
  203.9 0.8 convert_bitcast_fusion.1
  204.8 2.5 %collective-permute-done.13 = f16[288,128]{1,0:T(8,128)(2,1)S(1)} collective-permute-done((f16[288,128]{1,0:T(8,128)(2,1)S(1)}, f16[288,128]{1,0:T(8,128)(2,1)S(1)}, u32[]{:S(2)}, u32[]{:S(2)}) %collective-permute-start.13) | collective-permute-done | bytes 73760 | tf_op jit(solution)/shard_map/ppermute | solution.py:41
  207.4 3.7 %collective-permute-done.15 = f16[288,128]{1,0:T(8,128)(2,1)S(1)} collective-permute-done((f16[288,128]{1,0:T(8,128)(2,1)S(1)}, f16[288,128]{1,0:T(8,128)(2,1)S(1)}, u32[]{:S(2)}, u32[]{:S(2)}) %collective-permute-start.15) | collective-permute-done | bytes 73760 | tf_op jit(solution)/shard_map/ppermute | solution.py:41
  211.1 1.7 collective-permute-done.17
  214.2 0.7 fusion.4
  214.9 1.3 collective-permute-start.18
  216.2 2.7 %collective-permute-start.19 = (f32[32,6,256]{2,0,1:T(8,128)S(1)}, f32[32,6,256]{2,0,1:T(8,128)S(1)}, u32[]{:S(2)}, u32[]{:S(2)}) collective-permute-start(f32[32,6,256]{2,0,1:T(8,128)S(1)} %bitcast.118), channel_id=1, source_target_pairs={{0,2},{1,3},{2,0},{3,1},{4,6},{5,7},{6,4},{7,5},{8,10},{9,11},{10,... | collective-permute-start | bytes 589832 | tf_op jit(solution)/shard_map/ppermute | solution.py:41
  218.9 1.5 collective-permute-start.20
  220.4 4.3 %all-to-all-start.9 = ((f32[4,16,4,128]{3,1,2,0:T(8,128)}), f32[4,16,4,128]{3,1,2,0:T(8,128)S(1)}, u32[]{:S(2)}, u32[]{:S(2)}) async-start(f32[4,16,4,128]{3,1,2,0:T(8,128)} %bitcast.34), calls=%async_computation.9 | async-start | bytes 262144 | tf_op jit(solution)/shard_map/all_to_all | solution.py:29
  224.8 5.9 %all-to-all-done.9 = f32[4,16,4,128]{3,1,2,0:T(8,128)S(1)} async-done(((f32[4,16,4,128]{3,1,2,0:T(8,128)}), f32[4,16,4,128]{3,1,2,0:T(8,128)S(1)}, u32[]{:S(2)}, u32[]{:S(2)}) %all-to-all-start.9) | async-done | bytes 131104 | tf_op jit(solution)/shard_map/all_to_all | solution.py:29
  230.9 0.7 multiply_add_fusion
  231.8 0.9 copy-done.3
  (95 shorter events, 6.1 us)
Async XLA Ops:
  0.6 15.3 %copy-start.1 = (bf16[128,6,256]{2,0,1:T(8,128)(2,1)S(1)}, bf16[128,6,256]{2,0,1:T(8,128)(2,1)}, u32[]{:S(2)}) copy-start(bf16[128,6,256]{2,0,1:T(8,128)(2,1)} %param.5) | copy-start | bytes 1179652
  2.4 23.3 %all-to-all-start = ((f32[64,8,128]{2,1,0:T(8,128)}), f32[64,8,128]{2,1,0:T(8,128)S(1)}, u32[]{:S(2)}, u32[]{:S(2)}) async-start(f32[64,8,128]{2,1,0:T(8,128)} %shard_map.67), calls=%async_computation | async-start | bytes 524288 | tf_op jit(solution)/shard_map/all_to_all | solution.py:29
  26.9 24.0 %all-to-all-start.1 = ((bf16[8,256,128]{2,1,0:T(8,128)(2,1)}), bf16[8,256,128]{2,1,0:T(8,128)(2,1)S(1)}, u32[]{:S(2)}, u32[]{:S(2)}) async-start(bf16[8,256,128]{2,1,0:T(8,128)(2,1)} %broadcast_in_dim.52), calls=%async_computation.1 | async-start | bytes 1048576 | tf_op jit(solution)/shard_map/all_to_all | solution.py:29
  31.7 19.1 %collective-permute-start = (bf16[256,256]{1,0:T(8,128)(2,1)S(1)}, bf16[256,256]{1,0:T(8,128)(2,1)S(1)}, u32[]{:S(2)}, u32[]{:S(2)}) collective-permute-start(bf16[256,256]{1,0:T(8,128)(2,1)S(1)} %fusion.6), channel_id=1, source_target_pairs={{0,64},{64,128},{128,192},{192,0},{1,65},{65,129},{129,193},{193,1... | collective-permute-start | bytes 393224 | tf_op jit(solution)/shard_map/ppermute | solution.py:41
  32.4 18.6 %collective-permute-start.1 = (bf16[256,256]{1,0:T(8,128)(2,1)S(1)}, bf16[256,256]{1,0:T(8,128)(2,1)S(1)}, u32[]{:S(2)}, u32[]{:S(2)}) collective-permute-start(bf16[256,256]{1,0:T(8,128)(2,1)S(1)} %fusion.6), channel_id=1, source_target_pairs={{0,128},{64,192},{128,0},{192,64},{1,129},{65,193},{129,1},{193,65... | collective-permute-start | bytes 393224 | tf_op jit(solution)/shard_map/ppermute | solution.py:41
  35.1 15.9 %collective-permute-start.2 = (bf16[256,256]{1,0:T(8,128)(2,1)S(1)}, bf16[256,256]{1,0:T(8,128)(2,1)S(1)}, u32[]{:S(2)}, u32[]{:S(2)}) collective-permute-start(bf16[256,256]{1,0:T(8,128)(2,1)S(1)} %fusion.6), channel_id=1, source_target_pairs={{0,192},{64,0},{128,64},{192,128},{1,193},{65,1},{129,65},{193,129... | collective-permute-start | bytes 393224 | tf_op jit(solution)/shard_map/ppermute | solution.py:41
  36.4 14.6 %collective-permute-start.6 = (bf16[1,768,256]{2,1,0:T(8,128)(2,1)S(1)}, bf16[1,768,256]{2,1,0:T(8,128)(2,1)S(1)}, u32[]{:S(2)}, u32[]{:S(2)}) collective-permute-start(bf16[1,768,256]{2,1,0:T(8,128)(2,1)S(1)} %bitcast.110), channel_id=1, source_target_pairs={{0,64},{64,0},{128,192},{192,128},{1,65},{65,1},{129,193},{193,129... | collective-permute-start | bytes 1179656 | tf_op jit(solution)/shard_map/ppermute | solution.py:54
  37.1 13.7 %collective-permute-start.4 = (bf16[1,256,128]{2,1,0:T(8,128)(2,1)S(1)}, bf16[1,256,128]{2,1,0:T(8,128)(2,1)S(1)}, u32[]{:S(2)}, u32[]{:S(2)}) collective-permute-start(bf16[1,256,128]{2,1,0:T(8,128)(2,1)S(1)} %bitcast.116), channel_id=1, source_target_pairs={{0,32},{8,40},{16,48},{24,56},{32,0},{40,8},{48,16},{56,24},{1,33}... | collective-permute-start | bytes 196616 | tf_op jit(solution)/shard_map/ppermute | solution.py:54
  50.9 2.0 collective-permute-start.3
  58.6 5.6 %collective-permute-start.5 = (bf16[2,256,128]{2,1,0:T(8,128)(2,1)S(1)}, bf16[2,256,128]{2,1,0:T(8,128)(2,1)S(1)}, u32[]{:S(2)}, u32[]{:S(2)}) collective-permute-start(bf16[2,256,128]{2,1,0:T(8,128)(2,1)S(1)} %pad_maximum_fusion.18), channel_id=1, source_target_pairs={{0,8},{8,0},{16,24},{24,16},{32,40},{40,32},{48,56},{56,48},{1,9},... | collective-permute-start | bytes 393224 | tf_op jit(solution)/shard_map/ppermute | solution.py:54
  60.1 12.5 %all-to-all-start.2 = ((f32[16,24,128]{2,1,0:T(8,128)}), f32[16,24,128]{2,1,0:T(8,128)S(1)}, u32[]{:S(2)}, u32[]{:S(2)}) async-start(f32[16,24,128]{2,1,0:T(8,128)} %get-tuple-element.49), calls=%async_computation.2 | async-start | bytes 393216 | tf_op jit(solution)/shard_map/all_to_all | solution.py:29
  76.9 20.1 %collective-permute-start.7 = (bf16[4,256,128]{2,1,0:T(8,128)(2,1)S(1)}, bf16[4,256,128]{2,1,0:T(8,128)(2,1)S(1)}, u32[]{:S(2)}, u32[]{:S(2)}) collective-permute-start(bf16[4,256,128]{2,1,0:T(8,128)(2,1)S(1)} %pad_maximum_fusion.3), channel_id=1, source_target_pairs={{0,16},{8,24},{16,0},{24,8},{32,48},{40,56},{48,32},{56,40},{1,17}... | collective-permute-start | bytes 786440 | tf_op jit(solution)/shard_map/ppermute | solution.py:54
  78.7 14.1 %all-to-all-start.3 = ((f32[16,8,128]{2,1,0:T(8,128)}), f32[16,8,128]{2,1,0:T(8,128)S(1)}, u32[]{:S(2)}, u32[]{:S(2)}) async-start(f32[16,8,128]{2,1,0:T(8,128)} %get-tuple-element.54), calls=%async_computation.3 | async-start | bytes 131072 | tf_op jit(solution)/shard_map/all_to_all | solution.py:29
  97.1 19.4 %collective-permute-start.9 = (bf16[2,768,256]{2,1,0:T(8,128)(2,1)S(1)}, bf16[2,768,256]{2,1,0:T(8,128)(2,1)S(1)}, u32[]{:S(2)}, u32[]{:S(2)}) collective-permute-start(bf16[2,768,256]{2,1,0:T(8,128)(2,1)S(1)} %pad_maximum_fusion.1), channel_id=1, source_target_pairs={{0,128},{64,192},{128,0},{192,64},{1,129},{65,193},{129,1},{193,65... | collective-permute-start | bytes 2359304 | tf_op jit(solution)/shard_map/ppermute | solution.py:54
  98.4 16.6 %collective-permute-start.8 = (bf16[8,256,128]{2,1,0:T(8,128)(2,1)S(1)}, bf16[8,256,128]{2,1,0:T(8,128)(2,1)S(1)}, u32[]{:S(2)}, u32[]{:S(2)}) collective-permute-start(bf16[8,256,128]{2,1,0:T(8,128)(2,1)S(1)} %pad_maximum_fusion.2.own_ref), channel_id=1, source_target_pairs={{0,4},{4,0},{1,5},{5,1},{2,6},{6,2},{3,7},{7,3},{8,12},{12,8},{9,1... | collective-permute-start | bytes 1572872 | tf_op jit(solution)/shard_map/ppermute | solution.py:37
  98.5 12.3 %all-to-all-start.4 = ((f32[16,16,128]{2,1,0:T(8,128)}), f32[16,16,128]{2,1,0:T(8,128)S(1)}, u32[]{:S(2)}, u32[]{:S(2)}) async-start(f32[16,16,128]{2,1,0:T(8,128)} %shard_map.70), calls=%async_computation.4 | async-start | bytes 262144 | tf_op jit(solution)/shard_map/all_to_all | solution.py:29
  116.6 0.9 copy-start.4
  117.5 11.4 %all-to-all-start.5 = ((f32[16,8,128]{2,1,0:T(8,128)}), f32[16,8,128]{2,1,0:T(8,128)S(1)}, u32[]{:S(2)}, u32[]{:S(2)}) async-start(f32[16,8,128]{2,1,0:T(8,128)} %get-tuple-element.61), calls=%async_computation.5 | async-start | bytes 131072 | tf_op jit(solution)/shard_map/all_to_all | solution.py:29
  127.7 31.9 %copy-start = (bf16[256,2048]{1,0:T(8,128)(2,1)}, bf16[256,2048]{1,0:T(8,128)(2,1)S(1)}, u32[]{:S(2)}) copy-start(bf16[256,2048]{1,0:T(8,128)(2,1)S(1)} %get-tuple-element.75.proto_ref.ps_ref) | copy-start | bytes 3145732
  133.2 12.5 %all-to-all-start.6 = ((f32[16,16,128]{2,1,0:T(8,128)}), f32[16,16,128]{2,1,0:T(8,128)S(1)}, u32[]{:S(2)}, u32[]{:S(2)}) async-start(f32[16,16,128]{2,1,0:T(8,128)} %shard_map.72), calls=%async_computation.6 | async-start | bytes 262144 | tf_op jit(solution)/shard_map/all_to_all | solution.py:29
  150.0 15.8 %all-to-all-start.7 = ((f32[16,32,128]{2,1,0:T(8,128)}), f32[16,32,128]{2,1,0:T(8,128)S(1)}, u32[]{:S(2)}, u32[]{:S(2)}) async-start(f32[16,32,128]{2,1,0:T(8,128)} %get-tuple-element.72), calls=%async_computation.7 | async-start | bytes 524288 | tf_op jit(solution)/shard_map/all_to_all | solution.py:29
  165.7 0.7 copy-start.8
  183.6 5.5 %collective-permute-start.10 = (f32[2064,128]{1,0:T(8,128)}, f32[2064,128]{1,0:T(8,128)}, u32[]{:S(2)}, u32[]{:S(2)}) collective-permute-start(f32[2064,128]{1,0:T(8,128)} %get-tuple-element.77), channel_id=1, source_target_pairs={{0,4},{4,0},{1,5},{5,1},{2,6},{6,2},{3,7},{7,3},{8,12},{12,8},{9,1... | collective-permute-start | bytes 3170312 | tf_op jit(solution)/shard_map/ppermute | solution.py:37
  185.2 3.9 %copy-start.2 = (f32[2064,128]{1,0:T(8,128)S(1)}, f32[2064,128]{1,0:T(8,128)}, u32[]{:S(2)}) copy-start(f32[2064,128]{1,0:T(8,128)} %get-tuple-element.76) | copy-start | bytes 3170308
  185.2 28.8 %all-to-all-start.8 = ((f16[16,192,256]{2,1,0:T(8,128)(2,1)}), f16[16,192,256]{2,1,0:T(8,128)(2,1)S(1)}, u32[]{:S(2)}, u32[]{:S(2)}) async-start(f16[16,192,256]{2,1,0:T(8,128)(2,1)} %bitcast.107), calls=%async_computation.8 | async-start | bytes 3145728 | tf_op jit(solution)/shard_map/all_to_all | solution.py:29
  190.7 11.8 %collective-permute-start.11 = (f16[288,128]{1,0:T(8,128)(2,1)S(1)}, f16[288,128]{1,0:T(8,128)(2,1)S(1)}, u32[]{:S(2)}, u32[]{:S(2)}) collective-permute-start(f16[288,128]{1,0:T(8,128)(2,1)S(1)} %get-tuple-element.107), channel_id=1, source_target_pairs={{0,8},{8,16},{16,24},{24,32},{32,40},{40,48},{48,56},{56,0},{1,9},... | collective-permute-start | bytes 221192 | tf_op jit(solution)/shard_map/ppermute | solution.py:41
  191.5 11.1 %collective-permute-start.12 = (f16[288,128]{1,0:T(8,128)(2,1)S(1)}, f16[288,128]{1,0:T(8,128)(2,1)S(1)}, u32[]{:S(2)}, u32[]{:S(2)}) collective-permute-start(f16[288,128]{1,0:T(8,128)(2,1)S(1)} %get-tuple-element.108), channel_id=1, source_target_pairs={{0,16},{8,24},{16,32},{24,40},{32,48},{40,56},{48,0},{56,8},{1,17}... | collective-permute-start | bytes 221192 | tf_op jit(solution)/shard_map/ppermute | solution.py:41
  192.5 14.9 %collective-permute-start.13 = (f16[288,128]{1,0:T(8,128)(2,1)S(1)}, f16[288,128]{1,0:T(8,128)(2,1)S(1)}, u32[]{:S(2)}, u32[]{:S(2)}) collective-permute-start(f16[288,128]{1,0:T(8,128)(2,1)S(1)} %get-tuple-element.109), channel_id=1, source_target_pairs={{0,24},{8,32},{16,40},{24,48},{32,56},{40,0},{48,8},{56,16},{1,25}... | collective-permute-start | bytes 221192 | tf_op jit(solution)/shard_map/ppermute | solution.py:41
  194.9 12.5 %collective-permute-start.14 = (f16[288,128]{1,0:T(8,128)(2,1)S(1)}, f16[288,128]{1,0:T(8,128)(2,1)S(1)}, u32[]{:S(2)}, u32[]{:S(2)}) collective-permute-start(f16[288,128]{1,0:T(8,128)(2,1)S(1)} %get-tuple-element.110), channel_id=1, source_target_pairs={{0,32},{8,40},{16,48},{24,56},{32,0},{40,8},{48,16},{56,24},{1,33}... | collective-permute-start | bytes 221192 | tf_op jit(solution)/shard_map/ppermute | solution.py:41
  198.2 12.9 %collective-permute-start.15 = (f16[288,128]{1,0:T(8,128)(2,1)S(1)}, f16[288,128]{1,0:T(8,128)(2,1)S(1)}, u32[]{:S(2)}, u32[]{:S(2)}) collective-permute-start(f16[288,128]{1,0:T(8,128)(2,1)S(1)} %get-tuple-element.111), channel_id=1, source_target_pairs={{0,40},{8,48},{16,56},{24,0},{32,8},{40,16},{48,24},{56,32},{1,41}... | collective-permute-start | bytes 221192 | tf_op jit(solution)/shard_map/ppermute | solution.py:41
  202.5 8.6 %collective-permute-start.16 = (f16[288,128]{1,0:T(8,128)(2,1)S(1)}, f16[288,128]{1,0:T(8,128)(2,1)S(1)}, u32[]{:S(2)}, u32[]{:S(2)}) collective-permute-start(f16[288,128]{1,0:T(8,128)(2,1)S(1)} %get-tuple-element.112), channel_id=1, source_target_pairs={{0,48},{8,56},{16,0},{24,8},{32,16},{40,24},{48,32},{56,40},{1,49}... | collective-permute-start | bytes 221192 | tf_op jit(solution)/shard_map/ppermute | solution.py:41
  202.6 10.3 %collective-permute-start.17 = (f16[288,128]{1,0:T(8,128)(2,1)S(1)}, f16[288,128]{1,0:T(8,128)(2,1)S(1)}, u32[]{:S(2)}, u32[]{:S(2)}) collective-permute-start(f16[288,128]{1,0:T(8,128)(2,1)S(1)} %pad_maximum_fusion.4), channel_id=1, source_target_pairs={{0,56},{8,0},{16,8},{24,16},{32,24},{40,32},{48,40},{56,48},{1,57}... | collective-permute-start | bytes 221192 | tf_op jit(solution)/shard_map/ppermute | solution.py:41
  214.2 16.7 %copy-start.6 = (f32[4,8192]{1,0:T(4,128)S(1)}, f32[4,8192]{1,0:T(4,128)}, u32[]{:S(2)}) copy-start(f32[4,8192]{1,0:T(4,128)} %t_ref.1) | copy-start | bytes 393220
  214.2 16.7 %copy-start.7 = (f32[4,8192]{1,0:T(4,128)S(1)}, f32[4,8192]{1,0:T(4,128)}, u32[]{:S(2)}) copy-start(f32[4,8192]{1,0:T(4,128)} %s_ref.1) | copy-start | bytes 393220
  214.9 16.7 %collective-permute-start.18 = (f32[32,6,256]{2,0,1:T(8,128)S(1)}, f32[32,6,256]{2,0,1:T(8,128)S(1)}, u32[]{:S(2)}, u32[]{:S(2)}) collective-permute-start(f32[32,6,256]{2,0,1:T(8,128)S(1)} %bitcast.117), channel_id=1, source_target_pairs={{0,1},{1,2},{2,3},{3,0},{4,5},{5,6},{6,7},{7,4},{8,9},{9,10},{10,1... | collective-permute-start | bytes 589832 | tf_op jit(solution)/shard_map/ppermute | solution.py:41
  216.2 15.4 %collective-permute-start.19 = (f32[32,6,256]{2,0,1:T(8,128)S(1)}, f32[32,6,256]{2,0,1:T(8,128)S(1)}, u32[]{:S(2)}, u32[]{:S(2)}) collective-permute-start(f32[32,6,256]{2,0,1:T(8,128)S(1)} %bitcast.118), channel_id=1, source_target_pairs={{0,2},{1,3},{2,0},{3,1},{4,6},{5,7},{6,4},{7,5},{8,10},{9,11},{10,... | collective-permute-start | bytes 589832 | tf_op jit(solution)/shard_map/ppermute | solution.py:41
  218.9 12.8 %collective-permute-start.20 = (f32[32,6,256]{2,0,1:T(8,128)S(1)}, f32[32,6,256]{2,0,1:T(8,128)S(1)}, u32[]{:S(2)}, u32[]{:S(2)}) collective-permute-start(f32[32,6,256]{2,0,1:T(8,128)S(1)} %bitcast.119), channel_id=1, source_target_pairs={{0,3},{1,0},{2,1},{3,2},{4,7},{5,4},{6,5},{7,6},{8,11},{9,8},{10,9... | collective-permute-start | bytes 589832 | tf_op jit(solution)/shard_map/ppermute | solution.py:41
  220.4 10.3 %all-to-all-start.9 = ((f32[4,16,4,128]{3,1,2,0:T(8,128)}), f32[4,16,4,128]{3,1,2,0:T(8,128)S(1)}, u32[]{:S(2)}, u32[]{:S(2)}) async-start(f32[4,16,4,128]{3,1,2,0:T(8,128)} %bitcast.34), calls=%async_computation.9 | async-start | bytes 262144 | tf_op jit(solution)/shard_map/all_to_all | solution.py:29
  230.9 0.9 copy-start.5
  231.7 0.9 copy-start.3

commit v4 on v3

--- a/solution.py
+++ b/solution.py
@@ -1,5 +1,3 @@
-import functools
-
 import jax
 import jax.numpy as jnp
 from jax import lax
@@ -111,7 +109,7 @@
 def energy_kernel(place_ref, norm_ref, t_ref, own_ref, other_ref, e_ref, out_ref, proto_ref, acc_ref, held_ref, sem_ref):
     join_columns(place_ref, own_ref, other_ref, proto_ref)
     width = e_ref.shape[1]
-    tile = 256
+    tile = 512
 
     def copy(j):
         at = pl.ds(pl.multiple_of(j * tile, tile), tile)
@@ -120,13 +118,13 @@
     def columns(j, _):
         at = pl.ds(pl.multiple_of(j * tile, tile), tile)
         dots = jnp.dot(t_ref[...], proto_ref[:, at], preferred_element_type=jnp.float32)
-        energy = jnp.exp(dots * (1.0 / TEMP_T))
+        energy = jnp.exp2(dots * (LOG2E / TEMP_T))
         held_ref[:, at] = energy
         acc_ref[:, at] = fold(energy, 8)
         copy(j).start()
         return 0
 
-    lax.fori_loop(0, width // tile, columns, 0)
+    lax.fori_loop(0, width // tile, columns, 0, unroll=True)
     to_all(acc_ref[...], out_ref, out_ref.shape[0])
     for p in range(out_ref.shape[0]):
         out_ref[p, width // LANES : width // LANES + 1] = norm_ref[...]
@@ -220,8 +218,8 @@
 
 
 def slope_kernel(
-    factor, place_ref, got_ref, recip_ref, s_ref, st_ref, ps_ref, psp_ref, e_ref,
-    ug_ref, keep_ref, give_ref, slope_ref, total_ref, lines_ref, down_ref,
+    place_ref, lines_ref, recip_ref, s_ref, st_ref, ps_ref, psp_ref, e_ref,
+    ug_ref, keep_ref, give_ref, slope_ref, total_ref, down_ref,
 ):
     rows = st_ref.shape[2]
     width = ps_ref.shape[1]
@@ -232,7 +230,6 @@
 
     @pl.when(g == 0)
     def _():
-        lines_ref[...] = factor / jnp.sum(got_ref[...], axis=0)
         total_ref[...] = jnp.zeros_like(total_ref)
         slope_ref[1] = jnp.zeros_like(slope_ref[1])
 
@@ -341,7 +338,7 @@
             pltpu.VMEM((bottleneck, width), bf16),
             pltpu.VMEM((8, width), f32),
             pltpu.VMEM((NX * t_rows, width), f32),
-            pltpu.SemaphoreType.DMA((width // 256,)),
+            pltpu.SemaphoreType.DMA((width // 512,)),
         ],
         [HBM, VMEM],
         limit=24,
@@ -427,11 +424,11 @@
     s_o = jnp.einsum("pb,grb->gpr", ordered, s_all, preferred_element_type=f32).astype(bf16)
     size = bottleneck * width // (NC * NZ * LANES)
     unit_part, keep, give = call(
-        functools.partial(slope_kernel, total_k / 16.0),
+        slope_kernel,
         [pltpu.VMEM((NX, NY, s_rows // NY, bottleneck), f32)] + [pltpu.HBM((NZ * size + width // LANES, LANES), f32)] * NC,
         [
             SMEM,
-            whole(NX * NY, NX * (2 + CROPS), LANES),
+            whole(NX * (2 + CROPS), LANES),
             whole(1, width),
             pl.BlockSpec((1, s_rows, bottleneck), lambda g: (jnp.minimum(g, NX - 1), 0, 0)),
             pl.BlockSpec((1, bottleneck, s_rows), lambda g: (jnp.maximum(g - 1, 0), 0, 0)),
@@ -442,7 +439,6 @@
         [
             pltpu.VMEM((2, s_rows, width), bf16),
             pltpu.VMEM((bottleneck, width), f32),
-            pltpu.VMEM((NX * (2 + CROPS), LANES), f32),
             pltpu.VMEM((2 + CROPS, LANES, LANES), f32),
         ],
         [
@@ -457,7 +453,7 @@
         exps=exact * 3,
     )(
         place,
-        pltpu.with_memory_space_constraint(got, pltpu.HBM),
+        total_k / 16.0 / jnp.sum(got, axis=0),
         recip,
         *(pltpu.with_memory_space_constraint(v, pltpu.HBM) for v in (s_all, s_o, proto_s, proto_o)),
         energy,

time: 234 us -> 232 us (level)
  transfers between devices with their start and end apart: 31 -> 31, of which waited for: 16 -> 15; matrix products, arithmetic and copies ran while one was open for 8% -> 8% of each run, Pallas kernels for 7% -> 7%
where the time goes in v4:
time: 232 us; the launch traced here: 231 us
  starting transfers between devices  88.2 us (38%)
  waiting for transfers between devices  67.3 us (29%)
  Pallas kernels  52.6 us (23%)
  other arithmetic  12.4 us (5%)
  local copies, waits for them, and re-layouts  4.66 us (2%)
  matrix products  4.64 us (2%)
    all_to_all x10, starting transfers between devices, swap(): return lax.all_to_all(v, axes, 0, 0)  55.1 us
    all_to_all x10, waiting for transfers between devices, swap(): return lax.all_to_all(v, axes, 0, 0)  46.7 us
    ppermute x13, starting transfers between devices, shifted(): return lax.ppermute(v, axis, [(i, (i + k) % n) for i in range(n)])  23.2 us
    pallas_call x1, Pallas kernels, local(): call(slope_kernel, [pltpu.VMEM((NX, NY, s_rows // NY, bottleneck), f32)]...  17 us
    pallas_call x3, Pallas kernels, by_row(): call(by_row_kernel, [shape((1, width), f32), shape((NX * NY, lines, LANES...  12.9 us
    ppermute x5, waiting for transfers between devices, exchanged(): return (v, lax.ppermute(v, axis, [(i, i ^ step) for i in range(n)]))  10.8 us
    ppermute x5, starting transfers between devices, exchanged(): return (v, lax.ppermute(v, axis, [(i, i ^ step) for i in range(n)]))  9.82 us
    pallas_call x2, Pallas kernels, by_column(): call(by_column_kernel, [shape((NZ * NC, width // LANES, LANES), f32)], [V...  8.58 us
  transfers between devices with their start and end apart: 31, of which 15 were waited for; matrix products, arithmetic and copies ran while one was open for 8% of the time, Pallas kernels for 7%

profile of v4, /device:TPU:32, one launch (start us, length us, event | category | flops | bytes accessed | tf_op | source)
XLA Modules:
  0.0 231.2 jit_solution(3543665063029788363)
XLA Ops:
  0.6 1.8 shard_map.67
  2.4 11.6 %all-to-all-start = ((f32[64,8,128]{2,1,0:T(8,128)}), f32[64,8,128]{2,1,0:T(8,128)S(1)}, u32[]{:S(2)}, u32[]{:S(2)}) async-start(f32[64,8,128]{2,1,0:T(8,128)} %shard_map.67), calls=%async_computation | async-start | bytes 524288 | tf_op jit(solution)/shard_map/all_to_all | solution.py:27
  14.0 0.9 copy_convert_fusion
  14.9 1.0 multiply_reduce_fusion.1
  16.9 8.9 %all-to-all-done = f32[64,8,128]{2,1,0:T(8,128)S(1)} async-done(((f32[64,8,128]{2,1,0:T(8,128)}), f32[64,8,128]{2,1,0:T(8,128)S(1)}, u32[]{:S(2)}, u32[]{:S(2)}) %all-to-all-start) | async-done | bytes 262176 | tf_op jit(solution)/shard_map/all_to_all | solution.py:27
  26.0 0.9 broadcast_in_dim.52
  26.9 4.8 %all-to-all-start.1 = ((bf16[8,256,128]{2,1,0:T(8,128)(2,1)}), bf16[8,256,128]{2,1,0:T(8,128)(2,1)S(1)}, u32[]{:S(2)}, u32[]{:S(2)}) async-start(bf16[8,256,128]{2,1,0:T(8,128)(2,1)} %broadcast_in_dim.52), calls=%async_computation.1 | async-start | bytes 1048576 | tf_op jit(solution)/shard_map/all_to_all | solution.py:27
  32.4 2.7 %collective-permute-start.1 = (bf16[256,256]{1,0:T(8,128)(2,1)S(1)}, bf16[256,256]{1,0:T(8,128)(2,1)S(1)}, u32[]{:S(2)}, u32[]{:S(2)}) collective-permute-start(bf16[256,256]{1,0:T(8,128)(2,1)S(1)} %fusion.6), channel_id=1, source_target_pairs={{0,128},{64,192},{128,0},{192,64},{1,129},{65,193},{129,1},{193,65... | collective-permute-start | bytes 393224 | tf_op jit(solution)/shard_map/ppermute | solution.py:39
  35.1 1.4 collective-permute-start.2
  37.1 4.5 %collective-permute-start.4 = (bf16[1,256,128]{2,1,0:T(8,128)(2,1)S(1)}, bf16[1,256,128]{2,1,0:T(8,128)(2,1)S(1)}, u32[]{:S(2)}, u32[]{:S(2)}) collective-permute-start(bf16[1,256,128]{2,1,0:T(8,128)(2,1)S(1)} %bitcast.116), channel_id=1, source_target_pairs={{0,32},{8,40},{16,48},{24,56},{32,0},{40,8},{48,16},{56,24},{1,33}... | collective-permute-start | bytes 196616 | tf_op jit(solution)/shard_map/ppermute | solution.py:52
  41.7 9.1 %collective-permute-done.4 = bf16[1,256,128]{2,1,0:T(8,128)(2,1)S(1)} collective-permute-done((bf16[1,256,128]{2,1,0:T(8,128)(2,1)S(1)}, bf16[1,256,128]{2,1,0:T(8,128)(2,1)S(1)}, u32[]{:S(2)}, u32[]{:S(2)}) %collective-permute-start.4) | collective-permute-done | bytes 65568 | tf_op jit(solution)/shard_map/ppermute | solution.py:52
  51.1 1.7 collective-permute-done.3.other_ref
  52.9 5.2 %shard_map.68 = (f32[1024,2048]{1,0:T(8,128)}, f32[16,24,128]{2,1,0:T(8,128)}) custom-call(s32[2]{0:T(128)S(1)} %pad_add_fusion.place_ref, f32[1,128]{1,0:T(1,128)S(1)} %get-tuple-element.116.norm_ref, bf16[1024,256]{1,0:T(8,128)(2,1)S(1)} %bitcast.106, bf16[8,256,128]{2,1,0:T(8,128)(2,1)S(1)} %all-to-all-done.1.own_ref, ...), custom_call_target="tpu_custom_call" | custom-call | flops 1073741824 | tf_op jit(solution)/shard_map/pallas_call | solution.py:333
  58.0 1.6 collective-permute-start.5
  59.6 3.9 %all-to-all-start.2 = ((f32[16,24,128]{2,1,0:T(8,128)}), f32[16,24,128]{2,1,0:T(8,128)S(1)}, u32[]{:S(2)}, u32[]{:S(2)}) async-start(f32[16,24,128]{2,1,0:T(8,128)} %get-tuple-element.49), calls=%async_computation.2 | async-start | bytes 393216 | tf_op jit(solution)/shard_map/all_to_all | solution.py:27
  63.7 8.3 %all-to-all-done.2.got_ref = f32[16,24,128]{2,1,0:T(8,128)S(1)} async-done(((f32[16,24,128]{2,1,0:T(8,128)}), f32[16,24,128]{2,1,0:T(8,128)S(1)}, u32[]{:S(2)}, u32[]{:S(2)}) %all-to-all-start.2) | async-done | bytes 196640 | tf_op jit(solution)/shard_map/all_to_all | solution.py:27
  72.1 4.3 %shard_map.69 = (f32[1,2048]{1,0:T(1,128)}, f32[16,8,128]{2,1,0:T(8,128)}) custom-call(f32[16,24,128]{2,1,0:T(8,128)S(1)} %all-to-all-done.2.got_ref, f32[1024,2048]{1,0:T(8,128)} %get-tuple-element.50.e_ref), custom_call_target="tpu_custom_call" | custom-call | flops 4194304 | bytes 8388608 | tf_op jit(solution)/shard_map/pallas_call | solution.py:360
  76.3 1.8 collective-permute-start.7
  78.1 6.4 %all-to-all-start.3 = ((f32[16,8,128]{2,1,0:T(8,128)}), f32[16,8,128]{2,1,0:T(8,128)S(1)}, u32[]{:S(2)}, u32[]{:S(2)}) async-start(f32[16,8,128]{2,1,0:T(8,128)} %get-tuple-element.54), calls=%async_computation.3 | async-start | bytes 131072 | tf_op jit(solution)/shard_map/all_to_all | solution.py:27
  84.5 7.6 %all-to-all-done.3.got_ref = f32[16,8,128]{2,1,0:T(8,128)S(1)} async-done(((f32[16,8,128]{2,1,0:T(8,128)}), f32[16,8,128]{2,1,0:T(8,128)S(1)}, u32[]{:S(2)}, u32[]{:S(2)}) %all-to-all-start.3) | async-done | bytes 65568 | tf_op jit(solution)/shard_map/all_to_all | solution.py:27
  92.2 4.3 %shard_map.70 = f32[16,16,128]{2,1,0:T(8,128)} custom-call(f32[16,8,128]{2,1,0:T(8,128)S(1)} %all-to-all-done.3.got_ref, f32[1024,2048]{1,0:T(8,128)} %get-tuple-element.50.e_ref), custom_call_target="tpu_custom_call" | custom-call | flops 4194304 | bytes 8388608 | tf_op jit(solution)/shard_map/pallas_call | solution.py:371
  96.6 1.3 collective-permute-start.9
  97.9 4.9 %all-to-all-start.4 = ((f32[16,16,128]{2,1,0:T(8,128)}), f32[16,16,128]{2,1,0:T(8,128)S(1)}, u32[]{:S(2)}, u32[]{:S(2)}) async-start(f32[16,16,128]{2,1,0:T(8,128)} %shard_map.70), calls=%async_computation.4 | async-start | bytes 262144 | tf_op jit(solution)/shard_map/all_to_all | solution.py:27
  102.8 7.4 %all-to-all-done.4.got_ref = f32[16,16,128]{2,1,0:T(8,128)S(1)} async-done(((f32[16,16,128]{2,1,0:T(8,128)}), f32[16,16,128]{2,1,0:T(8,128)S(1)}, u32[]{:S(2)}, u32[]{:S(2)}) %all-to-all-start.4) | async-done | bytes 131104 | tf_op jit(solution)/shard_map/all_to_all | solution.py:27
  110.2 4.3 %shard_map.71 = (f32[1,2048]{1,0:T(1,128)}, f32[16,8,128]{2,1,0:T(8,128)}) custom-call(f32[16,16,128]{2,1,0:T(8,128)S(1)} %all-to-all-done.4.got_ref, f32[1024,2048]{1,0:T(8,128)} %get-tuple-element.50.e_ref), custom_call_target="tpu_custom_call" | custom-call | flops 4194304 | bytes 8388608 | tf_op jit(solution)/shard_map/pallas_call | solution.py:360
  114.5 1.6 collective-permute-done.9
  116.0 0.9 copy-done.4
  116.9 3.7 %all-to-all-start.5 = ((f32[16,8,128]{2,1,0:T(8,128)}), f32[16,8,128]{2,1,0:T(8,128)S(1)}, u32[]{:S(2)}, u32[]{:S(2)}) async-start(f32[16,8,128]{2,1,0:T(8,128)} %get-tuple-element.61), calls=%async_computation.5 | async-start | bytes 131072 | tf_op jit(solution)/shard_map/all_to_all | solution.py:27
  120.7 1.2 broadcast_select_fusion
  121.9 1.3 pad_maximum_fusion.s_ref
  123.2 4.0 %shard_map.73 = (bf16[256,2048]{1,0:T(8,128)(2,1)S(1)}, f32[12,128]{1,0:T(8,128)S(1)}) custom-call(s32[2]{0:T(128)S(1)} %pad_add_fusion.place_ref, bf16[1536,256]{1,0:T(8,128)(2,1)S(1)} %bitcast.104, bf16[8,256,128]{2,1,0:T(8,128)(2,1)S(1)} %pad_maximum_fusion.2.own_ref, bf16[8,256,128]{2,1,0:T(8,128)(2,1)S(1)} %collective-permute-done.8.other_ref), custom_call_target="tpu_custom_call" | custom-call | flops 1610612736 | tf_op jit(solution)/shard_map/pallas_call | solution.py:404
  127.2 1.1 all-to-all-done.5.got_ref
  128.3 4.3 %shard_map.72 = f32[16,16,128]{2,1,0:T(8,128)} custom-call(f32[16,8,128]{2,1,0:T(8,128)S(1)} %all-to-all-done.5.got_ref, f32[1024,2048]{1,0:T(8,128)} %get-tuple-element.50.e_ref), custom_call_target="tpu_custom_call" | custom-call | flops 4194304 | bytes 8388608 | tf_op jit(solution)/shard_map/pallas_call | solution.py:371
  132.6 4.9 %all-to-all-start.6 = ((f32[16,16,128]{2,1,0:T(8,128)}), f32[16,16,128]{2,1,0:T(8,128)S(1)}, u32[]{:S(2)}, u32[]{:S(2)}) async-start(f32[16,16,128]{2,1,0:T(8,128)} %shard_map.72), calls=%async_computation.6 | async-start | bytes 262144 | tf_op jit(solution)/shard_map/all_to_all | solution.py:27
  137.6 1.2 slice.114
  138.8 3.2 %shard_map.74.refs_1_ = f32[12,128]{1,0:T(8,128)S(1)} custom-call(bf16[1536,256]{1,0:T(8,128)(2,1)S(1)} %bitcast.105, bf16[256,2048]{1,0:T(8,128)(2,1)S(1)} %get-tuple-element.75.proto_ref.ps_ref), custom_call_target="tpu_custom_call" | custom-call | flops 1610612736 | tf_op jit(solution)/shard_map/pallas_call | solution.py:414
  142.0 2.9 %all-to-all-done.6.got_ref = f32[16,16,128]{2,1,0:T(8,128)S(1)} async-done(((f32[16,16,128]{2,1,0:T(8,128)}), f32[16,16,128]{2,1,0:T(8,128)S(1)}, u32[]{:S(2)}, u32[]{:S(2)}) %all-to-all-start.6) | async-done | bytes 131104 | tf_op jit(solution)/shard_map/all_to_all | solution.py:27
  144.9 4.3 %shard_map.75 = (f32[1,2048]{1,0:T(1,128)S(1)}, f32[16,32,128]{2,1,0:T(8,128)}) custom-call(f32[16,16,128]{2,1,0:T(8,128)S(1)} %all-to-all-done.6.got_ref, f32[1024,2048]{1,0:T(8,128)} %get-tuple-element.50.e_ref, f32[12,128]{1,0:T(8,128)S(1)} %get-tuple-element.68.refs_0_, f32[12,128]{1,0:T(8,128)S(1)} %shard_map.74.refs_1_), custom_call_target="tpu_custom_call" | custom-call | flops 4194304 | bytes 8388608 | tf_op jit(solution)/shard_map/pallas_call | solution.py:360
  149.2 6.5 %all-to-all-start.7 = ((f32[16,32,128]{2,1,0:T(8,128)}), f32[16,32,128]{2,1,0:T(8,128)S(1)}, u32[]{:S(2)}, u32[]{:S(2)}) async-start(f32[16,32,128]{2,1,0:T(8,128)} %get-tuple-element.72), calls=%async_computation.7 | async-start | bytes 524288 | tf_op jit(solution)/shard_map/all_to_all | solution.py:27
  155.7 3.2 %fusion.1.st_ref = bf16[4,256,768]{2,1,0:T(8,128)(2,1)} fusion(bf16[4,768,256]{2,1,0:T(8,128)(2,1)} %pad_maximum_fusion.s_ref, s32[256]{0:T(256)S(1)} %reshape.210), kind=kOutput, calls=%fused_computation.6 | convolution fusion | flops 403505152 | bytes 3146752 | tf_op jit(solution)/shard_map/pb,grb->gpr/dot_general | solution.py:424
  158.9 1.5 convolution_convert_fusion.psp_ref
  160.4 4.7 %all-to-all-done.7 = f32[16,32,128]{2,1,0:T(8,128)S(1)} async-done(((f32[16,32,128]{2,1,0:T(8,128)}), f32[16,32,128]{2,1,0:T(8,128)S(1)}, u32[]{:S(2)}, u32[]{:S(2)}) %all-to-all-start.7) | async-done | bytes 262176 | tf_op jit(solution)/shard_map/all_to_all | solution.py:27
  165.1 17.0 %shard_map.76 = (f32[4,4,192,256]{3,2,1,0:T(8,128)S(1)}, f32[2064,128]{1,0:T(8,128)}, f32[2064,128]{1,0:T(8,128)}) custom-call(s32[2]{0:T(128)S(1)} %pad_add_fusion.place_ref, f32[32,128]{1,0:T(8,128)S(1)} %broadcast_divide_fusion.lines_ref, f32[1,2048]{1,0:T(1,128)S(1)} %get-tuple-element.73.recip_ref, bf16[4,768,256]{2,1,0:T(8,128)(2,1)} %pad_maximum_fusion.s_ref, ...), custom_call_target="tpu_custom_call" | custom-call | flops 9663676416 | bytes 8388608 | tf_op jit(solution)/shard_map/pallas_call | solution.py:426
  182.1 1.6 multiply_convert_fusion
  183.7 4.1 %all-to-all-start.8 = ((f16[16,192,256]{2,1,0:T(8,128)(2,1)}), f16[16,192,256]{2,1,0:T(8,128)(2,1)S(1)}, u32[]{:S(2)}, u32[]{:S(2)}) async-start(f16[16,192,256]{2,1,0:T(8,128)(2,1)} %bitcast.107), calls=%async_computation.8 | async-start | bytes 3145728 | tf_op jit(solution)/shard_map/all_to_all | solution.py:27
  187.8 1.4 fusion.34
  189.5 0.8 collective-permute-start.11
  190.2 1.0 collective-permute-start.12
  191.3 2.3 %collective-permute-start.13 = (f16[288,128]{1,0:T(8,128)(2,1)S(1)}, f16[288,128]{1,0:T(8,128)(2,1)S(1)}, u32[]{:S(2)}, u32[]{:S(2)}) collective-permute-start(f16[288,128]{1,0:T(8,128)(2,1)S(1)} %get-tuple-element.109), channel_id=1, source_target_pairs={{0,24},{8,32},{16,40},{24,48},{32,56},{40,0},{48,8},{56,16},{1,25}... | collective-permute-start | bytes 221192 | tf_op jit(solution)/shard_map/ppermute | solution.py:39
  193.6 3.3 %collective-permute-start.14 = (f16[288,128]{1,0:T(8,128)(2,1)S(1)}, f16[288,128]{1,0:T(8,128)(2,1)S(1)}, u32[]{:S(2)}, u32[]{:S(2)}) collective-permute-start(f16[288,128]{1,0:T(8,128)(2,1)S(1)} %get-tuple-element.110), channel_id=1, source_target_pairs={{0,32},{8,40},{16,48},{24,56},{32,0},{40,8},{48,16},{56,24},{1,33}... | collective-permute-start | bytes 221192 | tf_op jit(solution)/shard_map/ppermute | solution.py:39
  196.9 4.3 %collective-permute-start.15 = (f16[288,128]{1,0:T(8,128)(2,1)S(1)}, f16[288,128]{1,0:T(8,128)(2,1)S(1)}, u32[]{:S(2)}, u32[]{:S(2)}) collective-permute-start(f16[288,128]{1,0:T(8,128)(2,1)S(1)} %get-tuple-element.111), channel_id=1, source_target_pairs={{0,40},{8,48},{16,56},{24,0},{32,8},{40,16},{48,24},{56,32},{1,41}... | collective-permute-start | bytes 221192 | tf_op jit(solution)/shard_map/ppermute | solution.py:39
  201.3 1.3 collective-permute-start.17
  202.6 0.8 convert_bitcast_fusion.1
  203.6 2.6 %collective-permute-done.13 = f16[288,128]{1,0:T(8,128)(2,1)S(1)} collective-permute-done((f16[288,128]{1,0:T(8,128)(2,1)S(1)}, f16[288,128]{1,0:T(8,128)(2,1)S(1)}, u32[]{:S(2)}, u32[]{:S(2)}) %collective-permute-start.13) | collective-permute-done | bytes 73760 | tf_op jit(solution)/shard_map/ppermute | solution.py:39
  206.2 3.4 %collective-permute-done.15 = f16[288,128]{1,0:T(8,128)(2,1)S(1)} collective-permute-done((f16[288,128]{1,0:T(8,128)(2,1)S(1)}, f16[288,128]{1,0:T(8,128)(2,1)S(1)}, u32[]{:S(2)}, u32[]{:S(2)}) %collective-permute-start.15) | collective-permute-done | bytes 73760 | tf_op jit(solution)/shard_map/ppermute | solution.py:39
  209.7 2.0 collective-permute-done.17
  212.7 0.7 fusion.4
  213.5 1.3 collective-permute-start.18
  214.8 2.7 %collective-permute-start.19 = (f32[32,6,256]{2,0,1:T(8,128)S(1)}, f32[32,6,256]{2,0,1:T(8,128)S(1)}, u32[]{:S(2)}, u32[]{:S(2)}) collective-permute-start(f32[32,6,256]{2,0,1:T(8,128)S(1)} %bitcast.118), channel_id=1, source_target_pairs={{0,2},{1,3},{2,0},{3,1},{4,6},{5,7},{6,4},{7,5},{8,10},{9,11},{10,... | collective-permute-start | bytes 589832 | tf_op jit(solution)/shard_map/ppermute | solution.py:39
  217.4 1.5 collective-permute-start.20
  218.9 4.3 %all-to-all-start.9 = ((f32[4,16,4,128]{3,1,2,0:T(8,128)}), f32[4,16,4,128]{3,1,2,0:T(8,128)S(1)}, u32[]{:S(2)}, u32[]{:S(2)}) async-start(f32[4,16,4,128]{3,1,2,0:T(8,128)} %bitcast.34), calls=%async_computation.9 | async-start | bytes 262144 | tf_op jit(solution)/shard_map/all_to_all | solution.py:27
  223.3 5.9 %all-to-all-done.9 = f32[4,16,4,128]{3,1,2,0:T(8,128)S(1)} async-done(((f32[4,16,4,128]{3,1,2,0:T(8,128)}), f32[4,16,4,128]{3,1,2,0:T(8,128)S(1)}, u32[]{:S(2)}, u32[]{:S(2)}) %all-to-all-start.9) | async-done | bytes 131104 | tf_op jit(solution)/shard_map/all_to_all | solution.py:27
  229.4 0.7 multiply_add_fusion
  230.3 0.9 copy-done.3
  (95 shorter events, 5.2 us)
Async XLA Ops:
  0.6 15.3 %copy-start.1 = (bf16[128,6,256]{2,0,1:T(8,128)(2,1)S(1)}, bf16[128,6,256]{2,0,1:T(8,128)(2,1)}, u32[]{:S(2)}) copy-start(bf16[128,6,256]{2,0,1:T(8,128)(2,1)} %param.5) | copy-start | bytes 1179652
  2.4 23.3 %all-to-all-start = ((f32[64,8,128]{2,1,0:T(8,128)}), f32[64,8,128]{2,1,0:T(8,128)S(1)}, u32[]{:S(2)}, u32[]{:S(2)}) async-start(f32[64,8,128]{2,1,0:T(8,128)} %shard_map.67), calls=%async_computation | async-start | bytes 524288 | tf_op jit(solution)/shard_map/all_to_all | solution.py:27
  26.9 24.0 %all-to-all-start.1 = ((bf16[8,256,128]{2,1,0:T(8,128)(2,1)}), bf16[8,256,128]{2,1,0:T(8,128)(2,1)S(1)}, u32[]{:S(2)}, u32[]{:S(2)}) async-start(bf16[8,256,128]{2,1,0:T(8,128)(2,1)} %broadcast_in_dim.52), calls=%async_computation.1 | async-start | bytes 1048576 | tf_op jit(solution)/shard_map/all_to_all | solution.py:27
  31.7 19.1 %collective-permute-start = (bf16[256,256]{1,0:T(8,128)(2,1)S(1)}, bf16[256,256]{1,0:T(8,128)(2,1)S(1)}, u32[]{:S(2)}, u32[]{:S(2)}) collective-permute-start(bf16[256,256]{1,0:T(8,128)(2,1)S(1)} %fusion.6), channel_id=1, source_target_pairs={{0,64},{64,128},{128,192},{192,0},{1,65},{65,129},{129,193},{193,1... | collective-permute-start | bytes 393224 | tf_op jit(solution)/shard_map/ppermute | solution.py:39
  32.4 18.6 %collective-permute-start.1 = (bf16[256,256]{1,0:T(8,128)(2,1)S(1)}, bf16[256,256]{1,0:T(8,128)(2,1)S(1)}, u32[]{:S(2)}, u32[]{:S(2)}) collective-permute-start(bf16[256,256]{1,0:T(8,128)(2,1)S(1)} %fusion.6), channel_id=1, source_target_pairs={{0,128},{64,192},{128,0},{192,64},{1,129},{65,193},{129,1},{193,65... | collective-permute-start | bytes 393224 | tf_op jit(solution)/shard_map/ppermute | solution.py:39
  35.1 15.9 %collective-permute-start.2 = (bf16[256,256]{1,0:T(8,128)(2,1)S(1)}, bf16[256,256]{1,0:T(8,128)(2,1)S(1)}, u32[]{:S(2)}, u32[]{:S(2)}) collective-permute-start(bf16[256,256]{1,0:T(8,128)(2,1)S(1)} %fusion.6), channel_id=1, source_target_pairs={{0,192},{64,0},{128,64},{192,128},{1,193},{65,1},{129,65},{193,129... | collective-permute-start | bytes 393224 | tf_op jit(solution)/shard_map/ppermute | solution.py:39
  36.4 14.6 %collective-permute-start.6 = (bf16[1,768,256]{2,1,0:T(8,128)(2,1)S(1)}, bf16[1,768,256]{2,1,0:T(8,128)(2,1)S(1)}, u32[]{:S(2)}, u32[]{:S(2)}) collective-permute-start(bf16[1,768,256]{2,1,0:T(8,128)(2,1)S(1)} %bitcast.110), channel_id=1, source_target_pairs={{0,64},{64,0},{128,192},{192,128},{1,65},{65,1},{129,193},{193,129... | collective-permute-start | bytes 1179656 | tf_op jit(solution)/shard_map/ppermute | solution.py:52
  37.1 13.7 %collective-permute-start.4 = (bf16[1,256,128]{2,1,0:T(8,128)(2,1)S(1)}, bf16[1,256,128]{2,1,0:T(8,128)(2,1)S(1)}, u32[]{:S(2)}, u32[]{:S(2)}) collective-permute-start(bf16[1,256,128]{2,1,0:T(8,128)(2,1)S(1)} %bitcast.116), channel_id=1, source_target_pairs={{0,32},{8,40},{16,48},{24,56},{32,0},{40,8},{48,16},{56,24},{1,33}... | collective-permute-start | bytes 196616 | tf_op jit(solution)/shard_map/ppermute | solution.py:52
  50.9 2.0 collective-permute-start.3
  58.0 5.6 %collective-permute-start.5 = (bf16[2,256,128]{2,1,0:T(8,128)(2,1)S(1)}, bf16[2,256,128]{2,1,0:T(8,128)(2,1)S(1)}, u32[]{:S(2)}, u32[]{:S(2)}) collective-permute-start(bf16[2,256,128]{2,1,0:T(8,128)(2,1)S(1)} %pad_maximum_fusion.18), channel_id=1, source_target_pairs={{0,8},{8,0},{16,24},{24,16},{32,40},{40,32},{48,56},{56,48},{1,9},... | collective-permute-start | bytes 393224 | tf_op jit(solution)/shard_map/ppermute | solution.py:52
  59.6 12.5 %all-to-all-start.2 = ((f32[16,24,128]{2,1,0:T(8,128)}), f32[16,24,128]{2,1,0:T(8,128)S(1)}, u32[]{:S(2)}, u32[]{:S(2)}) async-start(f32[16,24,128]{2,1,0:T(8,128)} %get-tuple-element.49), calls=%async_computation.2 | async-start | bytes 393216 | tf_op jit(solution)/shard_map/all_to_all | solution.py:27
  76.3 20.1 %collective-permute-start.7 = (bf16[4,256,128]{2,1,0:T(8,128)(2,1)S(1)}, bf16[4,256,128]{2,1,0:T(8,128)(2,1)S(1)}, u32[]{:S(2)}, u32[]{:S(2)}) collective-permute-start(bf16[4,256,128]{2,1,0:T(8,128)(2,1)S(1)} %pad_maximum_fusion.3), channel_id=1, source_target_pairs={{0,16},{8,24},{16,0},{24,8},{32,48},{40,56},{48,32},{56,40},{1,17}... | collective-permute-start | bytes 786440 | tf_op jit(solution)/shard_map/ppermute | solution.py:52
  78.1 14.1 %all-to-all-start.3 = ((f32[16,8,128]{2,1,0:T(8,128)}), f32[16,8,128]{2,1,0:T(8,128)S(1)}, u32[]{:S(2)}, u32[]{:S(2)}) async-start(f32[16,8,128]{2,1,0:T(8,128)} %get-tuple-element.54), calls=%async_computation.3 | async-start | bytes 131072 | tf_op jit(solution)/shard_map/all_to_all | solution.py:27
  96.6 19.4 %collective-permute-start.9 = (bf16[2,768,256]{2,1,0:T(8,128)(2,1)S(1)}, bf16[2,768,256]{2,1,0:T(8,128)(2,1)S(1)}, u32[]{:S(2)}, u32[]{:S(2)}) collective-permute-start(bf16[2,768,256]{2,1,0:T(8,128)(2,1)S(1)} %pad_maximum_fusion.1), channel_id=1, source_target_pairs={{0,128},{64,192},{128,0},{192,64},{1,129},{65,193},{129,1},{193,65... | collective-permute-start | bytes 2359304 | tf_op jit(solution)/shard_map/ppermute | solution.py:52
  97.9 16.6 %collective-permute-start.8 = (bf16[8,256,128]{2,1,0:T(8,128)(2,1)S(1)}, bf16[8,256,128]{2,1,0:T(8,128)(2,1)S(1)}, u32[]{:S(2)}, u32[]{:S(2)}) collective-permute-start(bf16[8,256,128]{2,1,0:T(8,128)(2,1)S(1)} %pad_maximum_fusion.2.own_ref), channel_id=1, source_target_pairs={{0,4},{4,0},{1,5},{5,1},{2,6},{6,2},{3,7},{7,3},{8,12},{12,8},{9,1... | collective-permute-start | bytes 1572872 | tf_op jit(solution)/shard_map/ppermute | solution.py:35
  97.9 12.3 %all-to-all-start.4 = ((f32[16,16,128]{2,1,0:T(8,128)}), f32[16,16,128]{2,1,0:T(8,128)S(1)}, u32[]{:S(2)}, u32[]{:S(2)}) async-start(f32[16,16,128]{2,1,0:T(8,128)} %shard_map.70), calls=%async_computation.4 | async-start | bytes 262144 | tf_op jit(solution)/shard_map/all_to_all | solution.py:27
  116.0 0.9 copy-start.4
  116.9 11.4 %all-to-all-start.5 = ((f32[16,8,128]{2,1,0:T(8,128)}), f32[16,8,128]{2,1,0:T(8,128)S(1)}, u32[]{:S(2)}, u32[]{:S(2)}) async-start(f32[16,8,128]{2,1,0:T(8,128)} %get-tuple-element.61), calls=%async_computation.5 | async-start | bytes 131072 | tf_op jit(solution)/shard_map/all_to_all | solution.py:27
  127.2 31.7 %copy-start = (bf16[256,2048]{1,0:T(8,128)(2,1)}, bf16[256,2048]{1,0:T(8,128)(2,1)S(1)}, u32[]{:S(2)}) copy-start(bf16[256,2048]{1,0:T(8,128)(2,1)S(1)} %get-tuple-element.75.proto_ref.ps_ref) | copy-start | bytes 3145732
  132.6 12.3 %all-to-all-start.6 = ((f32[16,16,128]{2,1,0:T(8,128)}), f32[16,16,128]{2,1,0:T(8,128)S(1)}, u32[]{:S(2)}, u32[]{:S(2)}) async-start(f32[16,16,128]{2,1,0:T(8,128)} %shard_map.72), calls=%async_computation.6 | async-start | bytes 262144 | tf_op jit(solution)/shard_map/all_to_all | solution.py:27
  149.2 15.8 %all-to-all-start.7 = ((f32[16,32,128]{2,1,0:T(8,128)}), f32[16,32,128]{2,1,0:T(8,128)S(1)}, u32[]{:S(2)}, u32[]{:S(2)}) async-start(f32[16,32,128]{2,1,0:T(8,128)} %get-tuple-element.72), calls=%async_computation.7 | async-start | bytes 524288 | tf_op jit(solution)/shard_map/all_to_all | solution.py:27
  182.1 5.7 %collective-permute-start.10 = (f32[2064,128]{1,0:T(8,128)}, f32[2064,128]{1,0:T(8,128)}, u32[]{:S(2)}, u32[]{:S(2)}) collective-permute-start(f32[2064,128]{1,0:T(8,128)} %get-tuple-element.77), channel_id=1, source_target_pairs={{0,4},{4,0},{1,5},{5,1},{2,6},{6,2},{3,7},{7,3},{8,12},{12,8},{9,1... | collective-permute-start | bytes 3170312 | tf_op jit(solution)/shard_map/ppermute | solution.py:35
  183.7 4.1 %copy-start.2 = (f32[2064,128]{1,0:T(8,128)S(1)}, f32[2064,128]{1,0:T(8,128)}, u32[]{:S(2)}) copy-start(f32[2064,128]{1,0:T(8,128)} %get-tuple-element.76) | copy-start | bytes 3170308
  183.7 28.7 %all-to-all-start.8 = ((f16[16,192,256]{2,1,0:T(8,128)(2,1)}), f16[16,192,256]{2,1,0:T(8,128)(2,1)S(1)}, u32[]{:S(2)}, u32[]{:S(2)}) async-start(f16[16,192,256]{2,1,0:T(8,128)(2,1)} %bitcast.107), calls=%async_computation.8 | async-start | bytes 3145728 | tf_op jit(solution)/shard_map/all_to_all | solution.py:27
  189.5 11.7 %collective-permute-start.11 = (f16[288,128]{1,0:T(8,128)(2,1)S(1)}, f16[288,128]{1,0:T(8,128)(2,1)S(1)}, u32[]{:S(2)}, u32[]{:S(2)}) collective-permute-start(f16[288,128]{1,0:T(8,128)(2,1)S(1)} %get-tuple-element.107), channel_id=1, source_target_pairs={{0,8},{8,16},{16,24},{24,32},{32,40},{40,48},{48,56},{56,0},{1,9},... | collective-permute-start | bytes 221192 | tf_op jit(solution)/shard_map/ppermute | solution.py:39
  190.2 11.1 %collective-permute-start.12 = (f16[288,128]{1,0:T(8,128)(2,1)S(1)}, f16[288,128]{1,0:T(8,128)(2,1)S(1)}, u32[]{:S(2)}, u32[]{:S(2)}) collective-permute-start(f16[288,128]{1,0:T(8,128)(2,1)S(1)} %get-tuple-element.108), channel_id=1, source_target_pairs={{0,16},{8,24},{16,32},{24,40},{32,48},{40,56},{48,0},{56,8},{1,17}... | collective-permute-start | bytes 221192 | tf_op jit(solution)/shard_map/ppermute | solution.py:39
  191.3 14.9 %collective-permute-start.13 = (f16[288,128]{1,0:T(8,128)(2,1)S(1)}, f16[288,128]{1,0:T(8,128)(2,1)S(1)}, u32[]{:S(2)}, u32[]{:S(2)}) collective-permute-start(f16[288,128]{1,0:T(8,128)(2,1)S(1)} %get-tuple-element.109), channel_id=1, source_target_pairs={{0,24},{8,32},{16,40},{24,48},{32,56},{40,0},{48,8},{56,16},{1,25}... | collective-permute-start | bytes 221192 | tf_op jit(solution)/shard_map/ppermute | solution.py:39
  193.6 12.6 %collective-permute-start.14 = (f16[288,128]{1,0:T(8,128)(2,1)S(1)}, f16[288,128]{1,0:T(8,128)(2,1)S(1)}, u32[]{:S(2)}, u32[]{:S(2)}) collective-permute-start(f16[288,128]{1,0:T(8,128)(2,1)S(1)} %get-tuple-element.110), channel_id=1, source_target_pairs={{0,32},{8,40},{16,48},{24,56},{32,0},{40,8},{48,16},{56,24},{1,33}... | collective-permute-start | bytes 221192 | tf_op jit(solution)/shard_map/ppermute | solution.py:39
  196.9 12.7 %collective-permute-start.15 = (f16[288,128]{1,0:T(8,128)(2,1)S(1)}, f16[288,128]{1,0:T(8,128)(2,1)S(1)}, u32[]{:S(2)}, u32[]{:S(2)}) collective-permute-start(f16[288,128]{1,0:T(8,128)(2,1)S(1)} %get-tuple-element.111), channel_id=1, source_target_pairs={{0,40},{8,48},{16,56},{24,0},{32,8},{40,16},{48,24},{56,32},{1,41}... | collective-permute-start | bytes 221192 | tf_op jit(solution)/shard_map/ppermute | solution.py:39
  201.2 8.4 %collective-permute-start.16 = (f16[288,128]{1,0:T(8,128)(2,1)S(1)}, f16[288,128]{1,0:T(8,128)(2,1)S(1)}, u32[]{:S(2)}, u32[]{:S(2)}) collective-permute-start(f16[288,128]{1,0:T(8,128)(2,1)S(1)} %get-tuple-element.112), channel_id=1, source_target_pairs={{0,48},{8,56},{16,0},{24,8},{32,16},{40,24},{48,32},{56,40},{1,49}... | collective-permute-start | bytes 221192 | tf_op jit(solution)/shard_map/ppermute | solution.py:39
  201.3 10.3 %collective-permute-start.17 = (f16[288,128]{1,0:T(8,128)(2,1)S(1)}, f16[288,128]{1,0:T(8,128)(2,1)S(1)}, u32[]{:S(2)}, u32[]{:S(2)}) collective-permute-start(f16[288,128]{1,0:T(8,128)(2,1)S(1)} %pad_maximum_fusion.4), channel_id=1, source_target_pairs={{0,56},{8,0},{16,8},{24,16},{32,24},{40,32},{48,40},{56,48},{1,57}... | collective-permute-start | bytes 221192 | tf_op jit(solution)/shard_map/ppermute | solution.py:39
  212.7 16.7 %copy-start.6 = (f32[4,8192]{1,0:T(4,128)S(1)}, f32[4,8192]{1,0:T(4,128)}, u32[]{:S(2)}) copy-start(f32[4,8192]{1,0:T(4,128)} %t_ref.1) | copy-start | bytes 393220
  212.7 16.7 %copy-start.7 = (f32[4,8192]{1,0:T(4,128)S(1)}, f32[4,8192]{1,0:T(4,128)}, u32[]{:S(2)}) copy-start(f32[4,8192]{1,0:T(4,128)} %s_ref.1) | copy-start | bytes 393220
  213.5 16.7 %collective-permute-start.18 = (f32[32,6,256]{2,0,1:T(8,128)S(1)}, f32[32,6,256]{2,0,1:T(8,128)S(1)}, u32[]{:S(2)}, u32[]{:S(2)}) collective-permute-start(f32[32,6,256]{2,0,1:T(8,128)S(1)} %bitcast.117), channel_id=1, source_target_pairs={{0,1},{1,2},{2,3},{3,0},{4,5},{5,6},{6,7},{7,4},{8,9},{9,10},{10,1... | collective-permute-start | bytes 589832 | tf_op jit(solution)/shard_map/ppermute | solution.py:39
  214.8 15.4 %collective-permute-start.19 = (f32[32,6,256]{2,0,1:T(8,128)S(1)}, f32[32,6,256]{2,0,1:T(8,128)S(1)}, u32[]{:S(2)}, u32[]{:S(2)}) collective-permute-start(f32[32,6,256]{2,0,1:T(8,128)S(1)} %bitcast.118), channel_id=1, source_target_pairs={{0,2},{1,3},{2,0},{3,1},{4,6},{5,7},{6,4},{7,5},{8,10},{9,11},{10,... | collective-permute-start | bytes 589832 | tf_op jit(solution)/shard_map/ppermute | solution.py:39
  217.4 12.8 %collective-permute-start.20 = (f32[32,6,256]{2,0,1:T(8,128)S(1)}, f32[32,6,256]{2,0,1:T(8,128)S(1)}, u32[]{:S(2)}, u32[]{:S(2)}) collective-permute-start(f32[32,6,256]{2,0,1:T(8,128)S(1)} %bitcast.119), channel_id=1, source_target_pairs={{0,3},{1,0},{2,1},{3,2},{4,7},{5,4},{6,5},{7,6},{8,11},{9,8},{10,9... | collective-permute-start | bytes 589832 | tf_op jit(solution)/shard_map/ppermute | solution.py:39
  218.9 10.3 %all-to-all-start.9 = ((f32[4,16,4,128]{3,1,2,0:T(8,128)}), f32[4,16,4,128]{3,1,2,0:T(8,128)S(1)}, u32[]{:S(2)}, u32[]{:S(2)}) async-start(f32[4,16,4,128]{3,1,2,0:T(8,128)} %bitcast.34), calls=%async_computation.9 | async-start | bytes 262144 | tf_op jit(solution)/shard_map/all_to_all | solution.py:27
  229.4 0.9 copy-start.5
  230.3 0.9 copy-start.3

commit v5 on v4

--- a/solution.py
+++ b/solution.py
@@ -219,7 +219,7 @@
 
 def slope_kernel(
     place_ref, lines_ref, recip_ref, s_ref, st_ref, ps_ref, psp_ref, e_ref,
-    ug_ref, keep_ref, give_ref, slope_ref, total_ref, down_ref,
+    ug_ref, keep_ref, give_ref, slope_ref, total_ref, down_ref, here_ref, sem_ref,
 ):
     rows = st_ref.shape[2]
     width = ps_ref.shape[1]
@@ -227,11 +227,13 @@
     tile = 1024
     g = pl.program_id(0)
     groups = pl.num_programs(0) - 1
+    ordered = pltpu.make_async_copy(psp_ref, here_ref, sem_ref)
 
     @pl.when(g == 0)
     def _():
         total_ref[...] = jnp.zeros_like(total_ref)
         slope_ref[1] = jnp.zeros_like(slope_ref[1])
+        ordered.start()
 
     def products(slot):
         total_ref[...] += jnp.dot(st_ref[0], slope_ref[slot], preferred_element_type=jnp.float32)
@@ -276,12 +278,13 @@
 
     @pl.when(g == groups)
     def _():
+        ordered.wait()
         blocks = width // LANES
         part = total_ref.shape[0] // (NC * NZ)
         size = blocks * part
         for b in range(blocks):
             lanes = slice(b * LANES, (b + 1) * LANES)
-            dot = jnp.sum(psp_ref[:, lanes].astype(jnp.float32) * total_ref[:, lanes], axis=0, keepdims=True)
+            dot = jnp.sum(here_ref[:, lanes].astype(jnp.float32) * total_ref[:, lanes], axis=0, keepdims=True)
             keep_ref[NZ * size + b : NZ * size + b + 1, :] = dot
             give_ref[NZ * size + b : NZ * size + b + 1, :] = dot
         for side, ref in enumerate((keep_ref, give_ref)):
@@ -433,13 +436,15 @@
             pl.BlockSpec((1, s_rows, bottleneck), lambda g: (jnp.minimum(g, NX - 1), 0, 0)),
             pl.BlockSpec((1, bottleneck, s_rows), lambda g: (jnp.maximum(g - 1, 0), 0, 0)),
             whole(bottleneck, width),
-            whole(bottleneck, width),
+            HBM,
             pl.BlockSpec((t_rows, width), lambda g: (jnp.minimum(g, NX - 1), 0)),
         ],
         [
             pltpu.VMEM((2, s_rows, width), bf16),
             pltpu.VMEM((bottleneck, width), f32),
             pltpu.VMEM((2 + CROPS, LANES, LANES), f32),
+            pltpu.VMEM((bottleneck, width), bf16),
+            pltpu.SemaphoreType.DMA,
         ],
         [
             pl.BlockSpec((1, NY, s_rows // NY, bottleneck), lambda g: (jnp.maximum(g - 1, 0), 0, 0, 0)),

time: 232 us -> 232 us (level)
  transfers between devices with their start and end apart: 31 -> 31, of which waited for: 15 -> 16; matrix products, arithmetic and copies ran while one was open for 8% -> 8% of each run, Pallas kernels for 7% -> 7%
where the time goes in v5:
time: 232 us; the launch traced here: 231 us
  starting transfers between devices  88.2 us (38%)
  waiting for transfers between devices  67.3 us (29%)
  Pallas kernels  52.5 us (23%)
  other arithmetic  12.4 us (5%)
  local copies, waits for them, and re-layouts  4.66 us (2%)
  matrix products  4.64 us (2%)
    all_to_all x10, starting transfers between devices, swap(): return lax.all_to_all(v, axes, 0, 0)  55 us
    all_to_all x10, waiting for transfers between devices, swap(): return lax.all_to_all(v, axes, 0, 0)  46.9 us
    ppermute x13, starting transfers between devices, shifted(): return lax.ppermute(v, axis, [(i, (i + k) % n) for i in range(n)])  23.1 us
    pallas_call x1, Pallas kernels, local(): call(slope_kernel, [pltpu.VMEM((NX, NY, s_rows // NY, bottleneck), f32)]...  16.9 us
    pallas_call x3, Pallas kernels, by_row(): call(by_row_kernel, [shape((1, width), f32), shape((NX * NY, lines, LANES...  12.9 us
    ppermute x5, waiting for transfers between devices, exchanged(): return (v, lax.ppermute(v, axis, [(i, i ^ step) for i in range(n)]))  10.8 us
    ppermute x5, starting transfers between devices, exchanged(): return (v, lax.ppermute(v, axis, [(i, i ^ step) for i in range(n)]))  9.82 us
    pallas_call x2, Pallas kernels, by_column(): call(by_column_kernel, [shape((NZ * NC, width // LANES, LANES), f32)], [V...  8.58 us
  transfers between devices with their start and end apart: 31, of which 16 were waited for; matrix products, arithmetic and copies ran while one was open for 8% of the time, Pallas kernels for 7%

profile of v5, /device:TPU:32, one launch (start us, length us, event | category | flops | bytes accessed | tf_op | source)
XLA Modules:
  0.0 231.1 jit_solution(14997993360407669667)
XLA Ops:
  0.6 1.8 shard_map.67
  2.4 11.6 %all-to-all-start = ((f32[64,8,128]{2,1,0:T(8,128)}), f32[64,8,128]{2,1,0:T(8,128)S(1)}, u32[]{:S(2)}, u32[]{:S(2)}) async-start(f32[64,8,128]{2,1,0:T(8,128)} %shard_map.67), calls=%async_computation | async-start | bytes 524288 | tf_op jit(solution)/shard_map/all_to_all | solution.py:27
  14.0 0.9 copy_convert_fusion
  14.9 1.0 multiply_reduce_fusion.1
  16.9 8.9 %all-to-all-done = f32[64,8,128]{2,1,0:T(8,128)S(1)} async-done(((f32[64,8,128]{2,1,0:T(8,128)}), f32[64,8,128]{2,1,0:T(8,128)S(1)}, u32[]{:S(2)}, u32[]{:S(2)}) %all-to-all-start) | async-done | bytes 262176 | tf_op jit(solution)/shard_map/all_to_all | solution.py:27
  26.0 0.9 broadcast_in_dim.52
  26.9 4.8 %all-to-all-start.1 = ((bf16[8,256,128]{2,1,0:T(8,128)(2,1)}), bf16[8,256,128]{2,1,0:T(8,128)(2,1)S(1)}, u32[]{:S(2)}, u32[]{:S(2)}) async-start(bf16[8,256,128]{2,1,0:T(8,128)(2,1)} %broadcast_in_dim.52), calls=%async_computation.1 | async-start | bytes 1048576 | tf_op jit(solution)/shard_map/all_to_all | solution.py:27
  32.4 2.7 %collective-permute-start.1 = (bf16[256,256]{1,0:T(8,128)(2,1)S(1)}, bf16[256,256]{1,0:T(8,128)(2,1)S(1)}, u32[]{:S(2)}, u32[]{:S(2)}) collective-permute-start(bf16[256,256]{1,0:T(8,128)(2,1)S(1)} %fusion.6), channel_id=1, source_target_pairs={{0,128},{64,192},{128,0},{192,64},{1,129},{65,193},{129,1},{193,65... | collective-permute-start | bytes 393224 | tf_op jit(solution)/shard_map/ppermute | solution.py:39
  35.1 1.4 collective-permute-start.2
  37.1 4.5 %collective-permute-start.4 = (bf16[1,256,128]{2,1,0:T(8,128)(2,1)S(1)}, bf16[1,256,128]{2,1,0:T(8,128)(2,1)S(1)}, u32[]{:S(2)}, u32[]{:S(2)}) collective-permute-start(bf16[1,256,128]{2,1,0:T(8,128)(2,1)S(1)} %bitcast.116), channel_id=1, source_target_pairs={{0,32},{8,40},{16,48},{24,56},{32,0},{40,8},{48,16},{56,24},{1,33}... | collective-permute-start | bytes 196616 | tf_op jit(solution)/shard_map/ppermute | solution.py:52
  41.7 9.1 %collective-permute-done.4 = bf16[1,256,128]{2,1,0:T(8,128)(2,1)S(1)} collective-permute-done((bf16[1,256,128]{2,1,0:T(8,128)(2,1)S(1)}, bf16[1,256,128]{2,1,0:T(8,128)(2,1)S(1)}, u32[]{:S(2)}, u32[]{:S(2)}) %collective-permute-start.4) | collective-permute-done | bytes 65568 | tf_op jit(solution)/shard_map/ppermute | solution.py:52
  51.1 1.7 collective-permute-done.3.other_ref
  52.9 5.2 %shard_map.68 = (f32[1024,2048]{1,0:T(8,128)}, f32[16,24,128]{2,1,0:T(8,128)}) custom-call(s32[2]{0:T(128)S(1)} %pad_add_fusion.place_ref, f32[1,128]{1,0:T(1,128)S(1)} %get-tuple-element.116.norm_ref, bf16[1024,256]{1,0:T(8,128)(2,1)S(1)} %bitcast.106, bf16[8,256,128]{2,1,0:T(8,128)(2,1)S(1)} %all-to-all-done.1.own_ref, ...), custom_call_target="tpu_custom_call" | custom-call | flops 1073741824 | tf_op jit(solution)/shard_map/pallas_call | solution.py:336
  58.0 1.6 collective-permute-start.5
  59.6 3.9 %all-to-all-start.2 = ((f32[16,24,128]{2,1,0:T(8,128)}), f32[16,24,128]{2,1,0:T(8,128)S(1)}, u32[]{:S(2)}, u32[]{:S(2)}) async-start(f32[16,24,128]{2,1,0:T(8,128)} %get-tuple-element.49), calls=%async_computation.2 | async-start | bytes 393216 | tf_op jit(solution)/shard_map/all_to_all | solution.py:27
  63.7 8.3 %all-to-all-done.2.got_ref = f32[16,24,128]{2,1,0:T(8,128)S(1)} async-done(((f32[16,24,128]{2,1,0:T(8,128)}), f32[16,24,128]{2,1,0:T(8,128)S(1)}, u32[]{:S(2)}, u32[]{:S(2)}) %all-to-all-start.2) | async-done | bytes 196640 | tf_op jit(solution)/shard_map/all_to_all | solution.py:27
  72.1 4.3 %shard_map.69 = (f32[1,2048]{1,0:T(1,128)}, f32[16,8,128]{2,1,0:T(8,128)}) custom-call(f32[16,24,128]{2,1,0:T(8,128)S(1)} %all-to-all-done.2.got_ref, f32[1024,2048]{1,0:T(8,128)} %get-tuple-element.50.e_ref), custom_call_target="tpu_custom_call" | custom-call | flops 4194304 | bytes 8388608 | tf_op jit(solution)/shard_map/pallas_call | solution.py:363
  76.3 1.8 collective-permute-start.7
  78.1 6.4 %all-to-all-start.3 = ((f32[16,8,128]{2,1,0:T(8,128)}), f32[16,8,128]{2,1,0:T(8,128)S(1)}, u32[]{:S(2)}, u32[]{:S(2)}) async-start(f32[16,8,128]{2,1,0:T(8,128)} %get-tuple-element.54), calls=%async_computation.3 | async-start | bytes 131072 | tf_op jit(solution)/shard_map/all_to_all | solution.py:27
  84.5 7.6 %all-to-all-done.3.got_ref = f32[16,8,128]{2,1,0:T(8,128)S(1)} async-done(((f32[16,8,128]{2,1,0:T(8,128)}), f32[16,8,128]{2,1,0:T(8,128)S(1)}, u32[]{:S(2)}, u32[]{:S(2)}) %all-to-all-start.3) | async-done | bytes 65568 | tf_op jit(solution)/shard_map/all_to_all | solution.py:27
  92.2 4.3 %shard_map.70 = f32[16,16,128]{2,1,0:T(8,128)} custom-call(f32[16,8,128]{2,1,0:T(8,128)S(1)} %all-to-all-done.3.got_ref, f32[1024,2048]{1,0:T(8,128)} %get-tuple-element.50.e_ref), custom_call_target="tpu_custom_call" | custom-call | flops 4194304 | bytes 8388608 | tf_op jit(solution)/shard_map/pallas_call | solution.py:374
  96.6 1.3 collective-permute-start.9
  97.9 4.9 %all-to-all-start.4 = ((f32[16,16,128]{2,1,0:T(8,128)}), f32[16,16,128]{2,1,0:T(8,128)S(1)}, u32[]{:S(2)}, u32[]{:S(2)}) async-start(f32[16,16,128]{2,1,0:T(8,128)} %shard_map.70), calls=%async_computation.4 | async-start | bytes 262144 | tf_op jit(solution)/shard_map/all_to_all | solution.py:27
  102.8 7.4 %all-to-all-done.4.got_ref = f32[16,16,128]{2,1,0:T(8,128)S(1)} async-done(((f32[16,16,128]{2,1,0:T(8,128)}), f32[16,16,128]{2,1,0:T(8,128)S(1)}, u32[]{:S(2)}, u32[]{:S(2)}) %all-to-all-start.4) | async-done | bytes 131104 | tf_op jit(solution)/shard_map/all_to_all | solution.py:27
  110.2 4.3 %shard_map.71 = (f32[1,2048]{1,0:T(1,128)}, f32[16,8,128]{2,1,0:T(8,128)}) custom-call(f32[16,16,128]{2,1,0:T(8,128)S(1)} %all-to-all-done.4.got_ref, f32[1024,2048]{1,0:T(8,128)} %get-tuple-element.50.e_ref), custom_call_target="tpu_custom_call" | custom-call | flops 4194304 | bytes 8388608 | tf_op jit(solution)/shard_map/pallas_call | solution.py:363
  114.5 1.6 collective-permute-done.9
  116.0 0.9 copy-done.4
  116.9 3.7 %all-to-all-start.5 = ((f32[16,8,128]{2,1,0:T(8,128)}), f32[16,8,128]{2,1,0:T(8,128)S(1)}, u32[]{:S(2)}, u32[]{:S(2)}) async-start(f32[16,8,128]{2,1,0:T(8,128)} %get-tuple-element.61), calls=%async_computation.5 | async-start | bytes 131072 | tf_op jit(solution)/shard_map/all_to_all | solution.py:27
  120.7 1.2 broadcast_select_fusion
  121.9 1.3 pad_maximum_fusion.s_ref
  123.2 4.0 %shard_map.73 = (bf16[256,2048]{1,0:T(8,128)(2,1)S(1)}, f32[12,128]{1,0:T(8,128)S(1)}) custom-call(s32[2]{0:T(128)S(1)} %pad_add_fusion.place_ref, bf16[1536,256]{1,0:T(8,128)(2,1)S(1)} %bitcast.104, bf16[8,256,128]{2,1,0:T(8,128)(2,1)S(1)} %pad_maximum_fusion.2.own_ref, bf16[8,256,128]{2,1,0:T(8,128)(2,1)S(1)} %collective-permute-done.8.other_ref), custom_call_target="tpu_custom_call" | custom-call | flops 1610612736 | tf_op jit(solution)/shard_map/pallas_call | solution.py:407
  127.2 1.1 all-to-all-done.5.got_ref
  128.3 4.3 %shard_map.72 = f32[16,16,128]{2,1,0:T(8,128)} custom-call(f32[16,8,128]{2,1,0:T(8,128)S(1)} %all-to-all-done.5.got_ref, f32[1024,2048]{1,0:T(8,128)} %get-tuple-element.50.e_ref), custom_call_target="tpu_custom_call" | custom-call | flops 4194304 | bytes 8388608 | tf_op jit(solution)/shard_map/pallas_call | solution.py:374
  132.6 4.9 %all-to-all-start.6 = ((f32[16,16,128]{2,1,0:T(8,128)}), f32[16,16,128]{2,1,0:T(8,128)S(1)}, u32[]{:S(2)}, u32[]{:S(2)}) async-start(f32[16,16,128]{2,1,0:T(8,128)} %shard_map.72), calls=%async_computation.6 | async-start | bytes 262144 | tf_op jit(solution)/shard_map/all_to_all | solution.py:27
  137.6 1.2 slice.114
  138.8 3.2 %shard_map.74.refs_1_ = f32[12,128]{1,0:T(8,128)S(1)} custom-call(bf16[1536,256]{1,0:T(8,128)(2,1)S(1)} %bitcast.105, bf16[256,2048]{1,0:T(8,128)(2,1)S(1)} %get-tuple-element.75.proto_ref.ps_ref), custom_call_target="tpu_custom_call" | custom-call | flops 1610612736 | tf_op jit(solution)/shard_map/pallas_call | solution.py:417
  142.0 2.9 %all-to-all-done.6.got_ref = f32[16,16,128]{2,1,0:T(8,128)S(1)} async-done(((f32[16,16,128]{2,1,0:T(8,128)}), f32[16,16,128]{2,1,0:T(8,128)S(1)}, u32[]{:S(2)}, u32[]{:S(2)}) %all-to-all-start.6) | async-done | bytes 131104 | tf_op jit(solution)/shard_map/all_to_all | solution.py:27
  144.9 4.3 %shard_map.75 = (f32[1,2048]{1,0:T(1,128)S(1)}, f32[16,32,128]{2,1,0:T(8,128)}) custom-call(f32[16,16,128]{2,1,0:T(8,128)S(1)} %all-to-all-done.6.got_ref, f32[1024,2048]{1,0:T(8,128)} %get-tuple-element.50.e_ref, f32[12,128]{1,0:T(8,128)S(1)} %get-tuple-element.68.refs_0_, f32[12,128]{1,0:T(8,128)S(1)} %shard_map.74.refs_1_), custom_call_target="tpu_custom_call" | custom-call | flops 4194304 | bytes 8388608 | tf_op jit(solution)/shard_map/pallas_call | solution.py:363
  149.2 6.5 %all-to-all-start.7 = ((f32[16,32,128]{2,1,0:T(8,128)}), f32[16,32,128]{2,1,0:T(8,128)S(1)}, u32[]{:S(2)}, u32[]{:S(2)}) async-start(f32[16,32,128]{2,1,0:T(8,128)} %get-tuple-element.72), calls=%async_computation.7 | async-start | bytes 524288 | tf_op jit(solution)/shard_map/all_to_all | solution.py:27
  155.7 3.2 %fusion.1.st_ref = bf16[4,256,768]{2,1,0:T(8,128)(2,1)} fusion(bf16[4,768,256]{2,1,0:T(8,128)(2,1)} %pad_maximum_fusion.s_ref, s32[256]{0:T(256)S(1)} %reshape.210), kind=kOutput, calls=%fused_computation.6 | convolution fusion | flops 403505152 | bytes 3146752 | tf_op jit(solution)/shard_map/pb,grb->gpr/dot_general | solution.py:427
  158.9 1.5 convolution_convert_fusion.psp_ref
  160.4 4.7 %all-to-all-done.7 = f32[16,32,128]{2,1,0:T(8,128)S(1)} async-done(((f32[16,32,128]{2,1,0:T(8,128)}), f32[16,32,128]{2,1,0:T(8,128)S(1)}, u32[]{:S(2)}, u32[]{:S(2)}) %all-to-all-start.7) | async-done | bytes 262176 | tf_op jit(solution)/shard_map/all_to_all | solution.py:27
  165.1 16.9 %shard_map.76 = (f32[4,4,192,256]{3,2,1,0:T(8,128)S(1)}, f32[2064,128]{1,0:T(8,128)}, f32[2064,128]{1,0:T(8,128)}) custom-call(s32[2]{0:T(128)S(1)} %pad_add_fusion.place_ref, f32[32,128]{1,0:T(8,128)S(1)} %broadcast_divide_fusion.lines_ref, f32[1,2048]{1,0:T(1,128)S(1)} %get-tuple-element.73.recip_ref, bf16[4,768,256]{2,1,0:T(8,128)(2,1)} %pad_maximum_fusion.s_ref, ...), custom_call_target="tpu_custom_call" | custom-call | flops 9663676416 | bytes 8388608 | tf_op jit(solution)/shard_map/pallas_call | solution.py:429
  182.2 1.6 multiply_convert_fusion
  183.8 4.1 %all-to-all-start.8 = ((f16[16,192,256]{2,1,0:T(8,128)(2,1)}), f16[16,192,256]{2,1,0:T(8,128)(2,1)S(1)}, u32[]{:S(2)}, u32[]{:S(2)}) async-start(f16[16,192,256]{2,1,0:T(8,128)(2,1)} %bitcast.107), calls=%async_computation.8 | async-start | bytes 3145728 | tf_op jit(solution)/shard_map/all_to_all | solution.py:27
  187.8 1.4 fusion.34
  189.5 0.8 collective-permute-start.11
  190.3 1.0 collective-permute-start.12
  191.3 2.4 %collective-permute-start.13 = (f16[288,128]{1,0:T(8,128)(2,1)S(1)}, f16[288,128]{1,0:T(8,128)(2,1)S(1)}, u32[]{:S(2)}, u32[]{:S(2)}) collective-permute-start(f16[288,128]{1,0:T(8,128)(2,1)S(1)} %get-tuple-element.109), channel_id=1, source_target_pairs={{0,24},{8,32},{16,40},{24,48},{32,56},{40,0},{48,8},{56,16},{1,25}... | collective-permute-start | bytes 221192 | tf_op jit(solution)/shard_map/ppermute | solution.py:39
  193.6 3.3 %collective-permute-start.14 = (f16[288,128]{1,0:T(8,128)(2,1)S(1)}, f16[288,128]{1,0:T(8,128)(2,1)S(1)}, u32[]{:S(2)}, u32[]{:S(2)}) collective-permute-start(f16[288,128]{1,0:T(8,128)(2,1)S(1)} %get-tuple-element.110), channel_id=1, source_target_pairs={{0,32},{8,40},{16,48},{24,56},{32,0},{40,8},{48,16},{56,24},{1,33}... | collective-permute-start | bytes 221192 | tf_op jit(solution)/shard_map/ppermute | solution.py:39
  196.9 4.3 %collective-permute-start.15 = (f16[288,128]{1,0:T(8,128)(2,1)S(1)}, f16[288,128]{1,0:T(8,128)(2,1)S(1)}, u32[]{:S(2)}, u32[]{:S(2)}) collective-permute-start(f16[288,128]{1,0:T(8,128)(2,1)S(1)} %get-tuple-element.111), channel_id=1, source_target_pairs={{0,40},{8,48},{16,56},{24,0},{32,8},{40,16},{48,24},{56,32},{1,41}... | collective-permute-start | bytes 221192 | tf_op jit(solution)/shard_map/ppermute | solution.py:39
  201.4 1.3 collective-permute-start.17
  202.7 0.8 convert_bitcast_fusion.1
  203.6 2.6 %collective-permute-done.13 = f16[288,128]{1,0:T(8,128)(2,1)S(1)} collective-permute-done((f16[288,128]{1,0:T(8,128)(2,1)S(1)}, f16[288,128]{1,0:T(8,128)(2,1)S(1)}, u32[]{:S(2)}, u32[]{:S(2)}) %collective-permute-start.13) | collective-permute-done | bytes 73760 | tf_op jit(solution)/shard_map/ppermute | solution.py:39
  206.2 3.2 %collective-permute-done.15 = f16[288,128]{1,0:T(8,128)(2,1)S(1)} collective-permute-done((f16[288,128]{1,0:T(8,128)(2,1)S(1)}, f16[288,128]{1,0:T(8,128)(2,1)S(1)}, u32[]{:S(2)}, u32[]{:S(2)}) %collective-permute-start.15) | collective-permute-done | bytes 73760 | tf_op jit(solution)/shard_map/ppermute | solution.py:39
  209.5 2.1 collective-permute-done.17
  212.8 0.7 fusion.4
  213.5 1.2 collective-permute-start.18
  214.7 2.7 %collective-permute-start.19 = (f32[32,6,256]{2,0,1:T(8,128)S(1)}, f32[32,6,256]{2,0,1:T(8,128)S(1)}, u32[]{:S(2)}, u32[]{:S(2)}) collective-permute-start(f32[32,6,256]{2,0,1:T(8,128)S(1)} %bitcast.118), channel_id=1, source_target_pairs={{0,2},{1,3},{2,0},{3,1},{4,6},{5,7},{6,4},{7,5},{8,10},{9,11},{10,... | collective-permute-start | bytes 589832 | tf_op jit(solution)/shard_map/ppermute | solution.py:39
  217.4 1.5 collective-permute-start.20
  218.8 4.3 %all-to-all-start.9 = ((f32[4,16,4,128]{3,1,2,0:T(8,128)}), f32[4,16,4,128]{3,1,2,0:T(8,128)S(1)}, u32[]{:S(2)}, u32[]{:S(2)}) async-start(f32[4,16,4,128]{3,1,2,0:T(8,128)} %bitcast.34), calls=%async_computation.9 | async-start | bytes 262144 | tf_op jit(solution)/shard_map/all_to_all | solution.py:27
  223.2 5.9 %all-to-all-done.9 = f32[4,16,4,128]{3,1,2,0:T(8,128)S(1)} async-done(((f32[4,16,4,128]{3,1,2,0:T(8,128)}), f32[4,16,4,128]{3,1,2,0:T(8,128)S(1)}, u32[]{:S(2)}, u32[]{:S(2)}) %all-to-all-start.9) | async-done | bytes 131104 | tf_op jit(solution)/shard_map/all_to_all | solution.py:27
  229.3 0.7 multiply_add_fusion
  230.2 0.9 copy-done.3
  (95 shorter events, 5.4 us)
Async XLA Ops:
  0.6 15.3 %copy-start.1 = (bf16[128,6,256]{2,0,1:T(8,128)(2,1)S(1)}, bf16[128,6,256]{2,0,1:T(8,128)(2,1)}, u32[]{:S(2)}) copy-start(bf16[128,6,256]{2,0,1:T(8,128)(2,1)} %param.5) | copy-start | bytes 1179652
  2.4 23.3 %all-to-all-start = ((f32[64,8,128]{2,1,0:T(8,128)}), f32[64,8,128]{2,1,0:T(8,128)S(1)}, u32[]{:S(2)}, u32[]{:S(2)}) async-start(f32[64,8,128]{2,1,0:T(8,128)} %shard_map.67), calls=%async_computation | async-start | bytes 524288 | tf_op jit(solution)/shard_map/all_to_all | solution.py:27
  26.9 24.0 %all-to-all-start.1 = ((bf16[8,256,128]{2,1,0:T(8,128)(2,1)}), bf16[8,256,128]{2,1,0:T(8,128)(2,1)S(1)}, u32[]{:S(2)}, u32[]{:S(2)}) async-start(bf16[8,256,128]{2,1,0:T(8,128)(2,1)} %broadcast_in_dim.52), calls=%async_computation.1 | async-start | bytes 1048576 | tf_op jit(solution)/shard_map/all_to_all | solution.py:27
  31.7 19.1 %collective-permute-start = (bf16[256,256]{1,0:T(8,128)(2,1)S(1)}, bf16[256,256]{1,0:T(8,128)(2,1)S(1)}, u32[]{:S(2)}, u32[]{:S(2)}) collective-permute-start(bf16[256,256]{1,0:T(8,128)(2,1)S(1)} %fusion.6), channel_id=1, source_target_pairs={{0,64},{64,128},{128,192},{192,0},{1,65},{65,129},{129,193},{193,1... | collective-permute-start | bytes 393224 | tf_op jit(solution)/shard_map/ppermute | solution.py:39
  32.4 18.6 %collective-permute-start.1 = (bf16[256,256]{1,0:T(8,128)(2,1)S(1)}, bf16[256,256]{1,0:T(8,128)(2,1)S(1)}, u32[]{:S(2)}, u32[]{:S(2)}) collective-permute-start(bf16[256,256]{1,0:T(8,128)(2,1)S(1)} %fusion.6), channel_id=1, source_target_pairs={{0,128},{64,192},{128,0},{192,64},{1,129},{65,193},{129,1},{193,65... | collective-permute-start | bytes 393224 | tf_op jit(solution)/shard_map/ppermute | solution.py:39
  35.1 15.9 %collective-permute-start.2 = (bf16[256,256]{1,0:T(8,128)(2,1)S(1)}, bf16[256,256]{1,0:T(8,128)(2,1)S(1)}, u32[]{:S(2)}, u32[]{:S(2)}) collective-permute-start(bf16[256,256]{1,0:T(8,128)(2,1)S(1)} %fusion.6), channel_id=1, source_target_pairs={{0,192},{64,0},{128,64},{192,128},{1,193},{65,1},{129,65},{193,129... | collective-permute-start | bytes 393224 | tf_op jit(solution)/shard_map/ppermute | solution.py:39
  36.4 14.6 %collective-permute-start.6 = (bf16[1,768,256]{2,1,0:T(8,128)(2,1)S(1)}, bf16[1,768,256]{2,1,0:T(8,128)(2,1)S(1)}, u32[]{:S(2)}, u32[]{:S(2)}) collective-permute-start(bf16[1,768,256]{2,1,0:T(8,128)(2,1)S(1)} %bitcast.110), channel_id=1, source_target_pairs={{0,64},{64,0},{128,192},{192,128},{1,65},{65,1},{129,193},{193,129... | collective-permute-start | bytes 1179656 | tf_op jit(solution)/shard_map/ppermute | solution.py:52
  37.1 13.7 %collective-permute-start.4 = (bf16[1,256,128]{2,1,0:T(8,128)(2,1)S(1)}, bf16[1,256,128]{2,1,0:T(8,128)(2,1)S(1)}, u32[]{:S(2)}, u32[]{:S(2)}) collective-permute-start(bf16[1,256,128]{2,1,0:T(8,128)(2,1)S(1)} %bitcast.116), channel_id=1, source_target_pairs={{0,32},{8,40},{16,48},{24,56},{32,0},{40,8},{48,16},{56,24},{1,33}... | collective-permute-start | bytes 196616 | tf_op jit(solution)/shard_map/ppermute | solution.py:52
  50.9 2.0 collective-permute-start.3
  58.0 5.6 %collective-permute-start.5 = (bf16[2,256,128]{2,1,0:T(8,128)(2,1)S(1)}, bf16[2,256,128]{2,1,0:T(8,128)(2,1)S(1)}, u32[]{:S(2)}, u32[]{:S(2)}) collective-permute-start(bf16[2,256,128]{2,1,0:T(8,128)(2,1)S(1)} %pad_maximum_fusion.18), channel_id=1, source_target_pairs={{0,8},{8,0},{16,24},{24,16},{32,40},{40,32},{48,56},{56,48},{1,9},... | collective-permute-start | bytes 393224 | tf_op jit(solution)/shard_map/ppermute | solution.py:52
  59.6 12.5 %all-to-all-start.2 = ((f32[16,24,128]{2,1,0:T(8,128)}), f32[16,24,128]{2,1,0:T(8,128)S(1)}, u32[]{:S(2)}, u32[]{:S(2)}) async-start(f32[16,24,128]{2,1,0:T(8,128)} %get-tuple-element.49), calls=%async_computation.2 | async-start | bytes 393216 | tf_op jit(solution)/shard_map/all_to_all | solution.py:27
  76.3 20.1 %collective-permute-start.7 = (bf16[4,256,128]{2,1,0:T(8,128)(2,1)S(1)}, bf16[4,256,128]{2,1,0:T(8,128)(2,1)S(1)}, u32[]{:S(2)}, u32[]{:S(2)}) collective-permute-start(bf16[4,256,128]{2,1,0:T(8,128)(2,1)S(1)} %pad_maximum_fusion.3), channel_id=1, source_target_pairs={{0,16},{8,24},{16,0},{24,8},{32,48},{40,56},{48,32},{56,40},{1,17}... | collective-permute-start | bytes 786440 | tf_op jit(solution)/shard_map/ppermute | solution.py:52
  78.1 14.1 %all-to-all-start.3 = ((f32[16,8,128]{2,1,0:T(8,128)}), f32[16,8,128]{2,1,0:T(8,128)S(1)}, u32[]{:S(2)}, u32[]{:S(2)}) async-start(f32[16,8,128]{2,1,0:T(8,128)} %get-tuple-element.54), calls=%async_computation.3 | async-start | bytes 131072 | tf_op jit(solution)/shard_map/all_to_all | solution.py:27
  96.6 19.4 %collective-permute-start.9 = (bf16[2,768,256]{2,1,0:T(8,128)(2,1)S(1)}, bf16[2,768,256]{2,1,0:T(8,128)(2,1)S(1)}, u32[]{:S(2)}, u32[]{:S(2)}) collective-permute-start(bf16[2,768,256]{2,1,0:T(8,128)(2,1)S(1)} %pad_maximum_fusion.1), channel_id=1, source_target_pairs={{0,128},{64,192},{128,0},{192,64},{1,129},{65,193},{129,1},{193,65... | collective-permute-start | bytes 2359304 | tf_op jit(solution)/shard_map/ppermute | solution.py:52
  97.9 16.6 %collective-permute-start.8 = (bf16[8,256,128]{2,1,0:T(8,128)(2,1)S(1)}, bf16[8,256,128]{2,1,0:T(8,128)(2,1)S(1)}, u32[]{:S(2)}, u32[]{:S(2)}) collective-permute-start(bf16[8,256,128]{2,1,0:T(8,128)(2,1)S(1)} %pad_maximum_fusion.2.own_ref), channel_id=1, source_target_pairs={{0,4},{4,0},{1,5},{5,1},{2,6},{6,2},{3,7},{7,3},{8,12},{12,8},{9,1... | collective-permute-start | bytes 1572872 | tf_op jit(solution)/shard_map/ppermute | solution.py:35
  97.9 12.3 %all-to-all-start.4 = ((f32[16,16,128]{2,1,0:T(8,128)}), f32[16,16,128]{2,1,0:T(8,128)S(1)}, u32[]{:S(2)}, u32[]{:S(2)}) async-start(f32[16,16,128]{2,1,0:T(8,128)} %shard_map.70), calls=%async_computation.4 | async-start | bytes 262144 | tf_op jit(solution)/shard_map/all_to_all | solution.py:27
  116.0 0.9 copy-start.4
  116.9 11.4 %all-to-all-start.5 = ((f32[16,8,128]{2,1,0:T(8,128)}), f32[16,8,128]{2,1,0:T(8,128)S(1)}, u32[]{:S(2)}, u32[]{:S(2)}) async-start(f32[16,8,128]{2,1,0:T(8,128)} %get-tuple-element.61), calls=%async_computation.5 | async-start | bytes 131072 | tf_op jit(solution)/shard_map/all_to_all | solution.py:27
  127.2 31.7 %copy-start = (bf16[256,2048]{1,0:T(8,128)(2,1)}, bf16[256,2048]{1,0:T(8,128)(2,1)S(1)}, u32[]{:S(2)}) copy-start(bf16[256,2048]{1,0:T(8,128)(2,1)S(1)} %get-tuple-element.75.proto_ref.ps_ref) | copy-start | bytes 3145732
  132.6 12.3 %all-to-all-start.6 = ((f32[16,16,128]{2,1,0:T(8,128)}), f32[16,16,128]{2,1,0:T(8,128)S(1)}, u32[]{:S(2)}, u32[]{:S(2)}) async-start(f32[16,16,128]{2,1,0:T(8,128)} %shard_map.72), calls=%async_computation.6 | async-start | bytes 262144 | tf_op jit(solution)/shard_map/all_to_all | solution.py:27
  149.2 15.8 %all-to-all-start.7 = ((f32[16,32,128]{2,1,0:T(8,128)}), f32[16,32,128]{2,1,0:T(8,128)S(1)}, u32[]{:S(2)}, u32[]{:S(2)}) async-start(f32[16,32,128]{2,1,0:T(8,128)} %get-tuple-element.72), calls=%async_computation.7 | async-start | bytes 524288 | tf_op jit(solution)/shard_map/all_to_all | solution.py:27
  181.9 5.9 %collective-permute-start.10 = (f32[2064,128]{1,0:T(8,128)}, f32[2064,128]{1,0:T(8,128)}, u32[]{:S(2)}, u32[]{:S(2)}) collective-permute-start(f32[2064,128]{1,0:T(8,128)} %get-tuple-element.77), channel_id=1, source_target_pairs={{0,4},{4,0},{1,5},{5,1},{2,6},{6,2},{3,7},{7,3},{8,12},{12,8},{9,1... | collective-permute-start | bytes 3170312 | tf_op jit(solution)/shard_map/ppermute | solution.py:35
  183.8 4.1 %copy-start.2 = (f32[2064,128]{1,0:T(8,128)S(1)}, f32[2064,128]{1,0:T(8,128)}, u32[]{:S(2)}) copy-start(f32[2064,128]{1,0:T(8,128)} %get-tuple-element.76) | copy-start | bytes 3170308
  183.8 28.8 %all-to-all-start.8 = ((f16[16,192,256]{2,1,0:T(8,128)(2,1)}), f16[16,192,256]{2,1,0:T(8,128)(2,1)S(1)}, u32[]{:S(2)}, u32[]{:S(2)}) async-start(f16[16,192,256]{2,1,0:T(8,128)(2,1)} %bitcast.107), calls=%async_computation.8 | async-start | bytes 3145728 | tf_op jit(solution)/shard_map/all_to_all | solution.py:27
  189.5 11.8 %collective-permute-start.11 = (f16[288,128]{1,0:T(8,128)(2,1)S(1)}, f16[288,128]{1,0:T(8,128)(2,1)S(1)}, u32[]{:S(2)}, u32[]{:S(2)}) collective-permute-start(f16[288,128]{1,0:T(8,128)(2,1)S(1)} %get-tuple-element.107), channel_id=1, source_target_pairs={{0,8},{8,16},{16,24},{24,32},{32,40},{40,48},{48,56},{56,0},{1,9},... | collective-permute-start | bytes 221192 | tf_op jit(solution)/shard_map/ppermute | solution.py:39
  190.3 11.1 %collective-permute-start.12 = (f16[288,128]{1,0:T(8,128)(2,1)S(1)}, f16[288,128]{1,0:T(8,128)(2,1)S(1)}, u32[]{:S(2)}, u32[]{:S(2)}) collective-permute-start(f16[288,128]{1,0:T(8,128)(2,1)S(1)} %get-tuple-element.108), channel_id=1, source_target_pairs={{0,16},{8,24},{16,32},{24,40},{32,48},{40,56},{48,0},{56,8},{1,17}... | collective-permute-start | bytes 221192 | tf_op jit(solution)/shard_map/ppermute | solution.py:39
  191.3 14.9 %collective-permute-start.13 = (f16[288,128]{1,0:T(8,128)(2,1)S(1)}, f16[288,128]{1,0:T(8,128)(2,1)S(1)}, u32[]{:S(2)}, u32[]{:S(2)}) collective-permute-start(f16[288,128]{1,0:T(8,128)(2,1)S(1)} %get-tuple-element.109), channel_id=1, source_target_pairs={{0,24},{8,32},{16,40},{24,48},{32,56},{40,0},{48,8},{56,16},{1,25}... | collective-permute-start | bytes 221192 | tf_op jit(solution)/shard_map/ppermute | solution.py:39
  193.6 12.5 %collective-permute-start.14 = (f16[288,128]{1,0:T(8,128)(2,1)S(1)}, f16[288,128]{1,0:T(8,128)(2,1)S(1)}, u32[]{:S(2)}, u32[]{:S(2)}) collective-permute-start(f16[288,128]{1,0:T(8,128)(2,1)S(1)} %get-tuple-element.110), channel_id=1, source_target_pairs={{0,32},{8,40},{16,48},{24,56},{32,0},{40,8},{48,16},{56,24},{1,33}... | collective-permute-start | bytes 221192 | tf_op jit(solution)/shard_map/ppermute | solution.py:39
  196.9 12.5 %collective-permute-start.15 = (f16[288,128]{1,0:T(8,128)(2,1)S(1)}, f16[288,128]{1,0:T(8,128)(2,1)S(1)}, u32[]{:S(2)}, u32[]{:S(2)}) collective-permute-start(f16[288,128]{1,0:T(8,128)(2,1)S(1)} %get-tuple-element.111), channel_id=1, source_target_pairs={{0,40},{8,48},{16,56},{24,0},{32,8},{40,16},{48,24},{56,32},{1,41}... | collective-permute-start | bytes 221192 | tf_op jit(solution)/shard_map/ppermute | solution.py:39
  201.3 8.1 %collective-permute-start.16 = (f16[288,128]{1,0:T(8,128)(2,1)S(1)}, f16[288,128]{1,0:T(8,128)(2,1)S(1)}, u32[]{:S(2)}, u32[]{:S(2)}) collective-permute-start(f16[288,128]{1,0:T(8,128)(2,1)S(1)} %get-tuple-element.112), channel_id=1, source_target_pairs={{0,48},{8,56},{16,0},{24,8},{32,16},{40,24},{48,32},{56,40},{1,49}... | collective-permute-start | bytes 221192 | tf_op jit(solution)/shard_map/ppermute | solution.py:39
  201.4 10.2 %collective-permute-start.17 = (f16[288,128]{1,0:T(8,128)(2,1)S(1)}, f16[288,128]{1,0:T(8,128)(2,1)S(1)}, u32[]{:S(2)}, u32[]{:S(2)}) collective-permute-start(f16[288,128]{1,0:T(8,128)(2,1)S(1)} %pad_maximum_fusion.4), channel_id=1, source_target_pairs={{0,56},{8,0},{16,8},{24,16},{32,24},{40,32},{48,40},{56,48},{1,57}... | collective-permute-start | bytes 221192 | tf_op jit(solution)/shard_map/ppermute | solution.py:39
  212.7 16.6 %copy-start.6 = (f32[4,8192]{1,0:T(4,128)S(1)}, f32[4,8192]{1,0:T(4,128)}, u32[]{:S(2)}) copy-start(f32[4,8192]{1,0:T(4,128)} %t_ref.1) | copy-start | bytes 393220
  212.8 16.6 %copy-start.7 = (f32[4,8192]{1,0:T(4,128)S(1)}, f32[4,8192]{1,0:T(4,128)}, u32[]{:S(2)}) copy-start(f32[4,8192]{1,0:T(4,128)} %s_ref.1) | copy-start | bytes 393220
  213.5 16.6 %collective-permute-start.18 = (f32[32,6,256]{2,0,1:T(8,128)S(1)}, f32[32,6,256]{2,0,1:T(8,128)S(1)}, u32[]{:S(2)}, u32[]{:S(2)}) collective-permute-start(f32[32,6,256]{2,0,1:T(8,128)S(1)} %bitcast.117), channel_id=1, source_target_pairs={{0,1},{1,2},{2,3},{3,0},{4,5},{5,6},{6,7},{7,4},{8,9},{9,10},{10,1... | collective-permute-start | bytes 589832 | tf_op jit(solution)/shard_map/ppermute | solution.py:39
  214.7 15.4 %collective-permute-start.19 = (f32[32,6,256]{2,0,1:T(8,128)S(1)}, f32[32,6,256]{2,0,1:T(8,128)S(1)}, u32[]{:S(2)}, u32[]{:S(2)}) collective-permute-start(f32[32,6,256]{2,0,1:T(8,128)S(1)} %bitcast.118), channel_id=1, source_target_pairs={{0,2},{1,3},{2,0},{3,1},{4,6},{5,7},{6,4},{7,5},{8,10},{9,11},{10,... | collective-permute-start | bytes 589832 | tf_op jit(solution)/shard_map/ppermute | solution.py:39
  217.4 12.8 %collective-permute-start.20 = (f32[32,6,256]{2,0,1:T(8,128)S(1)}, f32[32,6,256]{2,0,1:T(8,128)S(1)}, u32[]{:S(2)}, u32[]{:S(2)}) collective-permute-start(f32[32,6,256]{2,0,1:T(8,128)S(1)} %bitcast.119), channel_id=1, source_target_pairs={{0,3},{1,0},{2,1},{3,2},{4,7},{5,4},{6,5},{7,6},{8,11},{9,8},{10,9... | collective-permute-start | bytes 589832 | tf_op jit(solution)/shard_map/ppermute | solution.py:39
  218.8 10.3 %all-to-all-start.9 = ((f32[4,16,4,128]{3,1,2,0:T(8,128)}), f32[4,16,4,128]{3,1,2,0:T(8,128)S(1)}, u32[]{:S(2)}, u32[]{:S(2)}) async-start(f32[4,16,4,128]{3,1,2,0:T(8,128)} %bitcast.34), calls=%async_computation.9 | async-start | bytes 262144 | tf_op jit(solution)/shard_map/all_to_all | solution.py:27
  229.3 0.9 copy-start.5
  230.2 0.9 copy-start.3
